TPU v7x, 32 devices: a whole 2x2x4 slice. The times are simulated.
32 devices in a mesh: dp: 8 (over z, x), bn: 4 (over y, core).
Axes of the slice: x: 2, y: 2, z: 4, core: 2. Of those that a mesh axis runs over, the one named last changes fastest.
Arguments:
- images_coarse: bfloat16 [128, 10, 10, 1024], P(('dp', 'bn')), may hold values from -6 to 6
- images_medium: bfloat16 [64, 14, 14, 1024], P(('dp', 'bn')), may hold values from -6 to 6
- images_fine: bfloat16 [64, 18, 18, 1024], P(('dp', 'bn')), may hold values from -6 to 6
- live_coarse: int32 [128], replicated, may hold values from 0 to 1, as said below
- live_medium: int32 [64], replicated, may hold values from 0 to 1, as said below
- live_fine: int32 [64], replicated, may hold values from 0 to 1, as said below
- upstream_coarse: bfloat16 [128, 5, 5, 2048], P(('dp', 'bn')), may hold values from -6 to 6
- upstream_medium: bfloat16 [64, 7, 7, 2048], P(('dp', 'bn')), may hold values from -6 to 6
- upstream_fine: bfloat16 [64, 9, 9, 2048], P(('dp', 'bn')), may hold values from -6 to 6
- reduce_proj: float32 [1024, 512], P(('dp', 'bn')), may hold values from -0.1875 to 0.1875
- spatial_proj: float32 [4608, 512], P(('dp', 'bn')), may hold values from -0.09375 to 0.09375
- expand_proj: float32 [512, 2048], P(None, ('dp', 'bn')), may hold values from -0.25 to 0.25
- shortcut_proj: float32 [1024, 2048], P(None, ('dp', 'bn')), may hold values from -0.1875 to 0.1875
- reduce_ident: float32 [2048, 512], P(('dp', 'bn')), may hold values from -0.125 to 0.125
- spatial_ident: float32 [4608, 512], P(('dp', 'bn')), may hold values from -0.09375 to 0.09375
- expand_ident: float32 [512, 2048], P(None, ('dp', 'bn')), may hold values from -0.25 to 0.25
- norm_params: float32 [16384], P(('dp', 'bn')), may hold values from -0.6 to 1.4
- mean_reduce_proj: float32 [1024, 512], P(('dp', 'bn')), may hold values from -450.7913 to 450.7913
- mean_spatial_proj: float32 [4608, 512], P(('dp', 'bn')), may hold values from -418.59192 to 418.59192
- mean_expand_proj: float32 [512, 2048], P(None, ('dp', 'bn')), may hold values from -193.19627 to 193.19627
- mean_shortcut_proj: float32 [1024, 2048], P(None, ('dp', 'bn')), may hold values from -209.29596 to 209.29596
- mean_reduce_ident: float32 [2048, 512], P(('dp', 'bn')), may hold values from -386.39255 to 386.39255
- mean_spatial_ident: float32 [4608, 512], P(('dp', 'bn')), may hold values from -386.39255 to 386.39255
- mean_expand_ident: float32 [512, 2048], P(None, ('dp', 'bn')), may hold values from -193.19627 to 193.19627
- mean_norm_params: float32 [16384], P(('dp', 'bn')), may hold values from -321.99377 to 321.99377
- square_reduce_proj: float32 [1024, 512], P(('dp', 'bn')), may hold values from 22579.2 to 90316.8
- square_spatial_proj: float32 [4608, 512], P(('dp', 'bn')), may hold values from 19468.8 to 77875.2
- square_expand_proj: float32 [512, 2048], P(None, ('dp', 'bn')), may hold values from 4147.2 to 16588.8
- square_shortcut_proj: float32 [1024, 2048], P(None, ('dp', 'bn')), may hold values from 4838.4 to 19468.8
- square_reduce_ident: float32 [2048, 512], P(('dp', 'bn')), may hold values from 16588.8 to 66355.2
- square_spatial_ident: float32 [4608, 512], P(('dp', 'bn')), may hold values from 16588.8 to 66355.2
- square_expand_ident: float32 [512, 2048], P(None, ('dp', 'bn')), may hold values from 4147.2 to 16588.8
- square_norm_params: float32 [16384], P(('dp', 'bn')), may hold values from 11520 to 46080
Outputs:
- output_coarse: bfloat16 [128, 5, 5, 2048], P(('dp', 'bn'))
- output_medium: bfloat16 [64, 7, 7, 2048], P(('dp', 'bn'))
- output_fine: bfloat16 [64, 9, 9, 2048], P(('dp', 'bn'))
- grad_coarse: bfloat16 [128, 10, 10, 1024], P(('dp', 'bn'))
- grad_medium: bfloat16 [64, 14, 14, 1024], P(('dp', 'bn'))
- grad_fine: bfloat16 [64, 18, 18, 1024], P(('dp', 'bn'))
- next_reduce_proj: float32 [1024, 512], P(('dp', 'bn'))
- next_mean_reduce_proj: float32 [1024, 512], P(('dp', 'bn'))
- next_square_reduce_proj: float32 [1024, 512], P(('dp', 'bn'))
- next_spatial_proj: float32 [4608, 512], P(('dp', 'bn'))
- next_mean_spatial_proj: float32 [4608, 512], P(('dp', 'bn'))
- next_square_spatial_proj: float32 [4608, 512], P(('dp', 'bn'))
- next_expand_proj: float32 [512, 2048], P(None, ('dp', 'bn'))
- next_mean_expand_proj: float32 [512, 2048], P(None, ('dp', 'bn'))
- next_square_expand_proj: float32 [512, 2048], P(None, ('dp', 'bn'))
- next_shortcut_proj: float32 [1024, 2048], P(None, ('dp', 'bn'))
- next_mean_shortcut_proj: float32 [1024, 2048], P(None, ('dp', 'bn'))
- next_square_shortcut_proj: float32 [1024, 2048], P(None, ('dp', 'bn'))
- next_reduce_ident: float32 [2048, 512], P(('dp', 'bn'))
- next_mean_reduce_ident: float32 [2048, 512], P(('dp', 'bn'))
- next_square_reduce_ident: float32 [2048, 512], P(('dp', 'bn'))
- next_spatial_ident: float32 [4608, 512], P(('dp', 'bn'))
- next_mean_spatial_ident: float32 [4608, 512], P(('dp', 'bn'))
- next_square_spatial_ident: float32 [4608, 512], P(('dp', 'bn'))
- next_expand_ident: float32 [512, 2048], P(None, ('dp', 'bn'))
- next_mean_expand_ident: float32 [512, 2048], P(None, ('dp', 'bn'))
- next_square_expand_ident: float32 [512, 2048], P(None, ('dp', 'bn'))
- next_norm_params: float32 [16384], P(('dp', 'bn'))
- next_mean_norm_params: float32 [16384], P(('dp', 'bn'))
- next_square_norm_params: float32 [16384], P(('dp', 'bn'))
Inputs may be any that keep to these rules, and one draw needn't show every extreme that they name: `live_coarse`: 1 marks a slot that holds an image. On every device the live slots come first and its first slot is always live; in every draw some device has all of its slots live. `live_medium`: 1 marks a slot that holds an image. On every device the live slots come first and its first slot is always live; in every draw some device has all of its slots live. `live_fine`: 1 marks a slot that holds an image. On every device the live slots come first and its first slot is always live; in every draw some device has all of its slots live.
All inputs are finite; a program needn't handle non-finite values.
Results may differ from a plain program's by a relative error of at most 0.017.
The roundings to bfloat16 on the way count: a program that leaves them out, or rounds other values in their place, can miss the bound.
Values may be sent and summed in bfloat16 or wider, within the bound.
No kernel may reach another device: no remote copies, remote signals or barrier semaphores. Data moves between devices by JAX's collectives and lax.ppermute only.
A program may use at most 192 MiB of HBM per device.

v0:
```python
from functools import reduce

import jax
import jax.numpy as jnp
from jax import lax
from jax.sharding import PartitionSpec as P

STEP = 10


EPSILON = 1e-05
RATE_CONV = 0.03
RATE_NORM = 0.4
DECAY_CONV = 0.05


def add_all(members):
    return reduce(lambda left_side, right_side: left_side + right_side, members)


def silu_slope(values):
    sigma = jax.nn.sigmoid(values)
    return sigma * (1.0 + values * (1.0 - sigma))


def split_norm(vector, mid_width, out_width):
    widths = [mid_width, mid_width, out_width, out_width, mid_width, mid_width, out_width]
    halfway = vector.shape[0] // 2
    paired = []
    offset = 0
    for section in widths:
        paired.append(
            (
                vector[offset : offset + section],
                vector[halfway + offset : halfway + offset + section],
            )
        )
        offset = offset + section
    return paired


def in_batches(terms, width, adder):
    batches = [terms[start : start + width] for start in range(0, len(terms), width)]
    totals = []
    for batch in batches:
        totals.extend(list(adder(tuple(batch))))
    return totals


def normalize_many(items):
    spans = range(len(items))
    summed = in_batches(
        [jnp.sum(items[which][0] * items[which][1], axis=0) for which in spans],
        1,
        lambda group: lax.psum(group, "bn"),
    )
    centred = [items[which][0] - summed[which] / items[which][2] for which in spans]
    spread = in_batches(
        [jnp.sum(centred[which] * centred[which] * items[which][1], axis=0) for which in spans],
        1,
        lambda group: lax.psum(group, "bn"),
    )
    variance = [spread[which] / items[which][2] for which in spans]
    outputs = []
    states = []
    for which in spans:
        rescale = lax.rsqrt(variance[which] + EPSILON)
        normed = centred[which] * rescale
        gain_bias = items[which][3]
        outputs.append(gain_bias[0] * normed + gain_bias[1])
        states.append((normed, rescale, gain_bias[0]))
    return (outputs, states)


def norm_back_many(groups):
    terms = []
    for incoming, weight, counted, members in groups:
        terms.append(jnp.sum(incoming, axis=0))
        terms.append(jnp.stack([jnp.sum(incoming * member[0], axis=0) for member in members]))
    totals = in_batches(terms, 2, lambda group: lax.psum(group, "bn"))
    outgoing_all = []
    for which in range(len(groups)):
        incoming, weight, counted, members = groups[which]
        summed_bias, summed_gain = (totals[2 * which], totals[2 * which + 1])
        outgoing = []
        for position in range(len(members)):
            normed, rescale, norm_gain = members[position]
            correction = weight * (summed_bias + normed * summed_gain[position]) / counted
            outgoing.append((norm_gain * rescale * (incoming - correction)).astype(jnp.bfloat16))
        outgoing_all.append(outgoing)
    return (outgoing_all, add_all(terms[0::2]), add_all(terms[1::2]))


def outer_sum(left_side, right_side):
    return lax.dot_general(
        left_side, right_side, (((0,), (0,)), ((), ())), preferred_element_type=jnp.float32
    )


def back_through(incoming, matrix):
    return lax.dot_general(
        incoming, matrix, (((1,), (1,)), ((), ())), preferred_element_type=jnp.float32
    )


def collect_taps(pictures, stride, out_side):
    number, channels = (pictures.shape[0], pictures.shape[3])
    padded = jnp.pad(pictures, ((0, 0), (1, 1), (1, 1), (0, 0)))
    extent = stride * (out_side - 1) + 1
    pieces = []
    for tap_index in range(9):
        tap_row, tap_col = divmod(tap_index, 3)
        pieces.append(
            lax.slice(
                padded,
                (0, tap_row, tap_col, 0),
                (number, tap_row + extent, tap_col + extent, channels),
                (1, stride, stride, 1),
            )
        )
    return jnp.concatenate(pieces, axis=3).reshape(-1, 9 * channels)


def fold_taps(columns, number, in_side, out_side, stride):
    channels = columns.shape[1] // 9
    shaped = columns.reshape(number, out_side, out_side, 9, channels)
    folded = jnp.zeros((number, in_side + 2, in_side + 2, channels), jnp.float32)
    extent = stride * (out_side - 1) + 1
    for tap_index in range(9):
        tap_row, tap_col = divmod(tap_index, 3)
        folded = folded + lax.pad(
            shaped[:, :, :, tap_index, :],
            jnp.zeros((), jnp.float32),
            (
                (0, 0, 0),
                (tap_row, in_side + 2 - tap_row - extent, stride - 1),
                (tap_col, in_side + 2 - tap_col - extent, stride - 1),
                (0, 0, 0),
            ),
        )
    return folded[:, 1:-1, 1:-1, :]


def forward_all(inputs, proj_full, ident_full, paired):
    w_reduce, w_spatial, w_expand, w_short = proj_full
    w_narrow, w_middle, w_widen = ident_full
    in_width, mid_width, out_width = (w_reduce.shape[0], w_reduce.shape[1], w_expand.shape[1])
    shapes = []
    for pictures, alive_mask, counted in inputs:
        number, in_side = (pictures.shape[0], pictures.shape[1])
        out_side = in_side // 2
        weight_in = jnp.broadcast_to(alive_mask[:, None], (number, in_side * in_side)).reshape(
            -1, 1
        )
        weight_out = jnp.broadcast_to(alive_mask[:, None], (number, out_side * out_side)).reshape(
            -1, 1
        )
        shapes.append(
            (
                number,
                in_side,
                out_side,
                weight_in,
                weight_out,
                counted * (in_side * in_side),
                counted * (out_side * out_side),
            )
        )
    spans = range(len(inputs))
    flat_input = [inputs[which][0].reshape(-1, in_width) for which in spans]
    conv_one = [
        jnp.dot(flat_input[which], w_reduce, preferred_element_type=jnp.float32) for which in spans
    ]
    pre_one, state_one = normalize_many(
        [(conv_one[which], shapes[which][3], shapes[which][5], paired[0]) for which in spans]
    )
    act_one = [jax.nn.silu(member).astype(jnp.bfloat16) for member in pre_one]
    patches_two = [
        collect_taps(
            act_one[which].reshape(shapes[which][0], shapes[which][1], shapes[which][1], mid_width),
            2,
            shapes[which][2],
        )
        for which in spans
    ]
    conv_two = [
        jnp.dot(patches_two[which], w_spatial, preferred_element_type=jnp.float32)
        for which in spans
    ]
    pre_two, state_two = normalize_many(
        [(conv_two[which], shapes[which][4], shapes[which][6], paired[1]) for which in spans]
    )
    act_two = [jax.nn.silu(member).astype(jnp.bfloat16) for member in pre_two]
    conv_expand = [
        jnp.dot(act_two[which], w_expand, preferred_element_type=jnp.float32) for which in spans
    ]
    sub_flat = [inputs[which][0][:, ::2, ::2, :].reshape(-1, in_width) for which in spans]
    conv_short = [
        jnp.dot(sub_flat[which], w_short, preferred_element_type=jnp.float32) for which in spans
    ]
    pair_items = []
    for which in spans:
        pair_items.append((conv_expand[which], shapes[which][4], shapes[which][6], paired[2]))
        pair_items.append((conv_short[which], shapes[which][4], shapes[which][6], paired[3]))
    normed, state_pair = normalize_many(pair_items)
    joined_mid = [normed[2 * which] + normed[2 * which + 1] for which in spans]
    hidden = [jax.nn.silu(member) for member in joined_mid]
    hidden_low = [member.astype(jnp.bfloat16) for member in hidden]
    conv_four = [
        jnp.dot(hidden_low[which], w_narrow, preferred_element_type=jnp.float32) for which in spans
    ]
    pre_four, state_four = normalize_many(
        [(conv_four[which], shapes[which][4], shapes[which][6], paired[4]) for which in spans]
    )
    act_four = [jax.nn.silu(member).astype(jnp.bfloat16) for member in pre_four]
    patches_five = [
        collect_taps(
            act_four[which].reshape(
                shapes[which][0], shapes[which][2], shapes[which][2], mid_width
            ),
            1,
            shapes[which][2],
        )
        for which in spans
    ]
    conv_five = [
        jnp.dot(patches_five[which], w_middle, preferred_element_type=jnp.float32)
        for which in spans
    ]
    pre_five, state_five = normalize_many(
        [(conv_five[which], shapes[which][4], shapes[which][6], paired[5]) for which in spans]
    )
    act_five = [jax.nn.silu(member).astype(jnp.bfloat16) for member in pre_five]
    conv_six = [
        jnp.dot(act_five[which], w_widen, preferred_element_type=jnp.float32) for which in spans
    ]
    normed, state_six = normalize_many(
        [(conv_six[which], shapes[which][4], shapes[which][6], paired[6]) for which in spans]
    )
    results = []
    stored = []
    for which in spans:
        joined_out = normed[which] + hidden[which]
        results.append(
            (shapes[which][4] * jax.nn.silu(joined_out))
            .astype(jnp.bfloat16)
            .reshape(shapes[which][0], shapes[which][2], shapes[which][2], out_width)
        )
        states = (
            state_one[which],
            state_two[which],
            state_pair[2 * which],
            state_pair[2 * which + 1],
            state_four[which],
            state_five[which],
            state_six[which],
        )
        befores = (pre_one[which], pre_two[which], pre_four[which], pre_five[which])
        stored.append(
            (
                flat_input[which],
                sub_flat[which],
                act_one[which],
                patches_two[which],
                act_two[which],
                hidden_low[which],
                act_four[which],
                patches_five[which],
                act_five[which],
                joined_mid[which],
                joined_out,
                states,
                befores,
            )
        )
    return (results, stored, shapes)


def backward_all(upstreams, stored, shapes, proj_full, ident_full):
    w_reduce, w_spatial, w_expand, w_short = proj_full
    w_narrow, w_middle, w_widen = ident_full
    in_width, mid_width = (w_reduce.shape[0], w_reduce.shape[1])
    spans = range(len(stored))
    incoming = [
        upstreams[which].reshape(-1, upstreams[which].shape[3]).astype(jnp.float32)
        * shapes[which][4]
        * silu_slope(stored[which][10])
        for which in spans
    ]
    outgoing, bias_six, gain_six = norm_back_many(
        [
            (incoming[which], shapes[which][4], shapes[which][6], [stored[which][11][6]])
            for which in spans
        ]
    )
    delta_six = [member[0] for member in outgoing]
    grad_widen = add_all([outer_sum(stored[which][8], delta_six[which]) for which in spans])
    into_five = [
        back_through(delta_six[which], w_widen) * silu_slope(stored[which][12][3])
        for which in spans
    ]
    outgoing, bias_five, gain_five = norm_back_many(
        [
            (into_five[which], shapes[which][4], shapes[which][6], [stored[which][11][5]])
            for which in spans
        ]
    )
    delta_five = [member[0] for member in outgoing]
    grad_middle = add_all([outer_sum(stored[which][7], delta_five[which]) for which in spans])
    into_four = [
        fold_taps(
            back_through(delta_five[which], w_middle),
            shapes[which][0],
            shapes[which][2],
            shapes[which][2],
            1,
        ).reshape(-1, mid_width)
        * silu_slope(stored[which][12][2])
        for which in spans
    ]
    outgoing, bias_four, gain_four = norm_back_many(
        [
            (into_four[which], shapes[which][4], shapes[which][6], [stored[which][11][4]])
            for which in spans
        ]
    )
    delta_four = [member[0] for member in outgoing]
    grad_narrow = add_all([outer_sum(stored[which][5], delta_four[which]) for which in spans])
    into_mid = [
        (incoming[which] + back_through(delta_four[which], w_narrow)) * silu_slope(stored[which][9])
        for which in spans
    ]
    outgoing, bias_mid, gain_mid = norm_back_many(
        [
            (
                into_mid[which],
                shapes[which][4],
                shapes[which][6],
                [stored[which][11][2], stored[which][11][3]],
            )
            for which in spans
        ]
    )
    delta_expand = [member[0] for member in outgoing]
    delta_short = [member[1] for member in outgoing]
    grad_expand = add_all([outer_sum(stored[which][4], delta_expand[which]) for which in spans])
    grad_short = add_all([outer_sum(stored[which][1], delta_short[which]) for which in spans])
    into_two = [
        back_through(delta_expand[which], w_expand) * silu_slope(stored[which][12][1])
        for which in spans
    ]
    outgoing, bias_two, gain_two = norm_back_many(
        [
            (into_two[which], shapes[which][4], shapes[which][6], [stored[which][11][1]])
            for which in spans
        ]
    )
    delta_two = [member[0] for member in outgoing]
    grad_spatial = add_all([outer_sum(stored[which][3], delta_two[which]) for which in spans])
    into_one = [
        fold_taps(
            back_through(delta_two[which], w_spatial),
            shapes[which][0],
            shapes[which][1],
            shapes[which][2],
            2,
        ).reshape(-1, mid_width)
        * silu_slope(stored[which][12][0])
        for which in spans
    ]
    outgoing, bias_one, gain_one = norm_back_many(
        [
            (into_one[which], shapes[which][3], shapes[which][5], [stored[which][11][0]])
            for which in spans
        ]
    )
    delta_one = [member[0] for member in outgoing]
    grad_reduce = add_all([outer_sum(stored[which][0], delta_one[which]) for which in spans])
    input_grads = []
    for which in spans:
        number, in_side, out_side = (shapes[which][0], shapes[which][1], shapes[which][2])
        from_short = back_through(delta_short[which], w_short).reshape(
            number, out_side, out_side, in_width
        )
        spread_short = lax.pad(
            from_short, jnp.zeros((), jnp.float32), ((0, 0, 0), (0, 1, 1), (0, 1, 1), (0, 0, 0))
        )
        input_grads.append(
            (
                back_through(delta_one[which], w_reduce).reshape(number, in_side, in_side, in_width)
                + spread_short
            ).astype(jnp.bfloat16)
        )
    norm_grad = jnp.concatenate(
        [
            gain_one[0],
            gain_two[0],
            gain_mid[0],
            gain_mid[1],
            gain_four[0],
            gain_five[0],
            gain_six[0],
            bias_one,
            bias_two,
            bias_mid,
            bias_mid,
            bias_four,
            bias_five,
            bias_six,
        ]
    )
    return (
        input_grads,
        (grad_reduce, grad_spatial, grad_expand, grad_short),
        (grad_narrow, grad_middle, grad_widen),
        norm_grad,
    )


def adam_step(weight, moment_one, moment_two, gradient, step_rate, decay_rate):
    first_new = 0.5 * moment_one + 0.5 * gradient
    second_new = 0.5 * moment_two + 0.5 * gradient * gradient
    correct = 1.0 - 0.5**STEP
    update = first_new / correct / (jnp.sqrt(second_new / correct) + 1e-08) + decay_rate * weight
    return (weight - step_rate * update, first_new, second_new)


def on_device(
    images_coarse,
    images_medium,
    images_fine,
    live_coarse,
    live_medium,
    live_fine,
    upstream_coarse,
    upstream_medium,
    upstream_fine,
    reduce_proj,
    spatial_proj,
    expand_proj,
    shortcut_proj,
    reduce_ident,
    spatial_ident,
    expand_ident,
    norm_params,
    mean_reduce_proj,
    mean_spatial_proj,
    mean_expand_proj,
    mean_shortcut_proj,
    mean_reduce_ident,
    mean_spatial_ident,
    mean_expand_ident,
    mean_norm_params,
    square_reduce_proj,
    square_spatial_proj,
    square_expand_proj,
    square_shortcut_proj,
    square_reduce_ident,
    square_spatial_ident,
    square_expand_ident,
    square_norm_params,
):
    proj_low = (
        lax.all_gather(reduce_proj.astype(jnp.bfloat16), ("dp", "bn"), axis=0, tiled=True),
        lax.all_gather(spatial_proj.astype(jnp.bfloat16), ("dp", "bn"), axis=0, tiled=True),
        lax.all_gather(expand_proj.astype(jnp.bfloat16), ("dp", "bn"), axis=1, tiled=True),
        lax.all_gather(shortcut_proj.astype(jnp.bfloat16), ("dp", "bn"), axis=1, tiled=True),
        lax.all_gather(norm_params.astype(jnp.bfloat16), ("dp", "bn"), axis=0, tiled=True),
    )
    ident_low = (
        lax.all_gather(reduce_ident.astype(jnp.bfloat16), ("dp", "bn"), axis=0, tiled=True),
        lax.all_gather(spatial_ident.astype(jnp.bfloat16), ("dp", "bn"), axis=0, tiled=True),
        lax.all_gather(expand_ident.astype(jnp.bfloat16), ("dp", "bn"), axis=1, tiled=True),
    )
    proj_full = (proj_low[0], proj_low[1], proj_low[2], proj_low[3])
    paired = split_norm(proj_low[4].astype(jnp.float32), proj_low[0].shape[1], proj_low[2].shape[1])
    members = lax.axis_size("bn")
    group_index = lax.axis_index("dp")
    own_index = group_index * members + lax.axis_index("bn")
    inputs = []
    upstreams = []
    for pictures, alive_slots, upstream in (
        (images_coarse, live_coarse, upstream_coarse),
        (images_medium, live_medium, upstream_medium),
        (images_fine, live_fine, upstream_fine),
    ):
        per_device = pictures.shape[0]
        own_alive = lax.dynamic_slice_in_dim(alive_slots, own_index * per_device, per_device)
        group_alive = lax.dynamic_slice_in_dim(
            alive_slots, group_index * (members * per_device), members * per_device
        )
        counted = jnp.sum(group_alive).astype(jnp.float32)
        inputs.append((pictures, own_alive.astype(jnp.float32), counted))
        upstreams.append(upstream)
    results, stored, shapes = forward_all(inputs, proj_full, ident_low, paired)
    back_list, proj_total, ident_total, norm_total = backward_all(
        upstreams, stored, shapes, proj_full, ident_low
    )
    owned = (
        lax.psum_scatter(proj_total[0], ("dp", "bn"), scatter_dimension=0, tiled=True),
        lax.psum_scatter(proj_total[1], ("dp", "bn"), scatter_dimension=0, tiled=True),
        lax.psum_scatter(proj_total[2], ("dp", "bn"), scatter_dimension=1, tiled=True),
        lax.psum_scatter(proj_total[3], ("dp", "bn"), scatter_dimension=1, tiled=True),
        lax.psum_scatter(ident_total[0], ("dp", "bn"), scatter_dimension=0, tiled=True),
        lax.psum_scatter(ident_total[1], ("dp", "bn"), scatter_dimension=0, tiled=True),
        lax.psum_scatter(ident_total[2], ("dp", "bn"), scatter_dimension=1, tiled=True),
        lax.psum_scatter(norm_total, ("dp", "bn"), scatter_dimension=0, tiled=True),
    )
    params = (
        reduce_proj,
        spatial_proj,
        expand_proj,
        shortcut_proj,
        reduce_ident,
        spatial_ident,
        expand_ident,
        norm_params,
    )
    firsts = (
        mean_reduce_proj,
        mean_spatial_proj,
        mean_expand_proj,
        mean_shortcut_proj,
        mean_reduce_ident,
        mean_spatial_ident,
        mean_expand_ident,
        mean_norm_params,
    )
    seconds = (
        square_reduce_proj,
        square_spatial_proj,
        square_expand_proj,
        square_shortcut_proj,
        square_reduce_ident,
        square_spatial_ident,
        square_expand_ident,
        square_norm_params,
    )
    stepped = []
    for position in range(8):
        if position < 7:
            stepped.append(
                adam_step(
                    params[position],
                    firsts[position],
                    seconds[position],
                    owned[position],
                    RATE_CONV,
                    DECAY_CONV,
                )
            )
        else:
            stepped.append(
                adam_step(
                    params[position],
                    firsts[position],
                    seconds[position],
                    owned[position],
                    RATE_NORM,
                    0.0,
                )
            )
    return (
        results[0],
        results[1],
        results[2],
        back_list[0],
        back_list[1],
        back_list[2],
        stepped[0][0],
        stepped[0][1],
        stepped[0][2],
        stepped[1][0],
        stepped[1][1],
        stepped[1][2],
        stepped[2][0],
        stepped[2][1],
        stepped[2][2],
        stepped[3][0],
        stepped[3][1],
        stepped[3][2],
        stepped[4][0],
        stepped[4][1],
        stepped[4][2],
        stepped[5][0],
        stepped[5][1],
        stepped[5][2],
        stepped[6][0],
        stepped[6][1],
        stepped[6][2],
        stepped[7][0],
        stepped[7][1],
        stepped[7][2],
    )


def solution(mesh):
    placed = (
        P(("dp", "bn"), None, None, None),
        P(("dp", "bn"), None, None, None),
        P(("dp", "bn"), None, None, None),
        P(),
        P(),
        P(),
        P(("dp", "bn"), None, None, None),
        P(("dp", "bn"), None, None, None),
        P(("dp", "bn"), None, None, None),
        P(("dp", "bn"), None),
        P(("dp", "bn"), None),
        P(None, ("dp", "bn")),
        P(None, ("dp", "bn")),
        P(("dp", "bn"), None),
        P(("dp", "bn"), None),
        P(None, ("dp", "bn")),
        P(("dp", "bn")),
        P(("dp", "bn"), None),
        P(("dp", "bn"), None),
        P(None, ("dp", "bn")),
        P(None, ("dp", "bn")),
        P(("dp", "bn"), None),
        P(("dp", "bn"), None),
        P(None, ("dp", "bn")),
        P(("dp", "bn")),
        P(("dp", "bn"), None),
        P(("dp", "bn"), None),
        P(None, ("dp", "bn")),
        P(None, ("dp", "bn")),
        P(("dp", "bn"), None),
        P(("dp", "bn"), None),
        P(None, ("dp", "bn")),
        P(("dp", "bn")),
    )
    return jax.shard_map(
        on_device,
        mesh=mesh,
        in_specs=placed,
        out_specs=(
            P(("dp", "bn"), None, None, None),
            P(("dp", "bn"), None, None, None),
            P(("dp", "bn"), None, None, None),
            P(("dp", "bn"), None, None, None),
            P(("dp", "bn"), None, None, None),
            P(("dp", "bn"), None, None, None),
            P(("dp", "bn"), None),
            P(("dp", "bn"), None),
            P(("dp", "bn"), None),
            P(("dp", "bn"), None),
            P(("dp", "bn"), None),
            P(("dp", "bn"), None),
            P(None, ("dp", "bn")),
            P(None, ("dp", "bn")),
            P(None, ("dp", "bn")),
            P(None, ("dp", "bn")),
            P(None, ("dp", "bn")),
            P(None, ("dp", "bn")),
            P(("dp", "bn"), None),
            P(("dp", "bn"), None),
            P(("dp", "bn"), None),
            P(("dp", "bn"), None),
            P(("dp", "bn"), None),
            P(("dp", "bn"), None),
            P(None, ("dp", "bn")),
            P(None, ("dp", "bn")),
            P(None, ("dp", "bn")),
            P(("dp", "bn")),
            P(("dp", "bn")),
            P(("dp", "bn")),
        ),
        check_vma=False,
    )
```

profile of v0, /device:TPU:0, one launch (start us, length us, event | category | flops | bytes accessed | tf_op | source)
XLA Modules:
  0.0 2529.9 jit_solution(9904164544670616056)
XLA Ops:
  16.2 43.5 %all-gather = bf16[32,1,512]{2,1,0:T(2,128)(2,1)S(1)} all-gather(bf16[1,1,512]{2,1,0:T(2,128)(2,1)S(1)} %reshape.399), channel_id=1, replica_groups=mesh['dp'=8,'bn'=4] {'dp','bn'}, dimensions={0}, use_global_device_ids=true | all-gather | bytes 33792 | tf_op jit(solution)/shard_map/all_gather | solution.py:468
  87.5 6.2 all-reduce.82
  94.3 6.7 all-reduce.81
  131.6 6.2 slice.426
  174.7 6.2 slice.419
  180.9 6.2 slice.418
  263.1 6.4 all-reduce.80
  282.1 11.4 all-reduce.78
  301.7 10.9 all-reduce.77
  314.4 10.8 all-reduce.76
  338.0 6.7 all-reduce.75
  350.0 7.0 all-reduce.74
  462.1 6.4 all-reduce.73
  477.2 7.4 all-reduce.72
  495.0 11.4 all-reduce.71
  513.5 12.1 all-reduce.70
  536.4 11.6 all-reduce.69
  558.6 12.2 all-reduce.68
  581.0 8.6 fusion.100
  605.4 8.6 fusion.102
  632.7 11.8 fusion.98
  652.1 11.2 all-reduce.67
  677.8 26.2 %all-reduce.88.cloned.1.call-done = (f32[2,2048]{1,0:T(2,128)}, f32[2048]{0:T(1024)}, f32[2,2048]{1,0:T(2,128)}, f32[2048]{0:T(1024)}, f32[2,2048]{1,0:T(2,128)}, /*index=5*/f32[2048]{0:T(1024)}) async-done(((f32[2,2048]{1,0:T(2,128)}, f32[2048]{0:T(1024)}, f32[2,2048]{1,0:T(2,128)}, f32[2048]{0:T(1024)}, f32[2,2048]{1,0:T(2,128)}, /*index=5*/f32[2048]{0:T(1024)}), (f32[2,2048]{1,0:T(2,128)}, ...) | async-done | bytes 73744 | tf_op jit(solution)/shard_map/psum | solution.py:80
  717.1 12.0 all-reduce.65
  735.9 8.9 fusion.99
  748.0 8.8 pad.271
  756.8 8.8 pad.272
  765.6 8.8 pad.274
  774.4 8.8 pad.275
  783.6 8.8 pad.399
  792.4 9.3 pad.210
  801.7 12.7 pad.212
  814.5 12.7 pad.211
  844.2 9.0 fusion.101
  858.9 16.0 pad.283
  874.8 15.9 pad.284
  890.8 15.9 pad.286
  906.7 15.9 pad.287
  922.6 15.9 pad.402
  938.5 16.0 pad.401
  954.5 17.5 pad.229
  972.1 22.9 pad.231
  994.9 16.4 pad.230
  1033.7 11.6 fusion.97
  1053.5 28.3 %pad.295 = f32[2,18,18,512]{3,0,2,1:T(2,128)S(1)} pad(f32[2,9,9,512]{3,0,2,1:T(2,128)} %bitcast.336, f32[]{:T(128)} %constant.44.clone.1), padding=0_0_0x0_1_1x0_1_1x0_0_0 | pad | bytes 1658884 | tf_op jit(solution)/shard_map/slice | solution.py:141
  1081.9 36.4 %pad.296 = f32[2,18,18,512]{3,0,2,1:T(2,128)} pad(f32[2,9,9,512]{3,0,2,1:T(2,128)} %bitcast.335, f32[]{:T(128)} %constant.44.clone.1), padding=0_0_0x0_1_1x1_0_1x0_0_0 | pad | bytes 1658884 | tf_op jit(solution)/shard_map/slice | solution.py:141
  1118.2 36.4 %pad.298 = f32[2,18,18,512]{3,0,2,1:T(2,128)} pad(f32[2,9,9,512]{3,0,2,1:T(2,128)} %bitcast.331, f32[]{:T(128)} %constant.44.clone.1), padding=0_0_0x1_0_1x0_1_1x0_0_0 | pad | bytes 1658884 | tf_op jit(solution)/shard_map/slice | solution.py:141
  1154.6 36.3 %pad.299 = f32[2,18,18,512]{3,0,2,1:T(2,128)} pad(f32[2,9,9,512]{3,0,2,1:T(2,128)} %bitcast.328, f32[]{:T(128)} %constant.44.clone.1), padding=0_0_0x1_0_1x1_0_1x0_0_0 | pad | bytes 1658884 | tf_op jit(solution)/shard_map/slice | solution.py:141
  1190.9 36.3 %pad.404 = f32[2,18,19,512]{3,0,2,1:T(2,128)} pad(f32[2,9,9,512]{3,0,2,1:T(2,128)} %bitcast.333, f32[]{:T(128)} %constant.44.clone.1), padding=0_0_0x0_1_1x0_2_1x0_0_0 | pad | bytes 1732612
  1227.2 36.3 %pad.403 = f32[2,18,19,512]{3,0,2,1:T(2,128)} pad(f32[2,9,9,512]{3,0,2,1:T(2,128)} %bitcast.329, f32[]{:T(128)} %constant.44.clone.1), padding=0_0_0x1_0_1x0_2_1x0_0_0 | pad | bytes 1732612
  1263.5 36.4 %pad.248 = f32[2,20,20,512]{3,0,2,1:T(2,128)} pad(f32[2,9,9,512]{3,0,2,1:T(2,128)} %bitcast.334, f32[]{:T(128)} %constant.44.clone.1), padding=0_0_0x0_3_1x0_3_1x0_0_0 | pad | bytes 1970180 | tf_op jit(solution)/shard_map/pad | solution.py:131
  1299.9 36.5 %pad.250 = f32[2,20,20,512]{3,0,2,1:T(2,128)} pad(f32[2,9,9,512]{3,0,2,1:T(2,128)} %bitcast.332, f32[]{:T(128)} %constant.44.clone.1), padding=0_0_0x0_3_1x2_1_1x0_0_0 | pad | bytes 1970180 | tf_op jit(solution)/shard_map/pad | solution.py:131
  1336.4 36.4 %pad.249 = f32[2,20,20,512]{3,0,2,1:T(2,128)} pad(f32[2,9,9,512]{3,0,2,1:T(2,128)} %bitcast.327, f32[]{:T(128)} %constant.44.clone.1), padding=0_0_0x0_3_1x1_2_1x0_0_0 | pad | bytes 1970180 | tf_op jit(solution)/shard_map/pad | solution.py:131
  1395.8 11.2 all-reduce.64
  1449.8 6.5 add_add_fusion
  1497.4 8.0 pad.219
  1527.7 11.6 pad.257
  1546.0 128.6 %reduce-scatter.22.cloned.1.call-done = f32[32,512]{1,0:T(8,128)} async-done(((f32[1024,512]{1,0:T(8,128)}), f32[32,512]{1,0:T(8,128)}) %reduce-scatter.22.cloned.1.call-update) | async-done | bytes 65552 | tf_op jit(solution)/shard_map/reduce_scatter | solution.py:500
  1676.2 137.9 %reduce-scatter.16.cloned.1.call-done = f32[64,512]{1,0:T(8,128)} async-done(((f32[2048,512]{1,0:T(8,128)}), f32[64,512]{1,0:T(8,128)}) %reduce-scatter.16.cloned.1.call-update) | async-done | bytes 131088 | tf_op jit(solution)/shard_map/reduce_scatter | solution.py:504
  1815.8 137.2 %reduce-scatter.20.cloned.1.call-done = f32[512,64]{0,1:T(8,128)} async-done(((f32[512,2048]{0,1:T(8,128)}), f32[512,64]{0,1:T(8,128)}) %reduce-scatter.20.cloned.1.call-update) | async-done | bytes 131088 | tf_op jit(solution)/shard_map/reduce_scatter | solution.py:506
  1954.7 137.5 %reduce-scatter.12.cloned.1.call-done = f32[512,64]{0,1:T(8,128)} async-done(((f32[512,2048]{0,1:T(8,128)}), f32[512,64]{0,1:T(8,128)}) %reduce-scatter.12.cloned.1.call-update) | async-done | bytes 131088 | tf_op jit(solution)/shard_map/reduce_scatter | solution.py:502
  2093.9 135.6 %reduce-scatter.18.cloned.1.call-done = f32[144,512]{1,0:T(8,128)} async-done(((f32[4608,512]{1,0:T(8,128)}), f32[144,512]{1,0:T(8,128)}) %reduce-scatter.18.cloned.1.call-update) | async-done | bytes 294928 | tf_op jit(solution)/shard_map/reduce_scatter | solution.py:505
  2231.6 139.3 %reduce-scatter.10.cloned.1.call-done = f32[144,512]{1,0:T(8,128)} async-done(((f32[4608,512]{1,0:T(8,128)}), f32[144,512]{1,0:T(8,128)}) %reduce-scatter.10.cloned.1.call-update) | async-done | bytes 294928 | tf_op jit(solution)/shard_map/reduce_scatter | solution.py:501
  2372.9 148.0 %reduce-scatter.14.cloned.1.call-done = f32[1024,64]{0,1:T(8,128)} async-done(((f32[1024,2048]{0,1:T(8,128)}), f32[1024,64]{0,1:T(8,128)}) %reduce-scatter.14.cloned.1.call-update) | async-done | bytes 262160 | tf_op jit(solution)/shard_map/reduce_scatter | solution.py:503
  (1273 shorter events, 659.2 us)
Async XLA Ops:
  7.3 53.8 %copy-start.128 = (bf16[2,14,14,1024]{3,0,2,1:T(2,128)(2,1)S(1)}, bf16[2,14,14,1024]{3,0,2,1:T(2,128)(2,1)}, u32[]{:S(2)}) copy-start(bf16[2,14,14,1024]{3,0,2,1:T(2,128)(2,1)} %param.34) | copy-start | bytes 2408452
  7.3 75.5 %all-gather.9.cloned.1.call-start = ((), (), s32[]{:S(2)}) async-start(), calls=%async_computation.7 | async-start | bytes 1081344 | tf_op jit(solution)/shard_map/all_gather | solution.py:464
  8.9 247.8 %all-gather.11.cloned.1.call-start = ((), (), s32[]{:S(2)}) async-start(), calls=%async_computation.8 | async-start | bytes 4866048 | tf_op jit(solution)/shard_map/all_gather | solution.py:465
  10.6 266.1 %all-gather.13.cloned.1.call-start = ((), (), s32[]{:S(2)}) async-start(), calls=%async_computation.9 | async-start | bytes 2162688 | tf_op jit(solution)/shard_map/all_gather | solution.py:466
  12.2 281.3 %all-gather.15.cloned.1.call-start = ((), (), s32[]{:S(2)}) async-start(), calls=%async_computation.10 | async-start | bytes 4325376 | tf_op jit(solution)/shard_map/all_gather | solution.py:467
  13.9 318.8 %all-gather.17.cloned.1.call-start = ((), (), s32[]{:S(2)}) async-start(), calls=%async_computation.11 | async-start | bytes 2162688 | tf_op jit(solution)/shard_map/all_gather | solution.py:471
  14.6 47.7 %copy-start.127 = (bf16[4,10,10,1024]{3,0,2,1:T(4,128)(2,1)S(1)}, bf16[4,10,10,1024]{3,0,2,1:T(4,128)(2,1)}, u32[]{:S(2)}) copy-start(bf16[4,10,10,1024]{3,0,2,1:T(4,128)(2,1)} %param.33) | copy-start | bytes 2457604
  14.6 435.5 %all-gather.19.cloned.1.call-start = ((), (), s32[]{:S(2)}) async-start(), calls=%async_computation.12 | async-start | bytes 4866048 | tf_op jit(solution)/shard_map/all_gather | solution.py:472
  15.4 470.6 %all-gather.21.cloned.1.call-start = ((), (), s32[]{:S(2)}) async-start(), calls=%async_computation.13 | async-start | bytes 2162688 | tf_op jit(solution)/shard_map/all_gather | solution.py:473
  16.2 687.8 %all-reduce.88.cloned.1.call-start = ((), (), s32[]{:S(2)}) async-start(), calls=%async_computation.22 | async-start | bytes 147456 | tf_op jit(solution)/shard_map/psum | solution.py:80
  60.4 40.7 %copy-start.240 = (f32[1,1,512]{2,1,0:T(1,128)}, f32[1,1,512]{2,1,0:T(1,128)S(1)}, u32[]{:S(2)}) copy-start(f32[1,1,512]{2,1,0:T(1,128)S(1)} %get-tuple-element.711) | copy-start | bytes 6148
  86.7 44.2 %copy-start.24 = (f32[400,512]{1,0:T(8,128)}, f32[400,512]{1,0:T(8,128)S(1)}, u32[]{:S(2)}) copy-start(f32[400,512]{1,0:T(8,128)S(1)} %get-tuple-element.760) | copy-start | bytes 2457604
  87.5 99.6 %copy-start.3 = (f32[648,512]{1,0:T(8,128)}, f32[648,512]{1,0:T(8,128)S(1)}, u32[]{:S(2)}) copy-start(f32[648,512]{1,0:T(8,128)S(1)} %get-tuple-element.764) | copy-start | bytes 3981316
  103.3 27.5 %copy-start.241 = (f32[1,1,512]{2,1,0:T(1,128)S(1)}, f32[1,1,512]{2,1,0:T(1,128)}, u32[]{:S(2)}) copy-start(f32[1,1,512]{2,1,0:T(1,128)} %copy-done.240) | copy-start | bytes 6148
  103.3 27.5 %copy-start.256 = (f32[1,1,512]{2,1,0:T(1,128)S(1)}, f32[1,1,512]{2,1,0:T(1,128)}, u32[]{:S(2)}) copy-start(f32[1,1,512]{2,1,0:T(1,128)} %get-tuple-element.712) | copy-start | bytes 6148
  131.6 55.5 %copy-start.309 = (f32[512]{0:T(512)S(1)}, f32[512]{0:T(512)}, u32[]{:S(2)}) copy-start(f32[512]{0:T(512)} %copy-done.308) | copy-start | bytes 6148
  131.6 55.5 %copy-start.336 = (f32[512]{0:T(512)S(1)}, f32[512]{0:T(512)}, u32[]{:S(2)}) copy-start(f32[512]{0:T(512)} %get-tuple-element.570) | copy-start | bytes 6148
  210.8 28.4 %copy-start.179 = (bf16[2,7,7,512]{3,2,1,0:T(8,128)(2,1)S(1)}, bf16[2,7,7,512]{3,2,1,0:T(8,128)(2,1)}, u32[]{:S(2)}) copy-start(bf16[2,7,7,512]{3,2,1,0:T(8,128)(2,1)} %slice.443) | copy-start | bytes 301060
  210.8 28.4 %copy-start.178 = (bf16[2,7,7,512]{3,2,1,0:T(8,128)(2,1)S(1)}, bf16[2,7,7,512]{3,2,1,0:T(8,128)(2,1)}, u32[]{:S(2)}) copy-start(bf16[2,7,7,512]{3,2,1,0:T(8,128)(2,1)} %slice.444) | copy-start | bytes 301060
  293.4 35.7 %copy-start.220 = (f32[2048]{0:T(1024)}, f32[2048]{0:T(1024)S(1)}, u32[]{:S(2)}) copy-start(f32[2048]{0:T(1024)S(1)} %broadcast_divide_fusion.8) | copy-start | bytes 24580
  293.5 33.1 %copy-start.216 = (f32[2048]{0:T(1024)}, f32[2048]{0:T(1024)S(1)}, u32[]{:S(2)}) copy-start(f32[2048]{0:T(1024)S(1)} %broadcast_divide_fusion.5) | copy-start | bytes 24580
  293.5 38.5 %copy-start.214 = (f32[2048]{0:T(1024)}, f32[2048]{0:T(1024)S(1)}, u32[]{:S(2)}) copy-start(f32[2048]{0:T(1024)S(1)} %broadcast_divide_fusion.2) | copy-start | bytes 24580
  297.4 29.1 %copy-start.9 = (f32[98,2048]{1,0:T(8,128)}, f32[98,2048]{1,0:T(8,128)S(1)}, u32[]{:S(2)}) copy-start(f32[98,2048]{1,0:T(8,128)S(1)} %get-tuple-element.778) | copy-start | bytes 2408452
  673.1 33.3 %copy-start.221 = (f32[2048]{0:T(1024)S(1)}, f32[2048]{0:T(1024)}, u32[]{:S(2)}) copy-start(f32[2048]{0:T(1024)} %copy-done.220) | copy-start | bytes 24580
  673.1 33.3 %copy-start.225 = (f32[2048]{0:T(1024)S(1)}, f32[2048]{0:T(1024)}, u32[]{:S(2)}) copy-start(f32[2048]{0:T(1024)} %copy-done.224) | copy-start | bytes 24580
  673.1 33.3 %copy-start.285 = (f32[2048]{0:T(1024)S(1)}, f32[2048]{0:T(1024)}, u32[]{:S(2)}) copy-start(f32[2048]{0:T(1024)} %copy-done.284) | copy-start | bytes 24580
  673.1 33.3 %copy-start.287 = (f32[2048]{0:T(1024)S(1)}, f32[2048]{0:T(1024)}, u32[]{:S(2)}) copy-start(f32[2048]{0:T(1024)} %copy-done.286) | copy-start | bytes 24580
  673.1 33.3 %copy-start.330 = (f32[2048]{0:T(1024)S(1)}, f32[2048]{0:T(1024)}, u32[]{:S(2)}) copy-start(f32[2048]{0:T(1024)} %get-tuple-element.741) | copy-start | bytes 24580
  673.1 33.3 %copy-start.331 = (f32[2048]{0:T(1024)S(1)}, f32[2048]{0:T(1024)}, u32[]{:S(2)}) copy-start(f32[2048]{0:T(1024)} %get-tuple-element.737) | copy-start | bytes 24580
  677.2 867.4 %all-reduce.86.cloned.1.call-start = ((), (), s32[]{:S(2)}) async-start(), calls=%async_computation.21 | async-start | bytes 131072
  856.5 34.3 %copy-start.152 = (f32[2,7,7,1,512]{4,0,2,1,3:T(2,128)S(1)}, f32[2,7,7,1,512]{4,0,2,1,3:T(2,128)}, u32[]{:S(2)}) copy-start(f32[2,7,7,1,512]{4,0,2,1,3:T(2,128)} %copy.1316) | copy-start | bytes 602116
  858.9 47.9 %copy-start.151 = (f32[2,7,7,1,512]{4,0,2,1,3:T(2,128)S(1)}, f32[2,7,7,1,512]{4,0,2,1,3:T(2,128)}, u32[]{:S(2)}) copy-start(f32[2,7,7,1,512]{4,0,2,1,3:T(2,128)} %copy.1315) | copy-start | bytes 602116
  874.8 47.7 %copy-start.154 = (f32[2,7,7,1,512]{4,0,2,1,3:T(2,128)S(1)}, f32[2,7,7,1,512]{4,0,2,1,3:T(2,128)}, u32[]{:S(2)}) copy-start(f32[2,7,7,1,512]{4,0,2,1,3:T(2,128)} %copy.1320) | copy-start | bytes 602116
  890.8 47.7 %copy-start.153 = (f32[2,7,7,1,512]{4,0,2,1,3:T(2,128)S(1)}, f32[2,7,7,1,512]{4,0,2,1,3:T(2,128)}, u32[]{:S(2)}) copy-start(f32[2,7,7,1,512]{4,0,2,1,3:T(2,128)} %copy.1317) | copy-start | bytes 602116
  938.5 56.4 %copy-start.150 = (f32[2,7,7,1,512]{4,0,2,1,3:T(2,128)S(1)}, f32[2,7,7,1,512]{4,0,2,1,3:T(2,128)}, u32[]{:S(2)}) copy-start(f32[2,7,7,1,512]{4,0,2,1,3:T(2,128)} %copy.1322) | copy-start | bytes 602116
  1385.1 31.4 %copy-start.304 = (f32[512]{0:T(512)S(1)}, f32[512]{0:T(512)}, u32[]{:S(2)}) copy-start(f32[512]{0:T(512)} %copy-done.301) | copy-start | bytes 6148
  1416.3 258.3 %reduce-scatter.22.cloned.1.call-start = ((), (), s32[]{:S(2)}) async-start(), calls=%async_computation.20 | async-start | bytes 2162688 | tf_op jit(solution)/shard_map/reduce_scatter | solution.py:500
  1425.9 388.2 %reduce-scatter.16.cloned.1.call-start = ((), (), s32[]{:S(2)}) async-start(), calls=%async_computation.17 | async-start | bytes 4325376 | tf_op jit(solution)/shard_map/reduce_scatter | solution.py:504
  1431.6 521.3 %reduce-scatter.20.cloned.1.call-start = ((), (), s32[]{:S(2)}) async-start(), calls=%async_computation.19 | async-start | bytes 4325376 | tf_op jit(solution)/shard_map/reduce_scatter | solution.py:506
  1437.6 654.6 %reduce-scatter.12.cloned.1.call-start = ((), (), s32[]{:S(2)}) async-start(), calls=%async_computation.15 | async-start | bytes 4325376 | tf_op jit(solution)/shard_map/reduce_scatter | solution.py:502
  1443.6 785.9 %reduce-scatter.18.cloned.1.call-start = ((), (), s32[]{:S(2)}) async-start(), calls=%async_computation.18 | async-start | bytes 9732096 | tf_op jit(solution)/shard_map/reduce_scatter | solution.py:505
  1456.3 914.6 %reduce-scatter.10.cloned.1.call-start = ((), (), s32[]{:S(2)}) async-start(), calls=%async_computation.14 | async-start | bytes 9732096 | tf_op jit(solution)/shard_map/reduce_scatter | solution.py:501
  1465.4 1055.4 %reduce-scatter.14.cloned.1.call-start = ((), (), s32[]{:S(2)}) async-start(), calls=%async_computation.16 | async-start | bytes 8650752 | tf_op jit(solution)/shard_map/reduce_scatter | solution.py:503
  1542.0 132.7 %copy-start.198 = (f32[32,512]{1,0:T(8,128)S(1)}, f32[32,512]{1,0:T(8,128)}, u32[]{:S(2)}) copy-start(f32[32,512]{1,0:T(8,128)} %param.42) | copy-start | bytes 196612
  1542.0 132.6 %copy-start.296 = (f32[32,512]{1,0:T(8,128)S(1)}, f32[32,512]{1,0:T(8,128)}, u32[]{:S(2)}) copy-start(f32[32,512]{1,0:T(8,128)} %param.50) | copy-start | bytes 196612
  1542.0 132.6 %copy-start.297 = (f32[32,512]{1,0:T(8,128)S(1)}, f32[32,512]{1,0:T(8,128)}, u32[]{:S(2)}) copy-start(f32[32,512]{1,0:T(8,128)} %param.58) | copy-start | bytes 196612
  1542.0 272.1 %copy-start.170 = (f32[64,512]{1,0:T(8,128)S(1)}, f32[64,512]{1,0:T(8,128)}, u32[]{:S(2)}) copy-start(f32[64,512]{1,0:T(8,128)} %param.46) | copy-start | bytes 393220
  1542.0 272.1 %copy-start.231 = (f32[64,512]{1,0:T(8,128)S(1)}, f32[64,512]{1,0:T(8,128)}, u32[]{:S(2)}) copy-start(f32[64,512]{1,0:T(8,128)} %param.54) | copy-start | bytes 393220
  1542.0 272.1 %copy-start.232 = (f32[64,512]{1,0:T(8,128)S(1)}, f32[64,512]{1,0:T(8,128)}, u32[]{:S(2)}) copy-start(f32[64,512]{1,0:T(8,128)} %param.62) | copy-start | bytes 393220
  1542.0 410.9 %copy-start.172 = (f32[512,64]{0,1:T(8,128)S(1)}, f32[512,64]{0,1:T(8,128)}, u32[]{:S(2)}) copy-start(f32[512,64]{0,1:T(8,128)} %param.48) | copy-start | bytes 393220
  1542.0 410.9 %copy-start.233 = (f32[512,64]{0,1:T(8,128)S(1)}, f32[512,64]{0,1:T(8,128)}, u32[]{:S(2)}) copy-start(f32[512,64]{0,1:T(8,128)} %param.56) | copy-start | bytes 393220
  1542.1 410.9 %copy-start.234 = (f32[512,64]{0,1:T(8,128)S(1)}, f32[512,64]{0,1:T(8,128)}, u32[]{:S(2)}) copy-start(f32[512,64]{0,1:T(8,128)} %param.64) | copy-start | bytes 393220
  1544.5 547.7 %copy-start.173 = (f32[512,64]{0,1:T(8,128)S(1)}, f32[512,64]{0,1:T(8,128)}, u32[]{:S(2)}) copy-start(f32[512,64]{0,1:T(8,128)} %param.44) | copy-start | bytes 393220
  1544.5 547.7 %copy-start.235 = (f32[512,64]{0,1:T(8,128)S(1)}, f32[512,64]{0,1:T(8,128)}, u32[]{:S(2)}) copy-start(f32[512,64]{0,1:T(8,128)} %param.52) | copy-start | bytes 393220
  1544.5 547.7 %copy-start.236 = (f32[512,64]{0,1:T(8,128)S(1)}, f32[512,64]{0,1:T(8,128)}, u32[]{:S(2)}) copy-start(f32[512,64]{0,1:T(8,128)} %param.60) | copy-start | bytes 393220
  1546.0 683.6 %copy-start.136 = (f32[144,512]{1,0:T(8,128)S(1)}, f32[144,512]{1,0:T(8,128)}, u32[]{:S(2)}) copy-start(f32[144,512]{1,0:T(8,128)} %param.47) | copy-start | bytes 884740
  1546.0 683.6 %copy-start.192 = (f32[144,512]{1,0:T(8,128)S(1)}, f32[144,512]{1,0:T(8,128)}, u32[]{:S(2)}) copy-start(f32[144,512]{1,0:T(8,128)} %param.55) | copy-start | bytes 884740
  1546.0 683.6 %copy-start.193 = (f32[144,512]{1,0:T(8,128)S(1)}, f32[144,512]{1,0:T(8,128)}, u32[]{:S(2)}) copy-start(f32[144,512]{1,0:T(8,128)} %param.63) | copy-start | bytes 884740
  1954.7 416.2 %copy-start.137 = (f32[144,512]{1,0:T(8,128)S(1)}, f32[144,512]{1,0:T(8,128)}, u32[]{:S(2)}) copy-start(f32[144,512]{1,0:T(8,128)} %param.43) | copy-start | bytes 884740
  1954.7 416.2 %copy-start.194 = (f32[144,512]{1,0:T(8,128)S(1)}, f32[144,512]{1,0:T(8,128)}, u32[]{:S(2)}) copy-start(f32[144,512]{1,0:T(8,128)} %param.51) | copy-start | bytes 884740
  1954.7 416.2 %copy-start.195 = (f32[144,512]{1,0:T(8,128)S(1)}, f32[144,512]{1,0:T(8,128)}, u32[]{:S(2)}) copy-start(f32[144,512]{1,0:T(8,128)} %param.59) | copy-start | bytes 884740
  2231.6 289.3 %copy-start.138 = (f32[1024,64]{0,1:T(8,128)S(1)}, f32[1024,64]{0,1:T(8,128)}, u32[]{:S(2)}) copy-start(f32[1024,64]{0,1:T(8,128)} %param.45) | copy-start | bytes 786436
  2231.6 289.3 %copy-start.196 = (f32[1024,64]{0,1:T(8,128)S(1)}, f32[1024,64]{0,1:T(8,128)}, u32[]{:S(2)}) copy-start(f32[1024,64]{0,1:T(8,128)} %param.53) | copy-start | bytes 786436
  2231.6 289.3 %copy-start.197 = (f32[1024,64]{0,1:T(8,128)S(1)}, f32[1024,64]{0,1:T(8,128)}, u32[]{:S(2)}) copy-start(f32[1024,64]{0,1:T(8,128)} %param.61) | copy-start | bytes 786436
  (347 other events, 1618.4 us)
Sparse Core Ops, SparseCore 0:
  11.5 56.4 all-gather.8
  71.0 62.4 all-gather.10
  136.9 55.1 all-gather.12
  195.5 60.8 all-gather.14
  259.7 55.0 all-gather.16
  317.5 62.4 all-gather.18
  383.5 55.1 all-gather.20
  677.3 26.6 all-reduce.87
  1416.4 118.1 all-reduce.85
  1536.9 137.7 reduce-scatter.21
  1676.9 137.1 reduce-scatter.15
  1816.2 136.7 reduce-scatter.19
  1955.3 136.9 reduce-scatter.11
  2098.0 131.5 reduce-scatter.17
  2236.3 134.5 reduce-scatter.9
  2373.1 147.7 reduce-scatter.13
where the time goes:
time: 2560 us; the launch traced here: 2530 us
  local copies, waits for them, and re-layouts  998 us (39%)
  waiting for transfers between devices  991 us (39%)
  blocking collectives  212 us (8%)
  matrix products  158 us (6%)
  other arithmetic  149 us (6%)
    slice x18, local copies, waits for them, and re-layouts, fold_taps(): return folded[:, 1:-1, 1:-1, :]  242 us
    pad x9, local copies, waits for them, and re-layouts, fold_taps(): lax.pad(shaped[:, :, :, tap_index, :], jnp.zeros((), jnp.float32), ((0, 0...  201 us
    unnamed x854, local copies, waits for them, and re-layouts  192 us
    reduce_scatter x1, waiting for transfers between devices, on_device(): lax.psum_scatter(proj_total[3], ('dp', 'bn'), scatter_dimension=1, tiled=...  148 us
    slice x30, local copies, waits for them, and re-layouts, collect_taps(): lax.slice(padded, (0, tap_row, tap_col, 0), (number, tap_row + extent, ta...  143 us
    reduce_scatter x1, waiting for transfers between devices, on_device(): lax.psum_scatter(proj_total[1], ('dp', 'bn'), scatter_dimension=0, tiled=...  139 us
    reduce_scatter x1, waiting for transfers between devices, on_device(): lax.psum_scatter(ident_total[0], ('dp', 'bn'), scatter_dimension=0, tiled...  138 us
    reduce_scatter x1, waiting for transfers between devices, on_device(): lax.psum_scatter(proj_total[2], ('dp', 'bn'), scatter_dimension=1, tiled=...  138 us
  transfers between devices with their start and end apart: 16, of which 8 were waited for; matrix products, arithmetic and copies ran while one was open for 18% of the time, Pallas kernels for 0%

commit v1 on v0

v1 whole, which is shorter than its diff:
```python
import jax
import jax.numpy as jnp
import numpy as np
from jax import lax
from jax.experimental import pallas as pl
from jax.experimental.pallas import tpu as pltpu
from jax.sharding import PartitionSpec as P

STEP = 10
EPSILON = 1e-05
RATE_CONV = 0.03
RATE_NORM = 0.4
DECAY_CONV = 0.05
BF = jnp.bfloat16
F32 = jnp.float32
MID = 512
HALO = 32
NORM_ROW = {"1": 0, "2": 1, "3": 2, "S": 6, "4": 10, "5": 11, "6": 12}


class Grid:
    def __init__(self, counts, sides):
        self.counts, self.sides = counts, sides
        self.seg, self.size = [], []
        at = 0
        for number, side in zip(counts, sides):
            rows = -(-number * (side + 1) ** 2 // 16) * 16
            self.seg.append(at)
            self.size.append(rows)
            at += rows
        self.rows = at

    def lines(self):
        for which, (number, side) in enumerate(zip(self.counts, self.sides)):
            for line in range(side):
                for column in range(side):
                    yield which, line, column, self.seg[which] + (line * (side + 1) + column) * number


def silu(v):
    return v * jax.nn.sigmoid(v)


def slope(v):
    s = jax.nn.sigmoid(v)
    return s * (1.0 + v * (1.0 - s))


def dot_nn(a, b):
    return lax.dot_general(a, b, (((1,), (0,)), ((), ())), preferred_element_type=F32)


def dot_nt(a, b):
    return lax.dot_general(a, b, (((1,), (1,)), ((), ())), preferred_element_type=F32)


def dot_tn(a, b):
    return lax.dot_general(a, b, (((0,), (0,)), ((), ())), preferred_element_type=F32)


def aligned(row):
    return pl.multiple_of(row, 16)


def wide(mask):
    return jnp.concatenate([mask] * (MID // 128), axis=1)


VM = pl.BlockSpec(memory_space=pltpu.VMEM)
SM = pl.BlockSpec(memory_space=pltpu.SMEM)
HB = pl.BlockSpec(memory_space=pl.ANY)


def call(body, ins, outs, scratch=(), flops=0, moved=0, aliases=None):
    return pl.pallas_call(
        body,
        out_shape=[jax.ShapeDtypeStruct(shape, dtype) for shape, dtype, _ in outs],
        in_specs=[spec for _, spec in ins],
        out_specs=[spec for _, _, spec in outs],
        scratch_shapes=list(scratch),
        input_output_aliases=aliases or {},
        compiler_params=pltpu.CompilerParams(vmem_limit_bytes=58 * 1024 * 1024),
        cost_estimate=pl.CostEstimate(flops=flops, bytes_accessed=moved, transcendentals=0),
    )(*[array for array, _ in ins])


class Device:
    def __init__(self, grid, blocks, members):
        self.g = grid
        self.blocks = blocks
        self.members = members
        self.R = grid.rows


    def chunks(self, body):
        for which in range(3):
            start = self.g.seg[which]

            def step(i, _, which=which, start=start):
                body(which, aligned(start + i * 16))
                return 0

            lax.fori_loop(0, self.g.size[which] // 16, step, 0)

    def load_start(self, layout, ids, refs, off, rows, dst, sem):
        for ref, (base, places) in zip(refs, layout):
            low, high = max(base, off), min(base + ref.shape[1], off + rows)
            if high <= low:
                continue
            for pos, rel in enumerate(places):
                block = rel ^ ids[0]
                pltpu.make_async_copy(
                    ref.at[pos, pl.ds(low - base, high - low), :],
                    dst.at[pl.ds(pl.multiple_of(block * rows + (low - off), 16), high - low), :],
                    sem,
                ).start()

    def load_wait(self, dst, sem):
        pltpu.make_async_copy(dst, dst, sem).wait()

    def store_start(self, chains, ids, src, rows, split, offs, refs, sems):
        at, lo = 0, 0
        for places_list, take, off in zip(chains, split, offs):
            for places in places_list:
                for pos, rel in enumerate(places):
                    block = rel ^ ids[0]
                    pltpu.make_async_copy(
                        src.at[pl.ds(pl.multiple_of(block * rows + lo, 16), take), :],
                        refs[at].at[pos, pl.ds(off, take), :],
                        sems.at[at],
                    ).start()
                at += 1
            lo += take

    def store_wait(self, refs, sems, spans):
        for which, (ref, (off, size)) in enumerate(zip(refs, spans)):
            view = ref.at[:, pl.ds(off, size), :]
            pltpu.make_async_copy(view, view, sems.at[which]).wait()

    def local_stats(self, c_ref, m_ref, sc, out_ref, at, area, phases=1):
        cols = c_ref.shape[1]
        out_ref[pl.ds(at, 8), :] = jnp.zeros((8, cols), F32)
        for which in range(3):
            start, size = self.g.seg[which], self.g.size[which]
            held = sc[0, which] * float(area[which])
            for q in range(cols // MID):
                lane = slice(q * MID, (q + 1) * MID)

                def first(i, acc, start=start, lane=lane):
                    row = aligned(start + i * 16)
                    m = wide(m_ref[pl.ds(row, 16), :])
                    for phase in range(phases):
                        v = c_ref[pl.ds(aligned(row + phase * self.R), 16), lane] * m
                        acc = acc + v[:8] + v[8:]
                    return acc

                acc = lax.fori_loop(0, size // 16, first, jnp.zeros((8, MID), F32))
                total = jnp.sum(acc, axis=0, keepdims=True)
                mean = total / held

                def second(i, acc, start=start, lane=lane, mean=mean):
                    row = aligned(start + i * 16)
                    m = wide(m_ref[pl.ds(row, 16), :])
                    for phase in range(phases):
                        v = c_ref[pl.ds(aligned(row + phase * self.R), 16), lane] - mean
                        v = v * v * m
                        acc = acc + v[:8] + v[8:]
                    return acc

                acc = lax.fori_loop(0, size // 16, second, jnp.zeros((8, MID), F32))
                out_ref[at + which : at + which + 1, lane] = total
                out_ref[at + 3 + which : at + 4 + which, lane] = jnp.sum(acc, axis=0, keepdims=True)

    def group_norm(self, st_refs, at, sc, area, out_ref):
        cols = out_ref.shape[1]
        out_ref[...] = jnp.zeros(out_ref.shape, F32)
        for which in range(3):
            count = sc[self.members, which] * float(area[which])
            sums = [ref[at + which : at + which + 1, :] for ref in st_refs]
            mean = sum(sums[1:], sums[0]) / count
            spread = jnp.zeros((1, cols), F32)
            for k, ref in enumerate(st_refs):
                held = sc[k, which] * float(area[which])
                apart = sums[k] / held - mean
                spread = spread + (ref[at + 3 + which : at + 4 + which, :] + held * apart * apart)
            out_ref[which : which + 1, :] = mean
            out_ref[3 + which : 4 + which, :] = lax.rsqrt(spread / count + EPSILON)

    def group_sums(self, st_refs, at, sc, area, out_ref):
        out_ref[...] = jnp.zeros(out_ref.shape, F32)
        for which in range(3):
            count = sc[self.members, which] * float(area[which])
            for row in (which, 3 + which):
                rows = [ref[at + row : at + row + 1, :] for ref in st_refs]
                out_ref[row : row + 1, :] = sum(rows[1:], rows[0]) / count

    def xhat(self, c_ref, nrm, which, row, lane=slice(0, MID)):
        return (c_ref[pl.ds(row, 16), lane] - nrm[which : which + 1, lane]) * nrm[3 + which : 4 + which, lane]

    def affine(self, normp, name, q, xh):
        at = NORM_ROW[name] + q
        return normp[at : at + 1, :] * xh + normp[16 + at : 17 + at, :]

    def norm_back(self, normp, name, q, nrm, sums, which, lane, dz, xh, m):
        at = NORM_ROW[name] + q
        a = sums[which : which + 1, lane]
        b = sums[3 + which : 4 + which, lane]
        scale = normp[at : at + 1, :] * nrm[3 + which : 4 + which, lane]
        return scale * (dz - m * (a + xh * b))

    def add_rows(self, out_ref, row, value, lane=slice(0, MID)):
        out_ref[row : row + 1, lane] = out_ref[row : row + 1, lane] + jnp.sum(value, axis=0, keepdims=True)

    def shifted(self, hs_ref, dst_ref, col, sign_r, sign_c):
        for which in range(3):
            off = (sign_r * (self.g.sides[which] + 1) + sign_c) * self.g.counts[which]
            for i in range(self.g.size[which] // 16):
                row = self.g.seg[which] + i * 16
                dst_ref[row : row + 16, col : col + MID] = hs_ref[HALO + row + off : HALO + row + off + 16, :].astype(BF)

    def clear_halo(self, hs_ref):
        hs_ref[0:HALO, :] = jnp.zeros((HALO, MID), F32)
        hs_ref[HALO + self.R : 2 * HALO + self.R, :] = jnp.zeros((HALO, MID), F32)

    def area(self, side_scale):
        return [(side_scale * side) ** 2 for side in self.g.sides]


    def prepare(self, spot, lives, pictures):
        R = self.R
        g = self.g
        width = pictures[0].shape[3]
        members = self.members

        def body(spot, la, lb, lc, xa, xb, xc, xp, msk, sc, big):
            x_refs, l_refs = (xa, xb, xc), (la, lb, lc)
            own = []
            for which in range(3):
                per = g.counts[which]
                whole = jnp.zeros((), jnp.int32)
                for k in range(members):
                    first = (spot[0] * members + (spot[1] ^ k)) * per
                    flags = [l_refs[which][first + i] for i in range(per)]
                    held = sum(flags[1:], flags[0])
                    sc[k, which] = held.astype(F32)
                    whole = whole + held
                    if k == 0:
                        own.append(flags)
                sc[members, which] = whole.astype(F32)
            big[...] = jnp.zeros(big.shape, F32)
            msk[...] = jnp.zeros(msk.shape, F32)
            alive = []
            for which in range(3):
                per = g.counts[which]
                slot = lax.broadcasted_iota(jnp.int32, (per, 128), 0)
                mask = jnp.zeros((per, 128), F32)
                for i in range(per):
                    mask = jnp.where(slot == i, own[which][i].astype(F32), mask)
                alive.append(mask)
            for which, line, column, row in g.lines():
                per = g.counts[which]
                msk[row : row + per, :] = alive[which]
                for phase in range(4):
                    odd, second = divmod(phase, 2)
                    base = phase * R + row
                    big[base : base + per, :] = x_refs[which][2 * line + odd, 2 * column + second].astype(F32)

            def cast(i, _):
                row = aligned(i * 16)
                xp[pl.ds(row, 16), :] = big[pl.ds(row, 16), :].astype(BF)
                return 0

            lax.fori_loop(0, 4 * R // 16, cast, 0)

        return call(
            body,
            [(spot, SM)] + [(l, SM) for l in lives] + [(p, VM) for p in pictures],
            [((4 * R, width), BF, VM), ((R, 128), F32, VM), ((members + 1, 3), F32, SM)],
            [pltpu.VMEM((4 * R, width), F32)],
        )

    def conv_one(self, ids, sc, xp, msk, w, off, rows, norm_off):
        R = self.R
        width = xp.shape[1]
        layout, arrays = w
        with_norm = norm_off is not None

        def body(ids, sc, xp, msk, *rest):
            refs = rest[: len(arrays)]
            rest = rest[len(arrays) :]
            if with_norm:
                c, st, normp, ws, ns, sem, sem2 = rest
                self.load_start(layout, ids, refs, norm_off, 16, ns, sem2)
            else:
                c, st, ws, sem = rest
            self.load_start(layout, ids, refs, off, rows, ws, sem)
            if with_norm:
                self.load_wait(ns, sem2)
                for b in range(self.blocks):
                    normp[b : b + 1, :] = ns[b * 16 : b * 16 + 16, :].astype(F32)[0:1, :]
            self.load_wait(ws, sem)
            for phase in range(4):
                c[phase * R : (phase + 1) * R, :] = dot_nn(xp[phase * R : (phase + 1) * R, :], ws[...])
            self.local_stats(c, msk, sc, st, 0, self.area(2), 4)

        outs = [((4 * R, MID), F32, VM), ((8, MID), F32, VM)]
        scratch = [pltpu.VMEM((width, MID), BF)]
        if with_norm:
            outs.append(((32, MID), F32, VM))
            scratch.append(pltpu.VMEM((self.blocks * 16, MID), BF))
            scratch.append(pltpu.SemaphoreType.DMA)
        scratch.append(pltpu.SemaphoreType.DMA)
        return call(
            body,
            [(ids, SM), (sc, SM), (xp, VM), (msk, VM)] + [(a, HB) for a in arrays],
            outs,
            scratch,
            flops=2 * 4 * R * width * MID,
        )

    @staticmethod
    def tap_two(tap):
        i, j = divmod(tap, 3)
        return (0 if i == 1 else 2) + (0 if j == 1 else 1), (1 if i == 0 else 0), (1 if j == 0 else 0)

    def conv_two(self, ids, sc, c1, sts, normp, msk, w, off, rows):
        R = self.R
        layout, arrays = w
        nst, nw = len(sts), len(arrays)

        def body(ids, sc, c1, normp, msk, *rest):
            st_refs, refs = rest[:nst], rest[nst : nst + nw]
            a1, nrm, c2, st, ws, hs, patches, sem = rest[nst + nw :]
            self.load_start(layout, ids, refs, off, rows, ws, sem)
            self.group_norm(st_refs, 0, sc, self.area(2), nrm)
            self.clear_halo(hs)
            for phase in range(4):

                def act(which, row, phase=phase):
                    at = aligned(row + phase * R)
                    m = wide(msk[pl.ds(row, 16), :])
                    v = silu(self.affine(normp, "1", 0, self.xhat(c1, nrm, which, at))) * m
                    hs[pl.ds(aligned(row + HALO), 16), :] = v
                    a1[pl.ds(at, 16), :] = v.astype(BF)

                self.chunks(act)
                for tap in range(9):
                    source, back_r, back_c = self.tap_two(tap)
                    if source == phase:
                        self.shifted(hs, patches, tap * MID, -back_r, -back_c)
            self.load_wait(ws, sem)
            c2[...] = dot_nn(patches[...], ws[...])
            self.local_stats(c2, msk, sc, st, 0, self.area(1))

        return call(
            body,
            [(ids, SM), (sc, SM), (c1, VM), (normp, VM), (msk, VM)] + [(s, VM) for s in sts] + [(a, HB) for a in arrays],
            [((4 * R, MID), BF, VM), ((8, MID), F32, VM), ((R, MID), F32, VM), ((8, MID), F32, VM)],
            [
                pltpu.VMEM((9 * MID, MID), BF),
                pltpu.VMEM((R + 2 * HALO, MID), F32),
                pltpu.VMEM((R, 9 * MID), BF),
                pltpu.SemaphoreType.DMA,
            ],
            flops=2 * 9 * R * MID * MID,
        )

    def conv_short(self, ids, sc, xp, msk, w, off, rows):
        R = self.R
        layout, arrays = w
        nw = len(arrays)
        out_width = self.blocks * rows if self.blocks > 1 else rows

        def body(ids, sc, xp, msk, *rest):
            refs = rest[:nw]
            c, st, wa, wb, sem = rest[nw:]
            self.load_start(layout, ids, refs, off, rows, wa, sem.at[0])
            self.load_start(layout, ids, refs, off + rows, rows, wb, sem.at[1])
            self.load_wait(wa, sem.at[0])
            self.load_wait(wb, sem.at[1])
            for q in range(out_width // MID):
                lane = slice(q * MID, (q + 1) * MID)
                c[:, lane] = dot_nt(xp[0:R, 0:MID], wa[lane, :]) + dot_nt(xp[0:R, MID : 2 * MID], wb[lane, :])
            self.local_stats(c, msk, sc, st, 0, self.area(1))

        return call(
            body,
            [(ids, SM), (sc, SM), (xp, VM), (msk, VM)] + [(a, HB) for a in arrays],
            [((R, out_width), F32, VM), ((8, out_width), F32, VM)],
            [pltpu.VMEM((out_width, MID), BF), pltpu.VMEM((out_width, MID), BF), pltpu.SemaphoreType.DMA((2,))],
            flops=2 * R * 2 * MID * out_width,
        )

    def conv_expand(self, ids, sc, c, sts, normp, msk, w, off, rows, name, more=None):
        R = self.R
        layout, arrays = w
        nst, nw = len(sts), len(arrays)
        out_width = self.blocks * rows if self.blocks > 1 else rows
        stat_rows = 8 if more is None else 16

        def body(ids, sc, c, normp, msk, *rest):
            st_refs, refs = rest[:nst], rest[nst : nst + nw]
            rest = rest[nst + nw :]
            if more is not None:
                more_ref, rest = rest[0], rest[1:]
            act, nrm, prod, st, ws, sem = rest
            self.load_start(layout, ids, refs, off, rows, ws, sem)
            self.group_norm(st_refs, 0, sc, self.area(1), nrm)

            def one(which, row):
                m = wide(msk[pl.ds(row, 16), :])
                v = silu(self.affine(normp, name, 0, self.xhat(c, nrm, which, row))) * m
                act[pl.ds(row, 16), :] = v.astype(BF)

            self.chunks(one)
            self.load_wait(ws, sem)
            for q in range(out_width // MID):
                lane = slice(q * MID, (q + 1) * MID)
                prod[:, lane] = dot_nt(act[...], ws[lane, :])
            self.local_stats(prod, msk, sc, st, 0, self.area(1))
            if more is not None:
                st[8:16, :] = more_ref[...]

        ins = [(ids, SM), (sc, SM), (c, VM), (normp, VM), (msk, VM)] + [(s, VM) for s in sts] + [(a, HB) for a in arrays]
        if more is not None:
            ins.append((more, VM))
        return call(
            body,
            ins,
            [((R, MID), BF, VM), ((8, MID), F32, VM), ((R, out_width), F32, VM), ((stat_rows, out_width), F32, VM)],
            [pltpu.VMEM((out_width, MID), BF), pltpu.SemaphoreType.DMA],
            flops=2 * R * MID * out_width,
        )

    def conv_four(self, ids, sc, c3, cs, sts, normp, msk, w, off, rows):
        R = self.R
        layout, arrays = w
        nst, nw = len(sts), len(arrays)
        out_width = c3.shape[1]

        def body(ids, sc, c3, cs, normp, msk, *rest):
            st_refs, refs = rest[:nst], rest[nst : nst + nw]
            h, hb, nrm3, nrms, c4, st, ws, sem = rest[nst + nw :]
            self.load_start(layout, ids, refs, off, rows, ws, sem)
            self.group_norm(st_refs, 0, sc, self.area(1), nrm3)
            self.group_norm(st_refs, 8, sc, self.area(1), nrms)

            def one(which, row):
                m = wide(msk[pl.ds(row, 16), :])
                for q in range(out_width // MID):
                    lane = slice(q * MID, (q + 1) * MID)
                    pre = self.affine(normp, "3", q, self.xhat(c3, nrm3, which, row, lane)) + self.affine(
                        normp, "S", q, self.xhat(cs, nrms, which, row, lane)
                    )
                    v = silu(pre) * m
                    h[pl.ds(row, 16), lane] = v
                    hb[pl.ds(row, 16), lane] = v.astype(BF)

            self.chunks(one)
            self.load_wait(ws, sem)
            c4[...] = dot_nn(hb[...], ws[...])
            self.local_stats(c4, msk, sc, st, 0, self.area(1))

        return call(
            body,
            [(ids, SM), (sc, SM), (c3, VM), (cs, VM), (normp, VM), (msk, VM)]
            + [(s, VM) for s in sts]
            + [(a, HB) for a in arrays],
            [
                ((R, out_width), F32, VM),
                ((R, out_width), BF, VM),
                ((8, out_width), F32, VM),
                ((8, out_width), F32, VM),
                ((R, MID), F32, VM),
                ((8, MID), F32, VM),
            ],
            [pltpu.VMEM((out_width, MID), BF), pltpu.SemaphoreType.DMA],
            flops=2 * R * MID * out_width,
        )

    def conv_five(self, ids, sc, c4, sts, normp, msk, w, off, rows):
        R = self.R
        layout, arrays = w
        nst, nw = len(sts), len(arrays)

        def body(ids, sc, c4, normp, msk, *rest):
            st_refs, refs = rest[:nst], rest[nst : nst + nw]
            a4, nrm, c5, st, ws, hs, patches, sem = rest[nst + nw :]
            self.load_start(layout, ids, refs, off, rows, ws, sem)
            self.group_norm(st_refs, 0, sc, self.area(1), nrm)
            self.clear_halo(hs)

            def act(which, row):
                m = wide(msk[pl.ds(row, 16), :])
                v = silu(self.affine(normp, "4", 0, self.xhat(c4, nrm, which, row))) * m
                hs[pl.ds(aligned(row + HALO), 16), :] = v
                a4[pl.ds(row, 16), :] = v.astype(BF)

            self.chunks(act)
            for tap in range(9):
                i, j = divmod(tap, 3)
                self.shifted(hs, patches, tap * MID, i - 1, j - 1)
            self.load_wait(ws, sem)
            c5[...] = dot_nn(patches[...], ws[...])
            self.local_stats(c5, msk, sc, st, 0, self.area(1))

        return call(
            body,
            [(ids, SM), (sc, SM), (c4, VM), (normp, VM), (msk, VM)] + [(s, VM) for s in sts] + [(a, HB) for a in arrays],
            [((R, MID), BF, VM), ((8, MID), F32, VM), ((R, MID), F32, VM), ((8, MID), F32, VM)],
            [
                pltpu.VMEM((9 * MID, MID), BF),
                pltpu.VMEM((R + 2 * HALO, MID), F32),
                pltpu.VMEM((R, 9 * MID), BF),
                pltpu.SemaphoreType.DMA,
            ],
            flops=2 * 9 * R * MID * MID,
        )

    def finish(self, sc, c6, h, sts, normp, msk, ups):
        R = self.R
        g = self.g
        nst = len(sts)
        out_width = c6.shape[1]

        def body(sc, c6, h, normp, msk, ua, ub, uc, *rest):
            st_refs = rest[:nst]
            oa, ob, oc, dz, nrm, st, up, res = rest[nst:]
            u_refs, o_refs = (ua, ub, uc), (oa, ob, oc)
            self.group_norm(st_refs, 0, sc, self.area(1), nrm)
            up[...] = jnp.zeros(up.shape, F32)
            st[...] = jnp.zeros(st.shape, F32)
            for which, line, column, row in g.lines():
                up[row : row + g.counts[which], :] = u_refs[which][line, column].astype(F32)

            def one(which, row):
                m = wide(msk[pl.ds(row, 16), :])
                for q in range(out_width // MID):
                    lane = slice(q * MID, (q + 1) * MID)
                    xh = self.xhat(c6, nrm, which, row, lane)
                    pre = self.affine(normp, "6", q, xh) + h[pl.ds(row, 16), lane]
                    s = jax.nn.sigmoid(pre)
                    res[pl.ds(row, 16), lane] = m * (pre * s)
                    d = up[pl.ds(row, 16), lane] * m * (s * (1.0 + pre * (1.0 - s)))
                    dz[pl.ds(row, 16), lane] = d
                    self.add_rows(st, which, d, lane)
                    self.add_rows(st, 3 + which, d * xh, lane)

            self.chunks(one)
            for which, line, column, row in g.lines():
                o_refs[which][line, column] = res[row : row + g.counts[which], :].astype(BF)

        return call(
            body,
            [(sc, SM), (c6, VM), (h, VM), (normp, VM), (msk, VM)] + [(u, VM) for u in ups] + [(s, VM) for s in sts],
            [(u.shape, BF, VM) for u in ups]
            + [((R, out_width), F32, VM), ((8, out_width), F32, VM), ((8, out_width), F32, VM)],
            [pltpu.VMEM((R, out_width), F32), pltpu.VMEM((R, out_width), F32)],
        )

    def back_six(self, ids, sc, dz, c6, nrm6, sts, normp, msk, c5, nrm5, w, off, rows):
        R = self.R
        layout, arrays = w
        nst, nw = len(sts), len(arrays)
        out_width = c6.shape[1]

        def body(ids, sc, dz, c6, nrm6, normp, msk, c5, nrm5, *rest):
            st_refs, refs = rest[:nst], rest[nst : nst + nw]
            dc, dz5, st, sums, ws, sem = rest[nst + nw :]
            self.load_start(layout, ids, refs, off, rows, ws, sem)
            self.group_sums(st_refs, 0, sc, self.area(1), sums)
            st[...] = jnp.zeros(st.shape, F32)

            def one(which, row):
                m = wide(msk[pl.ds(row, 16), :])
                for q in range(out_width // MID):
                    lane = slice(q * MID, (q + 1) * MID)
                    xh = self.xhat(c6, nrm6, which, row, lane)
                    v = self.norm_back(normp, "6", q, nrm6, sums, which, lane, dz[pl.ds(row, 16), lane], xh, m)
                    dc[pl.ds(row, 16), lane] = v.astype(BF)

            self.chunks(one)
            self.load_wait(ws, sem)
            dz5[...] = dot_nn(dc[...], ws[...])
            self.through(dz5, c5, nrm5, normp, "5", msk, st)

        return call(
            body,
            [(ids, SM), (sc, SM), (dz, VM), (c6, VM), (nrm6, VM), (normp, VM), (msk, VM), (c5, VM), (nrm5, VM)]
            + [(s, VM) for s in sts]
            + [(a, HB) for a in arrays],
            [((R, out_width), BF, VM), ((R, MID), F32, VM), ((8, MID), F32, VM)],
            [pltpu.VMEM((8, out_width), F32), pltpu.VMEM((out_width, MID), BF), pltpu.SemaphoreType.DMA],
            flops=2 * R * MID * out_width,
        )

    def through(self, dz, c, nrm, normp, name, msk, st, phases=1):
        def one(which, row):
            m = wide(msk[pl.ds(row, 16), :])
            for phase in range(phases):
                at = aligned(row + phase * self.R)
                xh = self.xhat(c, nrm, which, at)
                d = dz[pl.ds(at, 16), :] * slope(self.affine(normp, name, 0, xh)) * m
                dz[pl.ds(at, 16), :] = d
                self.add_rows(st, which, d)
                self.add_rows(st, 3 + which, d * xh)

        self.chunks(one)

    def back_five(self, ids, sc, dz5, c5, nrm5, sts, normp, msk, c4, nrm4, w, off, rows):
        R = self.R
        layout, arrays = w
        nst, nw = len(sts), len(arrays)

        def body(ids, sc, dz5, c5, nrm5, normp, msk, c4, nrm4, *rest):
            st_refs, refs = rest[:nst], rest[nst : nst + nw]
            dc, dz4, st, sums, ws, hs, patches, sem = rest[nst + nw :]
            self.load_start(layout, ids, refs, off, rows, ws, sem)
            self.group_sums(st_refs, 0, sc, self.area(1), sums)
            self.clear_halo(hs)
            st[...] = jnp.zeros(st.shape, F32)
            self.own_dc(dz5, c5, nrm5, sums, normp, "5", msk, dc, hs)
            for tap in range(9):
                i, j = divmod(tap, 3)
                self.shifted(hs, patches, tap * MID, 1 - i, 1 - j)
            self.load_wait(ws, sem)
            for tap in range(9):
                part = dot_nt(patches[:, tap * MID : (tap + 1) * MID], ws[tap * MID : (tap + 1) * MID, :])
                if tap == 0:
                    dz4[...] = part
                else:
                    dz4[...] += part
            self.through(dz4, c4, nrm4, normp, "4", msk, st)

        return call(
            body,
            [(ids, SM), (sc, SM), (dz5, VM), (c5, VM), (nrm5, VM), (normp, VM), (msk, VM), (c4, VM), (nrm4, VM)]
            + [(s, VM) for s in sts]
            + [(a, HB) for a in arrays],
            [((R, MID), BF, VM), ((R, MID), F32, VM), ((8, MID), F32, VM)],
            [
                pltpu.VMEM((8, MID), F32),
                pltpu.VMEM((9 * MID, MID), BF),
                pltpu.VMEM((R + 2 * HALO, MID), F32),
                pltpu.VMEM((R, 9 * MID), BF),
                pltpu.SemaphoreType.DMA,
            ],
            flops=2 * 9 * R * MID * MID,
        )

    def own_dc(self, dz, c, nrm, sums, normp, name, msk, dc, hs=None, phases=1):
        def one(which, row):
            m = wide(msk[pl.ds(row, 16), :])
            for phase in range(phases):
                at = aligned(row + phase * self.R)
                xh = self.xhat(c, nrm, which, at)
                v = self.norm_back(normp, name, 0, nrm, sums, which, slice(0, MID), dz[pl.ds(at, 16), :], xh, m)
                dc[pl.ds(at, 16), :] = v.astype(BF)
                if hs is not None:
                    hs[pl.ds(aligned(row + HALO), 16), :] = v

        self.chunks(one)

    def back_four(self, ids, sc, dz4, c4, nrm4, sts, normp, msk, dz6, c3, nrm3, cs, nrms, w, off, rows):
        R = self.R
        layout, arrays = w
        nst, nw = len(sts), len(arrays)
        out_width = c3.shape[1]

        def body(ids, sc, dz4, c4, nrm4, normp, msk, dz6, c3, nrm3, cs, nrms, *rest):
            st_refs, refs = rest[:nst], rest[nst : nst + nw]
            dc, dz3, st, sums, ws, sem = rest[nst + nw :]
            self.load_start(layout, ids, refs, off, rows, ws, sem)
            self.group_sums(st_refs, 0, sc, self.area(1), sums)
            st[...] = jnp.zeros(st.shape, F32)
            self.own_dc(dz4, c4, nrm4, sums, normp, "4", msk, dc)
            self.load_wait(ws, sem)
            for q in range(out_width // MID):
                lane = slice(q * MID, (q + 1) * MID)
                dz3[:, lane] = dot_nt(dc[...], ws[lane, :])

            def one(which, row):
                m = wide(msk[pl.ds(row, 16), :])
                for q in range(out_width // MID):
                    lane = slice(q * MID, (q + 1) * MID)
                    xh3 = self.xhat(c3, nrm3, which, row, lane)
                    xhs = self.xhat(cs, nrms, which, row, lane)
                    pre = self.affine(normp, "3", q, xh3) + self.affine(normp, "S", q, xhs)
                    d = (dz6[pl.ds(row, 16), lane] + dz3[pl.ds(row, 16), lane]) * slope(pre) * m
                    dz3[pl.ds(row, 16), lane] = d
                    self.add_rows(st, which, d, lane)
                    self.add_rows(st, 3 + which, d * xh3, lane)
                    self.add_rows(st, 8 + 3 + which, d * xhs, lane)

            self.chunks(one)
            st[8:11, :] = st[0:3, :]

        return call(
            body,
            [(ids, SM), (sc, SM), (dz4, VM), (c4, VM), (nrm4, VM), (normp, VM), (msk, VM)]
            + [(dz6, VM), (c3, VM), (nrm3, VM), (cs, VM), (nrms, VM)]
            + [(s, VM) for s in sts]
            + [(a, HB) for a in arrays],
            [((R, MID), BF, VM), ((R, out_width), F32, VM), ((16, out_width), F32, VM)],
            [pltpu.VMEM((8, MID), F32), pltpu.VMEM((out_width, MID), BF), pltpu.SemaphoreType.DMA],
            flops=2 * R * MID * out_width,
        )

    def back_three(self, ids, sc, dz3, c3, nrm3, cs, nrms, sts, normp, msk, c2, nrm2, w, off, rows):
        R = self.R
        layout, arrays = w
        nst, nw = len(sts), len(arrays)
        out_width = c3.shape[1]

        def body(ids, sc, dz3, c3, nrm3, cs, nrms, normp, msk, c2, nrm2, *rest):
            st_refs, refs = rest[:nst], rest[nst : nst + nw]
            dc3, dcs, dz2, st, sums3, sumss, ws, sem = rest[nst + nw :]
            self.load_start(layout, ids, refs, off, rows, ws, sem)
            self.group_sums(st_refs, 0, sc, self.area(1), sums3)
            self.group_sums(st_refs, 8, sc, self.area(1), sumss)
            st[...] = jnp.zeros(st.shape, F32)

            def one(which, row):
                m = wide(msk[pl.ds(row, 16), :])
                for q in range(out_width // MID):
                    lane = slice(q * MID, (q + 1) * MID)
                    d = dz3[pl.ds(row, 16), lane]
                    xh = self.xhat(c3, nrm3, which, row, lane)
                    dc3[pl.ds(row, 16), lane] = self.norm_back(
                        normp, "3", q, nrm3, sums3, which, lane, d, xh, m
                    ).astype(BF)
                    xh = self.xhat(cs, nrms, which, row, lane)
                    dcs[pl.ds(row, 16), lane] = self.norm_back(
                        normp, "S", q, nrms, sumss, which, lane, d, xh, m
                    ).astype(BF)

            self.chunks(one)
            self.load_wait(ws, sem)
            dz2[...] = dot_nn(dc3[...], ws[...])
            self.through(dz2, c2, nrm2, normp, "2", msk, st)

        return call(
            body,
            [(ids, SM), (sc, SM), (dz3, VM), (c3, VM), (nrm3, VM), (cs, VM), (nrms, VM), (normp, VM), (msk, VM)]
            + [(c2, VM), (nrm2, VM)]
            + [(s, VM) for s in sts]
            + [(a, HB) for a in arrays],
            [((R, out_width), BF, VM), ((R, out_width), BF, VM), ((R, MID), F32, VM), ((8, MID), F32, VM)],
            [
                pltpu.VMEM((8, out_width), F32),
                pltpu.VMEM((8, out_width), F32),
                pltpu.VMEM((out_width, MID), BF),
                pltpu.SemaphoreType.DMA,
            ],
            flops=2 * R * MID * out_width,
        )

    SHIFTS = ((0, 0), (0, 1), (1, 0), (1, 1))

    def back_two(self, ids, sc, dz2, c2, nrm2, sts, normp, msk, c1, nrm1, w, off, rows):
        R = self.R
        layout, arrays = w
        nst, nw = len(sts), len(arrays)

        def body(ids, sc, dz2, c2, nrm2, normp, msk, c1, nrm1, *rest):
            st_refs, refs = rest[:nst], rest[nst : nst + nw]
            dc, dz1, st, sums, ws, hs, patches, sem = rest[nst + nw :]
            self.load_start(layout, ids, refs, off, rows, ws, sem)
            self.group_sums(st_refs, 0, sc, self.area(1), sums)
            self.clear_halo(hs)
            st[...] = jnp.zeros(st.shape, F32)
            self.own_dc(dz2, c2, nrm2, sums, normp, "2", msk, dc, hs)
            for k, (fwd_r, fwd_c) in enumerate(self.SHIFTS):
                self.shifted(hs, patches, k * MID, fwd_r, fwd_c)
            self.load_wait(ws, sem)
            seen = set()
            for tap in range(9):
                phase, back_r, back_c = self.tap_two(tap)
                k = self.SHIFTS.index((back_r, back_c))
                part = dot_nt(patches[:, k * MID : (k + 1) * MID], ws[tap * MID : (tap + 1) * MID, :])
                if phase in seen:
                    dz1[phase * R : (phase + 1) * R, :] += part
                else:
                    dz1[phase * R : (phase + 1) * R, :] = part
                seen.add(phase)
            self.through(dz1, c1, nrm1, normp, "1", msk, st, 4)

        return call(
            body,
            [(ids, SM), (sc, SM), (dz2, VM), (c2, VM), (nrm2, VM), (normp, VM), (msk, VM), (c1, VM), (nrm1, VM)]
            + [(s, VM) for s in sts]
            + [(a, HB) for a in arrays],
            [((R, MID), BF, VM), ((4 * R, MID), F32, VM), ((8, MID), F32, VM)],
            [
                pltpu.VMEM((8, MID), F32),
                pltpu.VMEM((9 * MID, MID), BF),
                pltpu.VMEM((R + 2 * HALO, MID), F32),
                pltpu.VMEM((R, 4 * MID), BF),
                pltpu.SemaphoreType.DMA,
            ],
            flops=2 * 9 * R * MID * MID,
        )

    def back_one(self, sc, dz1, c1, nrm1, sts, normp, msk):
        R = self.R
        nst = len(sts)

        def body(sc, dz1, c1, nrm1, normp, msk, *rest):
            st_refs = rest[:nst]
            dc, sums = rest[nst:]
            self.group_sums(st_refs, 0, sc, self.area(2), sums)
            self.own_dc(dz1, c1, nrm1, sums, normp, "1", msk, dc, None, 4)

        return call(
            body,
            [(sc, SM), (dz1, VM), (c1, VM), (nrm1, VM), (normp, VM), (msk, VM)] + [(s, VM) for s in sts],
            [((4 * R, MID), BF, VM)],
            [pltpu.VMEM((8, MID), F32)],
        )[0]

    def input_grad(self, ids, dc1, dcs, w1, off1, rows1, ids_s, ws, offs, rowss, pictures):
        R = self.R
        g = self.g
        lay1, arr1 = w1
        lays, arrs = ws
        n1, ns = len(arr1), len(arrs)
        width = pictures[0].shape[3]
        out_width = dcs.shape[1]

        def body(ids, ids_s, dc1, dcs, *rest):
            r1, rs = rest[:n1], rest[n1 : n1 + ns]
            ga, gb, gc, k1, ka, kb, dx, sem = rest[n1 + ns :]
            g_refs = (ga, gb, gc)
            self.load_start(lay1, ids, r1, off1, rows1, k1, sem.at[0])
            self.load_start(lays, ids_s, rs, offs, rowss, ka, sem.at[1])
            self.load_start(lays, ids_s, rs, offs + rowss, rowss, kb, sem.at[2])
            self.load_wait(k1, sem.at[0])
            self.load_wait(ka, sem.at[1])
            self.load_wait(kb, sem.at[2])
            for phase in range(4):
                for q in range(width // MID):
                    lane = slice(q * MID, (q + 1) * MID)
                    part = dot_nt(dc1[phase * R : (phase + 1) * R, :], k1[lane, :])
                    if phase == 0:
                        part = part + dot_nn(dcs[...], (ka, kb)[q][...])
                    dx[phase * R : (phase + 1) * R, lane] = part
            for which, line, column, row in g.lines():
                for phase in range(4):
                    odd, second = divmod(phase, 2)
                    base = phase * R + row
                    g_refs[which][2 * line + odd, 2 * column + second] = dx[base : base + g.counts[which], :].astype(BF)

        return call(
            body,
            [(ids, SM), (ids_s, SM), (dc1, VM), (dcs, VM)] + [(a, HB) for a in arr1] + [(a, HB) for a in arrs],
            [(p.shape, BF, VM) for p in pictures],
            [
                pltpu.VMEM((width, MID), BF),
                pltpu.VMEM((out_width, MID), BF),
                pltpu.VMEM((out_width, MID), BF),
                pltpu.VMEM((4 * R, width), F32),
                pltpu.SemaphoreType.DMA((3,)),
            ],
            flops=2 * (4 * R * width * MID + R * width * out_width),
        )


    def gradient(self, ids, chains, kind, ins, parts, heights, held=None, extra=None):
        fresh = held is None
        arrays, start = ([], [0] * len(chains)) if fresh else held
        outs, spans = [], []
        for c, places_list in enumerate(chains):
            size = sum(split[c] for _, split in parts)
            for places in places_list:
                outs.append(((len(places), heights[c], MID), BF, HB))
                spans.append((start[c], size))
        count, pieces = len(ins), len(outs)

        def body(ids, *rest):
            refs, rest = rest[:count], rest[count + len(arrays) :]
            out_refs, rest = rest[:pieces], rest[pieces:]
            bufs, rest = rest[: len(parts)], rest[len(parts) :]
            sems, tail = rest[0], rest[1:]
            offs = list(start)
            for part, (buf, (rows, split)) in enumerate(zip(bufs, parts)):
                kind(part, refs, buf, tail)
                self.store_start(chains, ids, buf, rows, split, offs, out_refs, sems)
                offs = [o + t for o, t in zip(offs, split)]
            self.store_wait(out_refs, sems, spans)

        tall = [rows * self.blocks if self.blocks > 1 else rows for rows, _ in parts]
        scratch = [pltpu.VMEM((t, MID), BF) for t in tall]
        scratch.append(pltpu.SemaphoreType.DMA((pieces,)))
        scratch.extend(extra or [])
        made = call(
            body,
            [(ids, SM)] + [(a, VM) for a in ins] + [(a, HB) for a in arrays],
            outs,
            scratch,
            flops=2 * self.R * sum(tall) * MID,
            aliases={1 + count + i: i for i in range(len(arrays))},
        )
        ends = [at + sum(split[c] for _, split in parts) for c, at in enumerate(start)]
        return list(made), ends

    def grad_outer(self, ids, chains, pairs, parts, heights, held=None):
        ins = []
        for left, right in pairs:
            ins += [left, right]

        def kind(part, refs, buf, tail):
            left, right = refs[2 * part], refs[2 * part + 1]
            for q in range(left.shape[1] // MID):
                buf[q * MID : (q + 1) * MID, :] = dot_tn(left[:, q * MID : (q + 1) * MID], right[...]).astype(BF)

        return self.gradient(ids, chains, kind, ins, parts, heights, held)

    def grad_short(self, ids, chains, a2, dc3, dcs, xp, parts, heights, held=None):
        R = self.R

        def kind(part, refs, buf, tail):
            a2, dc3, dcs, xp = refs
            left = dc3 if part == 0 else dcs
            for q in range(left.shape[1] // MID):
                cols = left[:, q * MID : (q + 1) * MID]
                right = a2[...] if part == 0 else xp[0:R, (part - 1) * MID : part * MID]
                buf[q * MID : (q + 1) * MID, :] = dot_tn(cols, right).astype(BF)

        return self.gradient(ids, chains, kind, [a2, dc3, dcs, xp], parts, heights, held)

    def grad_taps(self, ids, chains, act, dc, parts, heights, stride, held=None):
        R = self.R

        def kind(part, refs, buf, tail):
            act, dc = refs
            hs, patches = tail
            self.clear_halo(hs)

            def spread(which, row):
                hs[pl.ds(aligned(row + HALO), 16), :] = dc[pl.ds(row, 16), :].astype(F32)

            self.chunks(spread)
            if stride == 1:
                shifts = [(1 - tap // 3, 1 - tap % 3) for tap in range(9)]
            else:
                shifts = list(self.SHIFTS)
            for k, (sr, sc_) in enumerate(shifts):
                self.shifted(hs, patches, k * MID, sr, sc_)
            for tap in range(9):
                if stride == 1:
                    left, k = act[...], tap
                else:
                    phase, back_r, back_c = self.tap_two(tap)
                    left, k = act[phase * R : (phase + 1) * R, :], self.SHIFTS.index((back_r, back_c))
                buf[tap * MID : (tap + 1) * MID, :] = dot_tn(left, patches[:, k * MID : (k + 1) * MID]).astype(BF)

        wide_cols = 9 if stride == 1 else 4
        extra = [pltpu.VMEM((R + 2 * HALO, MID), F32), pltpu.VMEM((R, wide_cols * MID), BF)]
        return self.gradient(ids, chains, kind, [act, dc], parts, heights, held, extra)

    def grad_first(self, ids, chains, xp, dc1, sums, parts, heights):
        def kind(part, refs, buf, tail):
            if part == 0:
                xp, dc1 = refs[0], refs[1]
                for q in range(xp.shape[1] // MID):
                    buf[q * MID : (q + 1) * MID, :] = dot_tn(xp[:, q * MID : (q + 1) * MID], dc1[...]).astype(BF)
            else:
                row = 0
                for first in (3, 0):
                    for name in ("1", "2", "3", "S", "4", "5", "6"):
                        ref = refs[2 + ("1", "2", "3", "4", "5", "6").index("3" if name == "S" else name)]
                        at = first + (8 if name == "S" else 0)
                        total = ref[at : at + 1, :] + ref[at + 1 : at + 2, :] + ref[at + 2 : at + 3, :]
                        for q in range(ref.shape[1] // MID):
                            piece = total[:, q * MID : (q + 1) * MID]
                            buf[row * 16 : row * 16 + 16, :] = jnp.broadcast_to(piece, (16, MID)).astype(BF)
                            row += 1

        return self.gradient(ids, chains, kind, [xp, dc1] + list(sums), parts, heights)


def adam_step(weight, moment_one, moment_two, gradient, step_rate, decay_rate):
    first_new = 0.5 * moment_one + 0.5 * gradient
    second_new = 0.5 * moment_two + 0.5 * gradient * gradient
    correct = 1.0 - 0.5**STEP
    update = first_new / correct / (jnp.sqrt(second_new / correct) + 1e-08) + decay_rate * weight
    return (weight - step_rate * update, first_new, second_new)


BOTH = ("dp", "bn")


def orders(total):
    count = total.bit_length() - 1
    if count == 5:
        return [4, 2, 3, 1, 0], [4, 1, 3, 2, 0], [2, 1, 4, 3, 0]
    return (list(range(count))[::-1],) * 3


def on_device(*args):
    slots_inside = (1, 2, 0, 3)
    images = [jnp.transpose(args[k], slots_inside) for k in (0, 2, 1)]
    lives = (args[3], args[5], args[4])
    ups = [jnp.transpose(args[k], slots_inside) for k in (6, 8, 7)]
    params, firsts, seconds = args[9:17], args[17:25], args[25:33]
    groups, members = lax.axis_size("dp"), lax.axis_size("bn")
    total = groups * members
    pos_dp, pos_bn = lax.axis_index("dp"), lax.axis_index("bn")
    me = pos_dp * members + pos_bn
    grid = Grid([p.shape[2] for p in images], [u.shape[1] for u in ups])

    low = [p.astype(BF) for p in params]
    short_t = low[3].T
    shards = {
        "1": low[0],
        "2": low[1],
        "3": low[2].T,
        "S": jnp.concatenate([short_t[:, :MID], short_t[:, MID:]], axis=0),
        "4": low[4],
        "5": low[5],
        "6": low[6].T,
    }
    unit = {"1": 1, "2": 1, "3": 1, "S": 2, "4": 1, "5": 1, "6": 1}
    rows = {k: v.shape[0] // unit[k] for k, v in shards.items()}
    direct = all(r % 16 == 0 for r in rows.values()) and params[7].shape[0] == MID
    blocks = total if direct else 1
    if not direct:
        rows = {k: r * total for k, r in rows.items()}
    dev = Device(grid, blocks, members)

    spot = jnp.stack([pos_dp, pos_bn]).astype(jnp.int32)
    far = jnp.zeros((1,), jnp.int32)
    near = me.reshape(1).astype(jnp.int32) if direct else far

    def offsets(names):
        where, at = {}, 0
        for k in names:
            where[k] = at
            at += rows[k] * unit[k]
        return where, at

    def packed(names, with_norm=False):
        parts = [shards[k] for k in names]
        if with_norm:
            parts.append(jnp.broadcast_to(low[7].reshape(1, MID), (16, MID)))
        return jnp.concatenate(parts, axis=0) if len(parts) > 1 else parts[0]

    def gather(names):
        buf = packed(names)
        full = lax.all_gather(buf, BOTH, axis=0, tiled=True).reshape(total, buf.shape[0], MID)
        if direct:
            return ([(0, list(range(total)))], [full]), offsets(names)[0]
        pieces, spot_row = [], 0
        for k in names:
            for _ in range(unit[k]):
                r = rows[k] // total
                pieces.append(full[:, spot_row : spot_row + r, :].reshape(rows[k], MID))
                spot_row += r
        return ([(0, [0])], [jnp.concatenate(pieces, axis=0)[None]]), offsets(names)[0]

    def swap(array, bit):
        return lax.ppermute(array, BOTH, [(i, i ^ (1 << bit)) for i in range(total)])

    def butterfly_gather(buf, order):
        held, places, steps = buf[None], [0], []
        for step, bit in enumerate(order):
            got = swap(held, bit)
            steps.append(got)
            there = [r ^ (1 << bit) for r in places]
            if step == len(order) - 1:
                return [places, there], [held, got], steps
            held, places = jnp.concatenate([held, got]), places + there

    def gather_near(names, chains, with_norm=False, after=None):
        if not direct:
            made, where = gather(names)
            return made, where, None
        buf = packed(names, with_norm)
        if after is not None:
            buf = lax.optimization_barrier((buf, after))[0]
        layout, arrays, at, steps = [], [], 0, None
        for height, order in chains:
            places, got, steps = butterfly_gather(buf[at : at + height], order)
            for p, a in zip(places, got):
                layout.append((at, p))
                arrays.append(a)
            at += height
        return (layout, arrays), offsets(names)[0], steps

    def exchange(stat):
        return [stat] + [
            lax.ppermute(stat, "bn", [(i, i ^ k) for i in range(members)]) for k in range(1, members)
        ]

    first, second, third = orders(total)
    r2 = rows["2"] // 48 * 16
    w1, at_1, steps = gather_near(["1"], [(rows["1"] + 16, first)], True)
    w2, at_2, _ = gather_near(
        ["2"],
        [(r2, first), (r2, second), (rows["2"] - 2 * r2, third)],
        after=steps[1] if direct else None,
    )
    wb, at_b = gather(["3", "S", "4", "5", "6"])

    xp, msk, sc = dev.prepare(spot, lives, images)
    if direct:
        c1, st1, normp = dev.conv_one(near, sc, xp, msk, w1, at_1["1"], rows["1"], rows["1"])
    else:
        c1, st1 = dev.conv_one(near, sc, xp, msk, w1, at_1["1"], rows["1"], None)
        normp = lax.all_gather(low[7], BOTH, axis=0, tiled=True).astype(F32).reshape(32, MID)
    a1, nrm1, c2, st2 = dev.conv_two(near, sc, c1, exchange(st1), normp, msk, w2, at_2["2"], rows["2"])
    cs, sts = dev.conv_short(far, sc, xp, msk, wb, at_b["S"], rows["S"])
    a2, nrm2, c3, st3 = dev.conv_expand(
        far, sc, c2, exchange(st2), normp, msk, wb, at_b["3"], rows["3"], "2", sts
    )
    h, hb, nrm3, nrms, c4, st4 = dev.conv_four(
        far, sc, c3, cs, exchange(st3), normp, msk, wb, at_b["4"], rows["4"]
    )
    a4, nrm4, c5, st5 = dev.conv_five(far, sc, c4, exchange(st4), normp, msk, wb, at_b["5"], rows["5"])
    a5, nrm5, c6, st6 = dev.conv_expand(far, sc, c5, exchange(st5), normp, msk, wb, at_b["6"], rows["6"], "5")
    oc, oa, ob, dz6, nrm6, su6 = dev.finish(sc, c6, h, exchange(st6), normp, msk, ups)

    def split_places(order):
        places = [0]
        for bit in reversed(order[1:]):
            places = places + [r ^ (1 << bit) for r in places]
        return [places, [r ^ (1 << order[0]) for r in places]]

    def butterfly_scatter(pieces, order):
        kept, sent = [pieces[0]], pieces[1]
        for step, bit in enumerate(order):
            kept.append(swap(sent, bit))
            if step < len(order) - 1:
                half = kept[0].shape[0] // 2
                sent = sum([k[half:].astype(F32) for k in kept[1:]], kept[0][half:].astype(F32)).astype(BF)
                kept = [k[:half] for k in kept]
        return sum([k[0].astype(F32) for k in kept[1:]], kept[0][0].astype(F32))

    def scatter(piece, heights):
        if not direct:
            parts, spot_row = [], 0
            for height in heights:
                parts.append(piece[0, spot_row : spot_row + height].reshape(total, height // total, MID))
                spot_row += height
            piece = jnp.concatenate(parts, axis=1)
        owned = lax.psum_scatter(piece.reshape(-1, MID), BOTH, scatter_dimension=0, tiled=True)
        return owned.astype(F32)

    def scatter_near(pieces, used, heights):
        if not direct:
            return [scatter(pieces[0], heights)]
        return [butterfly_scatter(pieces[2 * c : 2 * c + 2], order) for c, order in enumerate(used)]

    def cut(owned, heights):
        parts, spot_row = [], 0
        for height in heights:
            height = height if direct else height // total
            parts.append(owned[spot_row : spot_row + height])
            spot_row += height
        return parts

    whole = [[list(range(total)) if direct else [0]]]
    back_first, back_second = first[::-1], second[::-1]

    def halves(k):
        if not direct:
            return [rows[k]]
        one = rows[k] // 32 * 16
        return [rows[k] - one, one]

    pair = [back_first, back_second] if direct else [None]
    pair_places = [split_places(order) for order in pair] if direct else whole
    single = [back_first] if direct else [None]
    single_places = [split_places(back_first)] if direct else whole

    dc6, dz5, su5 = dev.back_six(
        far, sc, dz6, c6, nrm6, exchange(su6), normp, msk, c5, nrm5, wb, at_b["6"], rows["6"]
    )
    high = [rows["6"] + rows["5"]]
    g65 = dev.grad_outer(far, whole, [(dc6, a5)], [(rows["6"], [rows["6"]])], high)
    dc5, dz4, su4 = dev.back_five(
        far, sc, dz5, c5, nrm5, exchange(su5), normp, msk, c4, nrm4, wb, at_b["5"], rows["5"]
    )
    g65 = dev.grad_taps(far, whole, a4, dc5, [(rows["5"], [rows["5"]])], high, 1, g65)
    hts65 = [rows["6"], rows["5"]]
    o6, o5 = cut(scatter(g65[0][0], hts65), hts65)

    dc4, dz3, su3 = dev.back_four(
        far, sc, dz4, c4, nrm4, exchange(su4), normp, msk, dz6, c3, nrm3, cs, nrms, wb, at_b["4"], rows["4"]
    )
    part4, part3 = (rows["4"], halves("4")), (rows["3"], halves("3"))
    mid = [a + 3 * b for a, b in zip(part4[1], part3[1])]
    g43 = dev.grad_outer(near, pair_places, [(hb, dc4)], [part4], mid)
    dc3, dcs, dz2, su2 = dev.back_three(
        far, sc, dz3, c3, nrm3, cs, nrms, exchange(su3), normp, msk, c2, nrm2, wb, at_b["3"], rows["3"]
    )
    g43 = dev.grad_short(near, pair_places, a2, dc3, dcs, xp, [part3] * 3, mid, g43)
    got = scatter_near(g43[0], pair, [rows["4"]] + [rows["3"]] * 3)
    cuts = [cut(owned, [part4[1][c]] + [part3[1][c]] * 3) for c, owned in enumerate(got)]
    o4, o3, osa, osb = [jnp.concatenate(p, axis=0) if len(p) > 1 else p[0] for p in zip(*cuts)]

    dc2, dz1, su1 = dev.back_two(
        near, sc, dz2, c2, nrm2, exchange(su2), normp, msk, c1, nrm1, w2, at_2["2"], rows["2"]
    )
    g2 = dev.grad_taps(near, pair_places, a1, dc2, [(rows["2"], halves("2"))], halves("2"), 2)
    got = scatter_near(g2[0], pair, [rows["2"]])
    o2 = jnp.concatenate(got, axis=0) if len(got) > 1 else got[0]
    dc1 = dev.back_one(sc, dz1, c1, nrm1, exchange(su1), normp, msk)
    sums = (su1, su2, su3, su4, su5, su6)
    parts = [(rows["1"], [rows["1"]])] + ([(16, [16])] if direct else [])
    g1 = dev.grad_first(near, single_places, xp, dc1, sums, parts, [sum(p for p, _ in parts)])
    grads = dev.input_grad(near, dc1, dcs, w1, at_1["1"], rows["1"], far, wb, at_b["S"], rows["S"], images)
    gc_, ga_, gb_ = grads
    last = scatter_near(g1[0], single, [rows["1"]])[0]
    o1 = last[: rows["1"]] if direct else last
    if direct:
        onorm = last[rows["1"]]
    else:

        def three(stat, at):
            return jnp.sum(stat[at : at + 3], axis=0)

        vec = [three(su1, 3), three(su2, 3), three(su3, 3), three(su3, 11), three(su4, 3), three(su5, 3), three(su6, 3)]
        vec += [three(su1, 0), three(su2, 0), three(su3, 0), three(su3, 8), three(su4, 0), three(su5, 0), three(su6, 0)]
        onorm = lax.psum_scatter(jnp.concatenate(vec), BOTH, scatter_dimension=0, tiled=True)
    owned = (o1, o2, o3.T, jnp.concatenate([osa, osb], axis=1).T, o4, o5, o6.T, onorm)
    stepped = []
    for k in range(8):
        rate, decay = (RATE_CONV, DECAY_CONV) if k < 7 else (RATE_NORM, 0.0)
        stepped.extend(adam_step(params[k], firsts[k], seconds[k], owned[k], rate, decay))
    images_out = [jnp.transpose(a, (2, 0, 1, 3)) for a in (oc, oa, ob, gc_, ga_, gb_)]
    order_out = [images_out[k] for k in (0, 2, 1, 3, 5, 4)]
    return (*order_out, *stepped)


def solution(mesh):
    batch = P(BOTH, None, None, None)
    by_row, by_col, flat = P(BOTH, None), P(None, BOTH), P(BOTH)
    weights = (by_row, by_row, by_col, by_col, by_row, by_row, by_col, flat)
    triple = tuple(spec for spec in weights for _ in range(3))
    return jax.shard_map(
        on_device,
        mesh=mesh,
        in_specs=(batch,) * 3 + (P(),) * 3 + (batch,) * 3 + weights * 3,
        out_specs=(batch,) * 6 + triple,
        check_vma=False,
    )
```

time: 2560 us -> 505 us (0.20)
  local copies, waits for them, and re-layouts: 998 us -> 12.5 us
  waiting for transfers between devices: 991 us -> 178 us
  blocking collectives: 212 us -> 0 us
  Pallas kernels: 0 us -> 195 us
  matrix products: 158 us -> 0 us
  other arithmetic: 149 us -> 27.3 us
  starting transfers between devices: 1.3 us -> 71.7 us
    reduce_scatter x7 -> x1, waiting for transfers between devices: 964 us -> 0.01 us  [scatter(): lax.psum_scatter(piece.reshape(-1, MID), BOTH, scatter_dimension=0, tiled...]
    slice x120 -> x3, local copies, waits for them, and re-layouts: 468 us -> 0.04 us  [the longest x2 0.04 us: cut(): parts.append(owned[spot_row:spot_row + height])]
    pad x15 -> x0, local copies, waits for them, and re-layouts: 227 us -> none  [the longest x9 201 us: fold_taps(): lax.pad(shaped[:, :, :, tap_index, :], jnp.zeros((), jnp.float32), ((0, 0...]
    pallas_call x0 -> x22, Pallas kernels: none -> 195 us  [call(): pl.pallas_call(body, out_shape=[jax.ShapeDtypeStruct(shape, dtype) for sh...]
    unnamed x854 -> x161, local copies, waits for them, and re-layouts: 192 us -> 11.5 us
    psum x18 -> x0, blocking collectives: 168 us -> none  [the longest x13 110 us: normalize_many(): lax.psum(group, 'bn')]
    dot_general x63 -> x0, matrix products: 158 us -> none  [the longest x21 66.4 us: back_through(): lax.dot_general(incoming, matrix, (((1,), (1,)), ((), ())), preferred_ele...]
    ppermute x0 -> x81, waiting for transfers between devices: none -> 151 us  [the longest x45 108 us: swap(): return lax.ppermute(array, BOTH, [(i, i ^ 1 << bit) for i in range(total)])]
  transfers between devices with their start and end apart: 16 -> 83, of which waited for: 8 -> 47; matrix products, arithmetic and copies ran while one was open for 18% -> 5% of each run, Pallas kernels for 0% -> 25%
where the time goes in v1:
time: 505 us; the launch traced here: 500 us
  Pallas kernels  195 us (39%)
  waiting for transfers between devices  178 us (35%)
  starting transfers between devices  71.7 us (14%)
  other arithmetic  27.3 us (5%)
  between operations  15.7 us (3%)
  local copies, waits for them, and re-layouts  12.5 us (2%)
    pallas_call x22, Pallas kernels, call(): pl.pallas_call(body, out_shape=[jax.ShapeDtypeStruct(shape, dtype) for sh...  195 us
    ppermute x45, waiting for transfers between devices, swap(): return lax.ppermute(array, BOTH, [(i, i ^ 1 << bit) for i in range(total)])  108 us
    ppermute x45, starting transfers between devices, swap(): return lax.ppermute(array, BOTH, [(i, i ^ 1 << bit) for i in range(total)])  47.1 us
    ppermute x36, waiting for transfers between devices, exchange(): lax.ppermute(stat, 'bn', [(i, i ^ k) for i in range(members)])  42.8 us
    all_gather x1, waiting for transfers between devices, gather(): lax.all_gather(buf, BOTH, axis=0, tiled=True)  26.7 us
    ppermute x36, starting transfers between devices, exchange(): lax.ppermute(stat, 'bn', [(i, i ^ k) for i in range(members)])  24.5 us
    unnamed x161, local copies, waits for them, and re-layouts  11.5 us
    convert_element_type x20, other arithmetic, butterfly_scatter(): sum([k[half:].astype(F32) for k in kept[1:]], kept[0][half:].astype(F32))  11.1 us
  transfers between devices with their start and end apart: 83, of which 47 were waited for; matrix products, arithmetic and copies ran while one was open for 5% of the time, Pallas kernels for 25%

profile of v1, /device:TPU:0, one launch (start us, length us, event | category | flops | bytes accessed | tf_op | source)
XLA Modules:
  0.0 500.1 jit_solution(4333896670012676757)
XLA Ops:
  13.0 4.1 collective-permute-start
  17.8 2.0 collective-permute-done
  19.7 1.8 collective-permute-start.1
  22.1 2.3 collective-permute-done.1
  24.4 1.9 collective-permute-start.18
  26.4 2.0 collective-permute-start.13
  39.0 2.3 collective-permute-start.15
  42.2 5.3 %collective-permute-done.2 = bf16[4,48,512]{2,1,0:T(8,128)(2,1)S(1)} collective-permute-done((bf16[4,48,512]{2,1,0:T(8,128)(2,1)S(1)}, bf16[4,48,512]{2,1,0:T(8,128)(2,1)S(1)}, u32[]{:S(2)}, u32[]{:S(2)}) %collective-permute-start.2) | collective-permute-done | bytes 196640 | tf_op jit(solution)/shard_map/ppermute | solution.py:1062
  54.1 9.1 %collective-permute-done.10 = bf16[4,48,512]{2,1,0:T(8,128)(2,1)S(1)} collective-permute-done((bf16[4,48,512]{2,1,0:T(8,128)(2,1)S(1)}, bf16[4,48,512]{2,1,0:T(8,128)(2,1)S(1)}, u32[]{:S(2)}, u32[]{:S(2)}) %collective-permute-start.10) | collective-permute-done | bytes 196640 | tf_op jit(solution)/shard_map/ppermute | solution.py:1062
  65.7 5.4 %collective-permute-done.11 = bf16[8,48,512]{2,1,0:T(8,128)(2,1)S(1)} collective-permute-done((bf16[8,48,512]{2,1,0:T(8,128)(2,1)S(1)}, bf16[8,48,512]{2,1,0:T(8,128)(2,1)S(1)}, u32[]{:S(2)}, u32[]{:S(2)}) %collective-permute-start.11) | collective-permute-done | bytes 393248 | tf_op jit(solution)/shard_map/ppermute | solution.py:1062
  71.8 7.1 %collective-permute-done.21 = bf16[8,48,512]{2,1,0:T(8,128)(2,1)S(1)} collective-permute-done((bf16[8,48,512]{2,1,0:T(8,128)(2,1)S(1)}, bf16[8,48,512]{2,1,0:T(8,128)(2,1)S(1)}, u32[]{:S(2)}, u32[]{:S(2)}) %collective-permute-start.21) | collective-permute-done | bytes 393248 | tf_op jit(solution)/shard_map/ppermute | solution.py:1062
  79.7 7.2 %shard_map.544 = (bf16[1920,1024]{1,0:T(8,128)(2,1)}, f32[480,128]{1,0:T(8,128)}, f32[5,3]{1,0:T(8,128)}) custom-call(s32[2]{0:T(128)} %pad_add_fusion.spot, s32[128]{0:T(128)} %la.1, s32[64]{0:T(128)} %lb.1, s32[64]{0:T(128)} %lc.1, bf16[10,10,4,1024]{3,2,1,0:T(4,128)(2,1)} %bitcast.104, bf16[18,18,2,1024]{3,2,1,0:T(2,128)(2,1)} %bitcast.103, ...), custom_call_target="tpu_custom_call" | custom-call | tf_op jit(solution)/shard_map/pallas_call | solution.py:75
  86.9 8.8 %shard_map.545 = (f32[1920,512]{1,0:T(8,128)}, f32[8,512]{1,0:T(8,128)}, f32[32,512]{1,0:T(8,128)}) custom-call(s32[1]{0:T(128)} %bitcast.5.ids, f32[5,3]{1,0:T(8,128)} %get-tuple-element.100.sc, bf16[1920,1024]{1,0:T(8,128)(2,1)} %get-tuple-element.101.xp.rest_0_.rest_3_, f32[480,128]{1,0:T(8,128)} %get-tuple-element.102.msk, ...), custom_call_target="tpu_custom_call" | custom-call | flops 2013265920 | tf_op jit(solution)/shard_map/pallas_call | solution.py:75
  97.8 1.6 collective-permute-done.7.rest_3_
  102.3 10.4 %shard_map.546 = (bf16[1920,512]{1,0:T(8,128)(2,1)}, f32[8,512]{1,0:T(8,128)}, f32[480,512]{1,0:T(8,128)}, f32[8,512]{1,0:T(8,128)}) custom-call(s32[1]{0:T(128)} %bitcast.5.ids, f32[5,3]{1,0:T(8,128)} %get-tuple-element.100.sc, f32[1920,512]{1,0:T(8,128)} %get-tuple-element.103.c1, f32[32,512]{1,0:T(8,128)} %get-tuple-element.104.normp, ...), custom_call_target="tpu_custom_call" | custom-call | flops 2264924160 | tf_op jit(solution)/shard_map/pallas_call | solution.py:75
  114.8 26.7 %all-gather.2.cloned.1.call-done = bf16[14848,512]{1,0:T(8,128)(2,1)} async-done(((bf16[464,512]{1,0:T(8,128)(2,1)}), bf16[14848,512]{1,0:T(8,128)(2,1)}) %all-gather.2.cloned.1.call-update) | async-done | bytes 15204368 | tf_op jit(solution)/shard_map/all_gather | solution.py:1050
  141.5 10.8 %shard_map.547 = (f32[480,2048]{1,0:T(8,128)}, f32[8,2048]{1,0:T(8,128)}) custom-call(s32[1]{0:T(128)} %constant.22.clone.1.ids.ids_s, f32[5,3]{1,0:T(8,128)} %get-tuple-element.100.sc, bf16[1920,1024]{1,0:T(8,128)(2,1)} %get-tuple-element.101.xp.rest_0_.rest_3_, f32[480,128]{1,0:T(8,128)} %get-tuple-element.102.msk, bf16[32,464,512]{2,1,0:T(8,128)(2,1)} %bitcast.92), custom_call_target="tpu_custom_call" | custom-call | flops 2013265920 | tf_op jit(solution)/shard_map/pallas_call | solution.py:75
  153.0 8.5 %shard_map.548 = (bf16[480,512]{1,0:T(8,128)(2,1)}, f32[8,512]{1,0:T(8,128)}, f32[480,2048]{1,0:T(8,128)}, f32[16,2048]{1,0:T(8,128)}) custom-call(s32[1]{0:T(128)} %constant.22.clone.1.ids.ids_s, f32[5,3]{1,0:T(8,128)} %get-tuple-element.100.sc, f32[480,512]{1,0:T(8,128)} %get-tuple-element.107.c.c2, f32[32,512]{1,0:T(8,128)} %get-tuple-element.104.normp, ...), custom_call_target="tpu_custom_call" | custom-call | flops 1006632960 | tf_op jit(solution)/shard_map/pallas_call | solution.py:75
  163.4 3.8 collective-permute-done.28.rest_3_
  167.2 3.2 collective-permute-done.27.rest_2_
  171.1 10.4 %shard_map.549 = (f32[480,2048]{1,0:T(8,128)}, bf16[480,2048]{1,0:T(8,128)(2,1)}, f32[8,2048]{1,0:T(8,128)}, f32[8,2048]{1,0:T(8,128)}, f32[480,512]{1,0:T(8,128)}, /*index=5*/f32[8,512]{1,0:T(8,128)}) custom-call(s32[1]{0:T(128)} %constant.22.clone.1.ids.ids_s, f32[5,3]{1,0:T(8,128)} %get-tuple-element.100.sc, f32[480,2048]{1,0:T(8,128)} %get-tuple-element.110.c3, ...), custom_call_target="tpu_custom_call" | custom-call | flops 1006632960 | tf_op jit(solution)/shard_map/pallas_call | solution.py:75
  186.2 7.9 %shard_map.550 = (bf16[480,512]{1,0:T(8,128)(2,1)}, f32[8,512]{1,0:T(8,128)}, f32[480,512]{1,0:T(8,128)}, f32[8,512]{1,0:T(8,128)}) custom-call(s32[1]{0:T(128)} %constant.22.clone.1.ids.ids_s, f32[5,3]{1,0:T(8,128)} %get-tuple-element.100.sc, f32[480,512]{1,0:T(8,128)} %get-tuple-element.113.c4, f32[32,512]{1,0:T(8,128)} %get-tuple-element.104.normp, ...), custom_call_target="tpu_custom_call" | custom-call | flops 2264924160 | tf_op jit(solution)/shard_map/pallas_call | solution.py:75
  199.3 8.5 %shard_map.551 = (bf16[480,512]{1,0:T(8,128)(2,1)}, f32[8,512]{1,0:T(8,128)}, f32[480,2048]{1,0:T(8,128)}, f32[8,2048]{1,0:T(8,128)}) custom-call(s32[1]{0:T(128)} %constant.22.clone.1.ids.ids_s, f32[5,3]{1,0:T(8,128)} %get-tuple-element.100.sc, f32[480,512]{1,0:T(8,128)} %get-tuple-element.115.c.c5, f32[32,512]{1,0:T(8,128)} %get-tuple-element.104.normp, ...), custom_call_target="tpu_custom_call" | custom-call | flops 1006632960 | tf_op jit(solution)/shard_map/pallas_call | solution.py:75
  208.0 1.7 collective-permute-start.36
  209.8 2.5 collective-permute-done.37.rest_3_
  212.3 1.6 collective-permute-done.36.rest_2_
  214.6 10.9 %shard_map.552 = (bf16[5,5,4,2048]{3,2,1,0:T(4,128)(2,1)}, bf16[9,9,2,2048]{3,2,1,0:T(2,128)(2,1)}, bf16[7,7,2,2048]{3,2,1,0:T(2,128)(2,1)}, f32[480,2048]{1,0:T...) custom-call(f32[5,3]{1,0:T(8,128)} %get-tuple-element.100.sc, f32[480,2048]{1,0:T(8,128)} %get-tuple-element.117.c6, ...), custom_call_target="tpu_custom_call" | custom-call | tf_op jit(solution)/shard_map/pallas_call | solution.py:75
  227.4 2.7 collective-permute-done.40.rest_3_
  232.2 9.2 %shard_map.553 = (bf16[480,2048]{1,0:T(8,128)(2,1)}, f32[480,512]{1,0:T(8,128)}, f32[8,512]{1,0:T(8,128)}) custom-call(s32[1]{0:T(128)} %constant.22.clone.1.ids.ids_s, f32[5,3]{1,0:T(8,128)} %get-tuple-element.100.sc, f32[480,2048]{1,0:T(8,128)} %get-tuple-element.123.dz.dz6, f32[480,2048]{1,0:T(8,128)} %get-tuple-element.117.c6, ...), custom_call_target="tpu_custom_call" | custom-call | flops 1006632960 | tf_op jit(solution)/shard_map/pallas_call | solution.py:75
  243.2 4.3 shard_map.564.rest_2_
  248.2 9.1 %shard_map.554 = (bf16[480,512]{1,0:T(8,128)(2,1)}, f32[480,512]{1,0:T(8,128)}, f32[8,512]{1,0:T(8,128)}) custom-call(s32[1]{0:T(128)} %constant.22.clone.1.ids.ids_s, f32[5,3]{1,0:T(8,128)} %get-tuple-element.100.sc, f32[480,512]{1,0:T(8,128)} %get-tuple-element.127.dz5, f32[480,512]{1,0:T(8,128)} %get-tuple-element.115.c.c5, ...), custom_call_target="tpu_custom_call" | custom-call | flops 2264924160 | tf_op jit(solution)/shard_map/pallas_call | solution.py:75
  257.3 6.6 %shard_map.565 = bf16[32,208,512]{2,1,0:T(8,128)(2,1)} custom-call(s32[1]{0:T(128)} %constant.22.clone.1.ids.ids_s, bf16[480,512]{1,0:T(8,128)(2,1)} %get-tuple-element.166.rest_0_, bf16[480,512]{1,0:T(8,128)(2,1)} %get-tuple-element.167.rest_1_, bf16[32,208,512]{2,1,0:T(8,128)(2,1)} %shard_map.564.rest_2_), custom_call_target="tpu_custom_call", output_to_operand_aliasing={{}: (3, {})} | custom-call | flops 2264924160 | tf_op jit(solution)/shard_map/pallas_call | solution.py:75
  269.4 14.9 %shard_map.555 = (bf16[480,512]{1,0:T(8,128)(2,1)}, f32[480,2048]{1,0:T(8,128)}, f32[16,2048]{1,0:T(8,128)}) custom-call(s32[1]{0:T(128)} %constant.22.clone.1.ids.ids_s, f32[5,3]{1,0:T(8,128)} %get-tuple-element.100.sc, f32[480,512]{1,0:T(8,128)} %get-tuple-element.130.dz4, f32[480,512]{1,0:T(8,128)} %get-tuple-element.113.c4, ...), custom_call_target="tpu_custom_call" | custom-call | flops 1006632960 | tf_op jit(solution)/shard_map/pallas_call | solution.py:75
  286.3 5.0 %collective-permute-done.49.rest_3_ = f32[16,2048]{1,0:T(8,128)S(1)} collective-permute-done((f32[16,2048]{1,0:T(8,128)}, f32[16,2048]{1,0:T(8,128)S(1)}, u32[]{:S(2)}, u32[]{:S(2)}) %collective-permute-start.49) | collective-permute-done | bytes 131104 | tf_op jit(solution)/shard_map/ppermute | solution.py:1092
  291.3 5.8 %collective-permute-done.48.rest_2_ = f32[16,2048]{1,0:T(8,128)S(1)} collective-permute-done((f32[16,2048]{1,0:T(8,128)}, f32[16,2048]{1,0:T(8,128)S(1)}, u32[]{:S(2)}, u32[]{:S(2)}) %collective-permute-start.48) | collective-permute-done | bytes 131104 | tf_op jit(solution)/shard_map/ppermute | solution.py:1092
  297.8 11.9 %shard_map.556 = (bf16[480,2048]{1,0:T(8,128)(2,1)}, bf16[480,2048]{1,0:T(8,128)(2,1)}, f32[480,512]{1,0:T(8,128)}, f32[8,512]{1,0:T(8,128)}) custom-call(s32[1]{0:T(128)} %constant.22.clone.1.ids.ids_s, f32[5,3]{1,0:T(8,128)} %get-tuple-element.100.sc, f32[480,2048]{1,0:T(8,128)} %get-tuple-element.134.dz3, f32[480,2048]{1,0:T(8,128)} %get-tuple-element.110.c3, ...), custom_call_target="tpu_custom_call" | custom-call | flops 1006632960 | tf_op jit(solution)/shard_map/pallas_call | solution.py:75
  309.8 1.9 collective-permute-start.52
  313.3 2.3 collective-permute-done.51.rest_2_
  316.2 12.9 %shard_map.557 = (bf16[480,512]{1,0:T(8,128)(2,1)}, f32[1920,512]{1,0:T(8,128)}, f32[8,512]{1,0:T(8,128)}) custom-call(s32[1]{0:T(128)} %bitcast.5.ids, f32[5,3]{1,0:T(8,128)} %get-tuple-element.100.sc, f32[480,512]{1,0:T(8,128)} %get-tuple-element.137.dz2, f32[480,512]{1,0:T(8,128)} %get-tuple-element.107.c.c2, f32[8,512]{1,0:T(8,128)} %get-tuple-element.135.nrm2, ...), custom_call_target="tpu_custom_call" | custom-call | flops 2264924160 | tf_op jit(solution)/shard_map/pallas_call | solution.py:75
  332.6 1.6 collective-permute-done.54.rest_2_
  334.8 5.9 %shard_map.558.dc1.rest_1_ = bf16[1920,512]{1,0:T(8,128)(2,1)} custom-call(f32[5,3]{1,0:T(8,128)} %get-tuple-element.100.sc, f32[1920,512]{1,0:T(8,128)} %get-tuple-element.140.dz1, f32[1920,512]{1,0:T(8,128)} %get-tuple-element.103.c1, f32[8,512]{1,0:T(8,128)} %get-tuple-element.138.nrm1, f32[32,512]{1,0:T(8,128)} %get-tuple-element.104.normp, ...), custom_call_target="tpu_custom_call" | custom-call | tf_op jit(solution)/shard_map/pallas_call | solution.py:75
  340.8 6.2 %shard_map.560 = (bf16[16,48,512]{2,1,0:T(8,128)(2,1)}, bf16[16,48,512]{2,1,0:T(8,128)(2,1)}) custom-call(s32[1]{0:T(128)} %bitcast.5.ids, bf16[1920,1024]{1,0:T(8,128)(2,1)} %get-tuple-element.101.xp.rest_0_.rest_3_, bf16[1920,512]{1,0:T(8,128)(2,1)} %shard_map.558.dc1.rest_1_, f32[8,512]{1,0:T(8,128)} %get-tuple-element.141.rest_0_.rest_2_, ...), custom_call_target="tpu_custom_call" | custom-call | flops 754974720 | tf_op jit(solution)/shard_map/pallas_call | solution.py:75
  347.1 4.5 shard_map.562
  353.9 7.0 %shard_map.561 = (bf16[16,80,512]{2,1,0:T(8,128)(2,1)}, bf16[16,80,512]{2,1,0:T(8,128)(2,1)}, bf16[16,64,512]{2,1,0:T(8,128)(2,1)}, bf16[16,64,512]{2,1,0:T(8,128)(2,1)}) custom-call(s32[1]{0:T(128)} %bitcast.5.ids, bf16[1920,512]{1,0:T(8,128)(2,1)} %get-tuple-element.148.rest_0_, bf16[480,512]{1,0:T(8,128)(2,1)} %get-tuple-element.149.rest_1_), custom_call_target="tpu_custom_call" | custom-call | flops 2264924160 | tf_op jit(solution)/shard_map/pallas_call | solution.py:75
  361.0 8.5 %shard_map.563 = (bf16[16,128,512]{2,1,0:T(8,128)(2,1)}, bf16[16,128,512]{2,1,0:T(8,128)(2,1)}, bf16[16,128,512]{2,1,0:T(8,128)(2,1)}, bf16[16,128,512]{2,1,0:T(8,128)(2,1)}) custom-call(s32[1]{0:T(128)} %bitcast.5.ids, bf16[480,512]{1,0:T(8,128)(2,1)} %get-tuple-element.154.rest_0_, ...), custom_call_target="tpu_custom_call", output_to_operand_aliasing={{0}: (5, {}), {1}: (6, {}), {2}: (7, {}), {3}: (8, {})} | custom-call | flops 3019898880 | tf_op jit(solution)/shard_map/pallas_call | solution.py:75
  370.8 1.8 add_convert_fusion.11
  373.8 10.8 %shard_map.559 = (bf16[10,10,4,1024]{3,2,1,0:T(4,128)(2,1)}, bf16[18,18,2,1024]{3,2,1,0:T(2,128)(2,1)}, bf16[14,14,2,1024]{3,2,1,0:T(2,128)(2,1)}) custom-call(s32[1]{0:T(128)} %bitcast.5.ids, s32[1]{0:T(128)} %constant.22.clone.1.ids.ids_s, bf16[1920,512]{1,0:T(8,128)(2,1)} %shard_map.558.dc1.rest_1_, bf16[480,2048]{1,0:T(8,128)(2,1)} %get-tuple-element.142.dcs.rest_2_, ...), custom_call_target="tpu_custom_call" | custom-call | flops 4026531840 | tf_op jit(solution)/shard_map/pallas_call | solution.py:75
  385.8 3.5 collective-permute-start.59
  390.8 1.9 collective-permute-done.59
  393.6 3.8 collective-permute-start.60
  397.7 2.2 collective-permute-done.60
  402.1 3.2 collective-permute-done.67
  406.5 10.1 %collective-permute-done.62 = bf16[8,80,512]{2,1,0:T(8,128)(2,1)S(1)} collective-permute-done((bf16[8,80,512]{2,1,0:T(8,128)(2,1)S(1)}, bf16[8,80,512]{2,1,0:T(8,128)(2,1)S(1)}, u32[]{:S(2)}, u32[]{:S(2)}) %collective-permute-start.62) | collective-permute-done | bytes 655392 | tf_op jit(solution)/shard_map/ppermute | solution.py:1062
  418.6 2.3 collective-permute-start.69
  420.9 4.0 collective-permute-done.63
  425.1 18.5 %collective-permute-done.69 = bf16[2,64,512]{2,1,0:T(8,128)(2,1)S(1)} collective-permute-done((bf16[2,64,512]{2,1,0:T(8,128)(2,1)S(1)}, bf16[2,64,512]{2,1,0:T(8,128)(2,1)S(1)}, u32[]{:S(2)}, u32[]{:S(2)}) %collective-permute-start.69) | collective-permute-done | bytes 131104 | tf_op jit(solution)/shard_map/ppermute | solution.py:1062
  444.8 2.9 collective-permute-start.65
  447.9 1.7 collective-permute-start.73
  451.3 11.6 %collective-permute-done.73 = bf16[4,128,512]{2,1,0:T(8,128)(2,1)S(1)} collective-permute-done((bf16[4,128,512]{2,1,0:T(8,128)(2,1)S(1)}, bf16[4,128,512]{2,1,0:T(8,128)(2,1)S(1)}, u32[]{:S(2)}, u32[]{:S(2)}) %collective-permute-start.73) | collective-permute-done | bytes 524320 | tf_op jit(solution)/shard_map/ppermute | solution.py:1062
  463.0 2.2 collective-permute-start.74
  465.2 7.8 %collective-permute-done.78 = bf16[4,128,512]{2,1,0:T(8,128)(2,1)S(1)} collective-permute-done((bf16[4,128,512]{2,1,0:T(8,128)(2,1)S(1)}, bf16[4,128,512]{2,1,0:T(8,128)(2,1)S(1)}, u32[]{:S(2)}, u32[]{:S(2)}) %collective-permute-start.78) | collective-permute-done | bytes 524320 | tf_op jit(solution)/shard_map/ppermute | solution.py:1062
  475.2 5.3 %collective-permute-done.79 = bf16[2,128,512]{2,1,0:T(8,128)(2,1)S(1)} collective-permute-done((bf16[2,128,512]{2,1,0:T(8,128)(2,1)S(1)}, bf16[2,128,512]{2,1,0:T(8,128)(2,1)S(1)}, u32[]{:S(2)}, u32[]{:S(2)}) %collective-permute-start.79) | collective-permute-done | bytes 262176 | tf_op jit(solution)/shard_map/ppermute | solution.py:1062
  480.7 3.1 collective-permute-done.75
  483.9 3.4 collective-permute-done.80
  (353 shorter events, 96.4 us)
Async XLA Ops:
  7.2 134.3 %all-gather.2.cloned.1.call-start = ((), (), s32[]{:S(2)}) async-start(), calls=%async_computation.1 | async-start | bytes 15679488 | tf_op jit(solution)/shard_map/all_gather | solution.py:1050
  12.9 477.3 %reduce-scatter.2.cloned.1.call-start = ((), (), s32[]{:S(2)}) async-start(), calls=%async_computation.2 | async-start | bytes 7028736 | tf_op jit(solution)/shard_map/reduce_scatter | solution.py:1146
  13.0 6.7 %collective-permute-start = (bf16[1,48,512]{2,1,0:T(8,128)(2,1)S(1)}, bf16[1,48,512]{2,1,0:T(8,128)(2,1)S(1)}, u32[]{:S(2)}, u32[]{:S(2)}) collective-permute-start(bf16[1,48,512]{2,1,0:T(8,128)(2,1)S(1)} %maximum_bitcast_fusion.2), channel_id=1, source_target_pairs={{0,16},{1,17},{2,18},{3,19},{4,20},{5,21},{6,22},{7,23},{8,24},{9,... | collective-permute-start | bytes 147464 | tf_op jit(solution)/shard_map/ppermute | solution.py:1062
  19.7 4.7 collective-permute-start.1
  24.4 6.7 %collective-permute-start.18 = (bf16[1,48,512]{2,1,0:T(8,128)(2,1)S(1)}, bf16[1,48,512]{2,1,0:T(8,128)(2,1)S(1)}, u32[]{:S(2)}, u32[]{:S(2)}) collective-permute-start(bf16[1,48,512]{2,1,0:T(8,128)(2,1)S(1)} %get-tuple-element.202), channel_id=1, source_target_pairs={{0,4},{1,5},{2,6},{3,7},{4,0},{5,1},{6,2},{7,3},{8,12},{9,13},{10,... | collective-permute-start | bytes 147464 | tf_op jit(solution)/shard_map/ppermute | solution.py:1062
  26.4 7.9 %collective-permute-start.13 = (bf16[1,48,512]{2,1,0:T(8,128)(2,1)S(1)}, bf16[1,48,512]{2,1,0:T(8,128)(2,1)S(1)}, u32[]{:S(2)}, u32[]{:S(2)}) collective-permute-start(bf16[1,48,512]{2,1,0:T(8,128)(2,1)S(1)} %get-tuple-element.203), channel_id=1, source_target_pairs={{0,16},{1,17},{2,18},{3,19},{4,20},{5,21},{6,22},{7,23},{8,24},{9,... | collective-permute-start | bytes 147464 | tf_op jit(solution)/shard_map/ppermute | solution.py:1062
  28.4 8.9 %collective-permute-start.8 = (bf16[1,48,512]{2,1,0:T(8,128)(2,1)S(1)}, bf16[1,48,512]{2,1,0:T(8,128)(2,1)S(1)}, u32[]{:S(2)}, u32[]{:S(2)}) collective-permute-start(bf16[1,48,512]{2,1,0:T(8,128)(2,1)S(1)} %get-tuple-element.204), channel_id=1, source_target_pairs={{0,16},{1,17},{2,18},{3,19},{4,20},{5,21},{6,22},{7,23},{8,24},{9,... | collective-permute-start | bytes 147464 | tf_op jit(solution)/shard_map/ppermute | solution.py:1062
  29.3 18.2 %collective-permute-start.2 = (bf16[4,48,512]{2,1,0:T(8,128)(2,1)S(1)}, bf16[4,48,512]{2,1,0:T(8,128)(2,1)S(1)}, u32[]{:S(2)}, u32[]{:S(2)}) collective-permute-start(bf16[4,48,512]{2,1,0:T(8,128)(2,1)S(1)} %pad_maximum_fusion.5), channel_id=1, source_target_pairs={{0,8},{1,9},{2,10},{3,11},{4,12},{5,13},{6,14},{7,15},{8,0},{9,1},... | collective-permute-start | bytes 589832 | tf_op jit(solution)/shard_map/ppermute | solution.py:1062
  31.2 6.3 %collective-permute-start.19 = (bf16[2,48,512]{2,1,0:T(8,128)(2,1)S(1)}, bf16[2,48,512]{2,1,0:T(8,128)(2,1)S(1)}, u32[]{:S(2)}, u32[]{:S(2)}) collective-permute-start(bf16[2,48,512]{2,1,0:T(8,128)(2,1)S(1)} %pad_maximum_fusion.13), channel_id=1, source_target_pairs={{0,2},{1,3},{2,0},{3,1},{4,6},{5,7},{6,4},{7,5},{8,10},{9,11},{10,... | collective-permute-start | bytes 294920 | tf_op jit(solution)/shard_map/ppermute | solution.py:1062
  34.3 4.7 collective-permute-start.14
  37.4 4.7 collective-permute-start.9
  37.5 12.3 %collective-permute-start.20 = (bf16[4,48,512]{2,1,0:T(8,128)(2,1)S(1)}, bf16[4,48,512]{2,1,0:T(8,128)(2,1)S(1)}, u32[]{:S(2)}, u32[]{:S(2)}) collective-permute-start(bf16[4,48,512]{2,1,0:T(8,128)(2,1)S(1)} %pad_maximum_fusion.8), channel_id=1, source_target_pairs={{0,16},{1,17},{2,18},{3,19},{4,20},{5,21},{6,22},{7,23},{8,24},{9,... | collective-permute-start | bytes 589832 | tf_op jit(solution)/shard_map/ppermute | solution.py:1062
  39.0 13.8 %collective-permute-start.15 = (bf16[4,48,512]{2,1,0:T(8,128)(2,1)S(1)}, bf16[4,48,512]{2,1,0:T(8,128)(2,1)S(1)}, u32[]{:S(2)}, u32[]{:S(2)}) collective-permute-start(bf16[4,48,512]{2,1,0:T(8,128)(2,1)S(1)} %pad_maximum_fusion.7), channel_id=1, source_target_pairs={{0,8},{1,9},{2,10},{3,11},{4,12},{5,13},{6,14},{7,15},{8,0},{9,1},... | collective-permute-start | bytes 589832 | tf_op jit(solution)/shard_map/ppermute | solution.py:1062
  42.1 21.2 %collective-permute-start.10 = (bf16[4,48,512]{2,1,0:T(8,128)(2,1)S(1)}, bf16[4,48,512]{2,1,0:T(8,128)(2,1)S(1)}, u32[]{:S(2)}, u32[]{:S(2)}) collective-permute-start(bf16[4,48,512]{2,1,0:T(8,128)(2,1)S(1)} %pad_maximum_fusion.6), channel_id=1, source_target_pairs={{0,8},{1,9},{2,10},{3,11},{4,12},{5,13},{6,14},{7,15},{8,0},{9,1},... | collective-permute-start | bytes 589832 | tf_op jit(solution)/shard_map/ppermute | solution.py:1062
  47.6 17.3 %collective-permute-start.3 = (bf16[8,48,512]{2,1,0:T(8,128)(2,1)S(1)}, bf16[8,48,512]{2,1,0:T(8,128)(2,1)S(1)}, u32[]{:S(2)}, u32[]{:S(2)}) collective-permute-start(bf16[8,48,512]{2,1,0:T(8,128)(2,1)S(1)} %pad_maximum_fusion), channel_id=1, source_target_pairs={{0,2},{1,3},{2,0},{3,1},{4,6},{5,7},{6,4},{7,5},{8,10},{9,11},{10,... | collective-permute-start | bytes 1179656 | tf_op jit(solution)/shard_map/ppermute | solution.py:1062
  49.9 29.1 %collective-permute-start.21 = (bf16[8,48,512]{2,1,0:T(8,128)(2,1)S(1)}, bf16[8,48,512]{2,1,0:T(8,128)(2,1)S(1)}, u32[]{:S(2)}, u32[]{:S(2)}) collective-permute-start(bf16[8,48,512]{2,1,0:T(8,128)(2,1)S(1)} %pad_maximum_fusion.3), channel_id=1, source_target_pairs={{0,8},{1,9},{2,10},{3,11},{4,12},{5,13},{6,14},{7,15},{8,0},{9,1},... | collective-permute-start | bytes 1179656 | tf_op jit(solution)/shard_map/ppermute | solution.py:1062
  52.8 18.6 %collective-permute-start.16 = (bf16[8,48,512]{2,1,0:T(8,128)(2,1)S(1)}, bf16[8,48,512]{2,1,0:T(8,128)(2,1)S(1)}, u32[]{:S(2)}, u32[]{:S(2)}) collective-permute-start(bf16[8,48,512]{2,1,0:T(8,128)(2,1)S(1)} %pad_maximum_fusion.2), channel_id=1, source_target_pairs={{0,4},{1,5},{2,6},{3,7},{4,0},{5,1},{6,2},{7,3},{8,12},{9,13},{10,... | collective-permute-start | bytes 1179656 | tf_op jit(solution)/shard_map/ppermute | solution.py:1062
  63.3 7.8 %collective-permute-start.11 = (bf16[8,48,512]{2,1,0:T(8,128)(2,1)S(1)}, bf16[8,48,512]{2,1,0:T(8,128)(2,1)S(1)}, u32[]{:S(2)}, u32[]{:S(2)}) collective-permute-start(bf16[8,48,512]{2,1,0:T(8,128)(2,1)S(1)} %pad_maximum_fusion.1), channel_id=1, source_target_pairs={{0,2},{1,3},{2,0},{3,1},{4,6},{5,7},{6,4},{7,5},{8,10},{9,11},{10,... | collective-permute-start | bytes 1179656 | tf_op jit(solution)/shard_map/ppermute | solution.py:1062
  65.7 21.2 %collective-permute-start.4 = (bf16[16,48,512]{2,1,0:T(8,128)(2,1)}, bf16[16,48,512]{2,1,0:T(8,128)(2,1)}, u32[]{:S(2)}, u32[]{:S(2)}) collective-permute-start(bf16[16,48,512]{2,1,0:T(8,128)(2,1)} %constant_dynamic-update-slice_fusion.rest_0_), channel_id=1, source_target_pairs={{0,1},{1,0},{2,3},{3,2},{4,5},{5,4},{6,7},{7,6},{8,9},{9,8},{10,11... | collective-permute-start | bytes 2359304 | tf_op jit(solution)/shard_map/ppermute | solution.py:1062
  71.2 30.3 %collective-permute-start.12 = (bf16[16,48,512]{2,1,0:T(8,128)(2,1)S(1)}, bf16[16,48,512]{2,1,0:T(8,128)(2,1)S(1)}, u32[]{:S(2)}, u32[]{:S(2)}) collective-permute-start(bf16[16,48,512]{2,1,0:T(8,128)(2,1)S(1)} %constant_dynamic-update-slice_fusion.5.rest_4_), channel_id=1, source_target_pairs={{0,1},{1,0},{2,3},{3,2},{4,5},{5,4},{6,7},{7,6},{8,9},{9,8},{10,11... | collective-permute-start | bytes 2359304 | tf_op jit(solution)/shard_map/ppermute | solution.py:1062
  71.4 30.1 %collective-permute-start.17 = (bf16[16,48,512]{2,1,0:T(8,128)(2,1)S(1)}, bf16[16,48,512]{2,1,0:T(8,128)(2,1)}, u32[]{:S(2)}, u32[]{:S(2)}) collective-permute-start(bf16[16,48,512]{2,1,0:T(8,128)(2,1)S(1)} %constant_dynamic-update-slice_fusion.10.rest_6_), channel_id=1, source_target_pairs={{0,1},{1,0},{2,3},{3,2},{4,5},{5,4},{6,7},{7,6},{8,9},{9,8},{10,11... | collective-permute-start | bytes 2359304 | tf_op jit(solution)/shard_map/ppermute | solution.py:1062
  78.9 22.5 %collective-permute-start.22 = (bf16[16,48,512]{2,1,0:T(8,128)(2,1)S(1)}, bf16[16,48,512]{2,1,0:T(8,128)(2,1)}, u32[]{:S(2)}, u32[]{:S(2)}) collective-permute-start(bf16[16,48,512]{2,1,0:T(8,128)(2,1)S(1)} %constant_dynamic-update-slice_fusion.15.rest_8_), channel_id=1, source_target_pairs={{0,1},{1,0},{2,3},{3,2},{4,5},{5,4},{6,7},{7,6},{8,9},{9,8},{10,11... | collective-permute-start | bytes 2359304 | tf_op jit(solution)/shard_map/ppermute | solution.py:1062
  112.8 39.5 %collective-permute-start.25 = (f32[8,512]{1,0:T(8,128)}, f32[8,512]{1,0:T(8,128)S(1)}, u32[]{:S(2)}, u32[]{:S(2)}) collective-permute-start(f32[8,512]{1,0:T(8,128)} %get-tuple-element.108.rest_0_), channel_id=1, source_target_pairs={{0,3},{1,2},{2,1},{3,0},{4,7},{5,6},{6,5},{7,4},{8,11},{9,10},{10,... | collective-permute-start | bytes 49160 | tf_op jit(solution)/shard_map/ppermute | solution.py:1092
  114.0 38.4 %collective-permute-start.24 = (f32[8,512]{1,0:T(8,128)}, f32[8,512]{1,0:T(8,128)S(1)}, u32[]{:S(2)}, u32[]{:S(2)}) collective-permute-start(f32[8,512]{1,0:T(8,128)} %get-tuple-element.108.rest_0_), channel_id=1, source_target_pairs={{0,2},{1,3},{2,0},{3,1},{4,6},{5,7},{6,4},{7,5},{8,10},{9,11},{10,... | collective-permute-start | bytes 49160 | tf_op jit(solution)/shard_map/ppermute | solution.py:1092
  114.8 37.5 %collective-permute-start.23 = (f32[8,512]{1,0:T(8,128)}, f32[8,512]{1,0:T(8,128)S(1)}, u32[]{:S(2)}, u32[]{:S(2)}) collective-permute-start(f32[8,512]{1,0:T(8,128)} %get-tuple-element.108.rest_0_), channel_id=1, source_target_pairs={{0,1},{1,0},{2,3},{3,2},{4,5},{5,4},{6,7},{7,6},{8,9},{9,8},{10,11... | collective-permute-start | bytes 49160 | tf_op jit(solution)/shard_map/ppermute | solution.py:1092
  161.5 5.7 %collective-permute-start.28 = (f32[16,2048]{1,0:T(8,128)}, f32[16,2048]{1,0:T(8,128)S(1)}, u32[]{:S(2)}, u32[]{:S(2)}) collective-permute-start(f32[16,2048]{1,0:T(8,128)} %get-tuple-element.112.rest_0_), channel_id=1, source_target_pairs={{0,3},{1,2},{2,1},{3,0},{4,7},{5,6},{6,5},{7,4},{8,11},{9,10},{10,... | collective-permute-start | bytes 393224 | tf_op jit(solution)/shard_map/ppermute | solution.py:1092
  162.0 8.4 %collective-permute-start.27 = (f32[16,2048]{1,0:T(8,128)}, f32[16,2048]{1,0:T(8,128)S(1)}, u32[]{:S(2)}, u32[]{:S(2)}) collective-permute-start(f32[16,2048]{1,0:T(8,128)} %get-tuple-element.112.rest_0_), channel_id=1, source_target_pairs={{0,2},{1,3},{2,0},{3,1},{4,6},{5,7},{6,4},{7,5},{8,10},{9,11},{10,... | collective-permute-start | bytes 393224 | tf_op jit(solution)/shard_map/ppermute | solution.py:1092
  163.4 6.9 %collective-permute-start.26 = (f32[16,2048]{1,0:T(8,128)}, f32[16,2048]{1,0:T(8,128)S(1)}, u32[]{:S(2)}, u32[]{:S(2)}) collective-permute-start(f32[16,2048]{1,0:T(8,128)} %get-tuple-element.112.rest_0_), channel_id=1, source_target_pairs={{0,1},{1,0},{2,3},{3,2},{4,5},{5,4},{6,7},{7,6},{8,9},{9,8},{10,11... | collective-permute-start | bytes 393224 | tf_op jit(solution)/shard_map/ppermute | solution.py:1092
  207.9 4.4 collective-permute-start.37
  208.0 6.0 %collective-permute-start.36 = (f32[8,2048]{1,0:T(8,128)}, f32[8,2048]{1,0:T(8,128)S(1)}, u32[]{:S(2)}, u32[]{:S(2)}) collective-permute-start(f32[8,2048]{1,0:T(8,128)} %get-tuple-element.119.rest_0_), channel_id=1, source_target_pairs={{0,2},{1,3},{2,0},{3,1},{4,6},{5,7},{6,4},{7,5},{8,10},{9,11},{10,... | collective-permute-start | bytes 196616 | tf_op jit(solution)/shard_map/ppermute | solution.py:1092
  225.5 4.6 collective-permute-start.40
  225.5 6.0 %collective-permute-start.39 = (f32[8,2048]{1,0:T(8,128)}, f32[8,2048]{1,0:T(8,128)S(1)}, u32[]{:S(2)}, u32[]{:S(2)}) collective-permute-start(f32[8,2048]{1,0:T(8,128)} %get-tuple-element.126.rest_0_.rest_7_), channel_id=1, source_target_pairs={{0,2},{1,3},{2,0},{3,1},{4,6},{5,7},{6,4},{7,5},{8,10},{9,11},{10,... | collective-permute-start | bytes 196616 | tf_op jit(solution)/shard_map/ppermute | solution.py:1092
  227.0 4.5 collective-permute-start.38
  241.3 6.3 %collective-permute-start.43 = (f32[8,512]{1,0:T(8,128)}, f32[8,512]{1,0:T(8,128)S(1)}, u32[]{:S(2)}, u32[]{:S(2)}) collective-permute-start(f32[8,512]{1,0:T(8,128)} %get-tuple-element.129.rest_0_.rest_6_), channel_id=1, source_target_pairs={{0,3},{1,2},{2,1},{3,0},{4,7},{5,6},{6,5},{7,4},{8,11},{9,10},{10,... | collective-permute-start | bytes 49160 | tf_op jit(solution)/shard_map/ppermute | solution.py:1092
  241.5 6.1 %collective-permute-start.42 = (f32[8,512]{1,0:T(8,128)}, f32[8,512]{1,0:T(8,128)S(1)}, u32[]{:S(2)}, u32[]{:S(2)}) collective-permute-start(f32[8,512]{1,0:T(8,128)} %get-tuple-element.129.rest_0_.rest_6_), channel_id=1, source_target_pairs={{0,2},{1,3},{2,0},{3,1},{4,6},{5,7},{6,4},{7,5},{8,10},{9,11},{10,... | collective-permute-start | bytes 49160 | tf_op jit(solution)/shard_map/ppermute | solution.py:1092
  243.1 4.6 collective-permute-start.41
  284.3 7.0 %collective-permute-start.49 = (f32[16,2048]{1,0:T(8,128)}, f32[16,2048]{1,0:T(8,128)S(1)}, u32[]{:S(2)}, u32[]{:S(2)}) collective-permute-start(f32[16,2048]{1,0:T(8,128)} %get-tuple-element.136.rest_0_.rest_4_), channel_id=1, source_target_pairs={{0,3},{1,2},{2,1},{3,0},{4,7},{5,6},{6,5},{7,4},{8,11},{9,10},{10,... | collective-permute-start | bytes 393224 | tf_op jit(solution)/shard_map/ppermute | solution.py:1092
  284.7 12.5 %collective-permute-start.48 = (f32[16,2048]{1,0:T(8,128)}, f32[16,2048]{1,0:T(8,128)S(1)}, u32[]{:S(2)}, u32[]{:S(2)}) collective-permute-start(f32[16,2048]{1,0:T(8,128)} %get-tuple-element.136.rest_0_.rest_4_), channel_id=1, source_target_pairs={{0,2},{1,3},{2,0},{3,1},{4,6},{5,7},{6,4},{7,5},{8,10},{9,11},{10,... | collective-permute-start | bytes 393224 | tf_op jit(solution)/shard_map/ppermute | solution.py:1092
  286.1 11.0 %collective-permute-start.47 = (f32[16,2048]{1,0:T(8,128)}, f32[16,2048]{1,0:T(8,128)S(1)}, u32[]{:S(2)}, u32[]{:S(2)}) collective-permute-start(f32[16,2048]{1,0:T(8,128)} %get-tuple-element.136.rest_0_.rest_4_), channel_id=1, source_target_pairs={{0,1},{1,0},{2,3},{3,2},{4,5},{5,4},{6,7},{7,6},{8,9},{9,8},{10,11... | collective-permute-start | bytes 393224 | tf_op jit(solution)/shard_map/ppermute | solution.py:1092
  347.0 4.5 collective-permute-start.56
  352.6 18.2 %collective-permute-start.57 = (bf16[8,48,512]{2,1,0:T(8,128)(2,1)}, bf16[8,48,512]{2,1,0:T(8,128)(2,1)S(1)}, u32[]{:S(2)}, u32[]{:S(2)}) collective-permute-start(bf16[8,48,512]{2,1,0:T(8,128)(2,1)} %add_convert_fusion.6), channel_id=1, source_target_pairs={{0,2},{1,3},{2,0},{3,1},{4,6},{5,7},{6,4},{7,5},{8,10},{9,11},{10,... | collective-permute-start | bytes 1179656 | tf_op jit(solution)/shard_map/ppermute | solution.py:1062
  360.9 28.4 %collective-permute-start.66 = (bf16[16,64,512]{2,1,0:T(8,128)(2,1)}, bf16[16,64,512]{2,1,0:T(8,128)(2,1)}, u32[]{:S(2)}, u32[]{:S(2)}) collective-permute-start(bf16[16,64,512]{2,1,0:T(8,128)(2,1)} %get-tuple-element.153), channel_id=1, source_target_pairs={{0,1},{1,0},{2,3},{3,2},{4,5},{5,4},{6,7},{7,6},{8,9},{9,8},{10,11... | collective-permute-start | bytes 3145736 | tf_op jit(solution)/shard_map/ppermute | solution.py:1062
  369.5 47.3 %collective-permute-start.71 = (bf16[16,128,512]{2,1,0:T(8,128)(2,1)}, bf16[16,128,512]{2,1,0:T(8,128)(2,1)S(1)}, u32[]{:S(2)}, u32[]{:S(2)}) collective-permute-start(bf16[16,128,512]{2,1,0:T(8,128)(2,1)} %get-tuple-element.163), channel_id=1, source_target_pairs={{0,1},{1,0},{2,3},{3,2},{4,5},{5,4},{6,7},{7,6},{8,9},{9,8},{10,11... | collective-permute-start | bytes 6291464 | tf_op jit(solution)/shard_map/ppermute | solution.py:1062
  370.0 47.2 %collective-permute-start.76 = (bf16[16,128,512]{2,1,0:T(8,128)(2,1)}, bf16[16,128,512]{2,1,0:T(8,128)(2,1)S(1)}, u32[]{:S(2)}, u32[]{:S(2)}) collective-permute-start(bf16[16,128,512]{2,1,0:T(8,128)(2,1)} %get-tuple-element.165), channel_id=1, source_target_pairs={{0,1},{1,0},{2,3},{3,2},{4,5},{5,4},{6,7},{7,6},{8,9},{9,8},{10,11... | collective-permute-start | bytes 6291464 | tf_op jit(solution)/shard_map/ppermute | solution.py:1062
  370.1 27.3 %collective-permute-start.61 = (bf16[16,80,512]{2,1,0:T(8,128)(2,1)}, bf16[16,80,512]{2,1,0:T(8,128)(2,1)S(1)}, u32[]{:S(2)}, u32[]{:S(2)}) collective-permute-start(bf16[16,80,512]{2,1,0:T(8,128)(2,1)} %get-tuple-element.151), channel_id=1, source_target_pairs={{0,1},{1,0},{2,3},{3,2},{4,5},{5,4},{6,7},{7,6},{8,9},{9,8},{10,11... | collective-permute-start | bytes 3932168 | tf_op jit(solution)/shard_map/ppermute | solution.py:1062
  372.6 12.1 %collective-permute-start.58 = (bf16[4,48,512]{2,1,0:T(8,128)(2,1)}, bf16[4,48,512]{2,1,0:T(8,128)(2,1)}, u32[]{:S(2)}, u32[]{:S(2)}) collective-permute-start(bf16[4,48,512]{2,1,0:T(8,128)(2,1)} %add_convert_fusion.11), channel_id=1, source_target_pairs={{0,8},{1,9},{2,10},{3,11},{4,12},{5,13},{6,14},{7,15},{8,0},{9,1},... | collective-permute-start | bytes 589832 | tf_op jit(solution)/shard_map/ppermute | solution.py:1062
  385.8 7.0 %collective-permute-start.59 = (bf16[2,48,512]{2,1,0:T(8,128)(2,1)S(1)}, bf16[2,48,512]{2,1,0:T(8,128)(2,1)S(1)}, u32[]{:S(2)}, u32[]{:S(2)}) collective-permute-start(bf16[2,48,512]{2,1,0:T(8,128)(2,1)S(1)} %add_convert_fusion.16), channel_id=1, source_target_pairs={{0,4},{1,5},{2,6},{3,7},{4,0},{5,1},{6,2},{7,3},{8,12},{9,13},{10,... | collective-permute-start | bytes 294920 | tf_op jit(solution)/shard_map/ppermute | solution.py:1062
  390.7 14.6 %collective-permute-start.67 = (bf16[8,64,512]{2,1,0:T(8,128)(2,1)S(1)}, bf16[8,64,512]{2,1,0:T(8,128)(2,1)S(1)}, u32[]{:S(2)}, u32[]{:S(2)}) collective-permute-start(bf16[8,64,512]{2,1,0:T(8,128)(2,1)S(1)} %add_convert_fusion.5), channel_id=1, source_target_pairs={{0,4},{1,5},{2,6},{3,7},{4,0},{5,1},{6,2},{7,3},{8,12},{9,13},{10,... | collective-permute-start | bytes 1572872 | tf_op jit(solution)/shard_map/ppermute | solution.py:1062
  393.6 6.3 %collective-permute-start.60 = (bf16[1,48,512]{2,1,0:T(8,128)(2,1)S(1)}, bf16[1,48,512]{2,1,0:T(8,128)(2,1)S(1)}, u32[]{:S(2)}, u32[]{:S(2)}) collective-permute-start(bf16[1,48,512]{2,1,0:T(8,128)(2,1)S(1)} %add_convert_fusion.19), channel_id=1, source_target_pairs={{0,16},{1,17},{2,18},{3,19},{4,20},{5,21},{6,22},{7,23},{8,24},{9,... | collective-permute-start | bytes 147464 | tf_op jit(solution)/shard_map/ppermute | solution.py:1062
  397.6 19.0 %collective-permute-start.62 = (bf16[8,80,512]{2,1,0:T(8,128)(2,1)S(1)}, bf16[8,80,512]{2,1,0:T(8,128)(2,1)S(1)}, u32[]{:S(2)}, u32[]{:S(2)}) collective-permute-start(bf16[8,80,512]{2,1,0:T(8,128)(2,1)S(1)} %add_convert_fusion.2), channel_id=1, source_target_pairs={{0,2},{1,3},{2,0},{3,1},{4,6},{5,7},{6,4},{7,5},{8,10},{9,11},{10,... | collective-permute-start | bytes 1966088 | tf_op jit(solution)/shard_map/ppermute | solution.py:1062
  406.4 11.2 %collective-permute-start.68 = (bf16[4,64,512]{2,1,0:T(8,128)(2,1)S(1)}, bf16[4,64,512]{2,1,0:T(8,128)(2,1)S(1)}, u32[]{:S(2)}, u32[]{:S(2)}) collective-permute-start(bf16[4,64,512]{2,1,0:T(8,128)(2,1)S(1)} %add_convert_fusion.10), channel_id=1, source_target_pairs={{0,8},{1,9},{2,10},{3,11},{4,12},{5,13},{6,14},{7,15},{8,0},{9,1},... | collective-permute-start | bytes 786440 | tf_op jit(solution)/shard_map/ppermute | solution.py:1062
  416.7 8.2 %collective-permute-start.63 = (bf16[4,80,512]{2,1,0:T(8,128)(2,1)S(1)}, bf16[4,80,512]{2,1,0:T(8,128)(2,1)S(1)}, u32[]{:S(2)}, u32[]{:S(2)}) collective-permute-start(bf16[4,80,512]{2,1,0:T(8,128)(2,1)S(1)} %add_convert_fusion.7), channel_id=1, source_target_pairs={{0,8},{1,9},{2,10},{3,11},{4,12},{5,13},{6,14},{7,15},{8,0},{9,1},... | collective-permute-start | bytes 983048 | tf_op jit(solution)/shard_map/ppermute | solution.py:1062
  417.1 30.5 %collective-permute-start.72 = (bf16[8,128,512]{2,1,0:T(8,128)(2,1)S(1)}, bf16[8,128,512]{2,1,0:T(8,128)(2,1)S(1)}, u32[]{:S(2)}, u32[]{:S(2)}) collective-permute-start(bf16[8,128,512]{2,1,0:T(8,128)(2,1)S(1)} %add_convert_fusion.1), channel_id=1, source_target_pairs={{0,2},{1,3},{2,0},{3,1},{4,6},{5,7},{6,4},{7,5},{8,10},{9,11},{10,... | collective-permute-start | bytes 3145736 | tf_op jit(solution)/shard_map/ppermute | solution.py:1062
  417.6 32.0 %collective-permute-start.77 = (bf16[8,128,512]{2,1,0:T(8,128)(2,1)S(1)}, bf16[8,128,512]{2,1,0:T(8,128)(2,1)S(1)}, u32[]{:S(2)}, u32[]{:S(2)}) collective-permute-start(bf16[8,128,512]{2,1,0:T(8,128)(2,1)S(1)} %add_convert_fusion), channel_id=1, source_target_pairs={{0,4},{1,5},{2,6},{3,7},{4,0},{5,1},{6,2},{7,3},{8,12},{9,13},{10,... | collective-permute-start | bytes 3145736 | tf_op jit(solution)/shard_map/ppermute | solution.py:1062
  418.6 25.0 %collective-permute-start.69 = (bf16[2,64,512]{2,1,0:T(8,128)(2,1)S(1)}, bf16[2,64,512]{2,1,0:T(8,128)(2,1)S(1)}, u32[]{:S(2)}, u32[]{:S(2)}) collective-permute-start(bf16[2,64,512]{2,1,0:T(8,128)(2,1)S(1)} %add_convert_fusion.15), channel_id=1, source_target_pairs={{0,2},{1,3},{2,0},{3,1},{4,6},{5,7},{6,4},{7,5},{8,10},{9,11},{10,... | collective-permute-start | bytes 393224 | tf_op jit(solution)/shard_map/ppermute | solution.py:1062
  425.0 19.7 %collective-permute-start.64 = (bf16[2,80,512]{2,1,0:T(8,128)(2,1)S(1)}, bf16[2,80,512]{2,1,0:T(8,128)(2,1)S(1)}, u32[]{:S(2)}, u32[]{:S(2)}) collective-permute-start(bf16[2,80,512]{2,1,0:T(8,128)(2,1)S(1)} %add_convert_fusion.12), channel_id=1, source_target_pairs={{0,4},{1,5},{2,6},{3,7},{4,0},{5,1},{6,2},{7,3},{8,12},{9,13},{10,... | collective-permute-start | bytes 491528 | tf_op jit(solution)/shard_map/ppermute | solution.py:1062
  444.5 5.8 %collective-permute-start.70 = (bf16[1,64,512]{2,1,0:T(8,128)(2,1)S(1)}, bf16[1,64,512]{2,1,0:T(8,128)(2,1)S(1)}, u32[]{:S(2)}, u32[]{:S(2)}) collective-permute-start(bf16[1,64,512]{2,1,0:T(8,128)(2,1)S(1)} %add_convert_fusion.18), channel_id=1, source_target_pairs={{0,16},{1,17},{2,18},{3,19},{4,20},{5,21},{6,22},{7,23},{8,24},{9,... | collective-permute-start | bytes 196616 | tf_op jit(solution)/shard_map/ppermute | solution.py:1062
  444.8 6.4 %collective-permute-start.65 = (bf16[1,80,512]{2,1,0:T(8,128)(2,1)S(1)}, bf16[1,80,512]{2,1,0:T(8,128)(2,1)S(1)}, u32[]{:S(2)}, u32[]{:S(2)}) collective-permute-start(bf16[1,80,512]{2,1,0:T(8,128)(2,1)S(1)} %add_convert_fusion.17), channel_id=1, source_target_pairs={{0,16},{1,17},{2,18},{3,19},{4,20},{5,21},{6,22},{7,23},{8,24},{9,... | collective-permute-start | bytes 245768 | tf_op jit(solution)/shard_map/ppermute | solution.py:1062
  447.9 14.9 %collective-permute-start.73 = (bf16[4,128,512]{2,1,0:T(8,128)(2,1)S(1)}, bf16[4,128,512]{2,1,0:T(8,128)(2,1)S(1)}, u32[]{:S(2)}, u32[]{:S(2)}) collective-permute-start(bf16[4,128,512]{2,1,0:T(8,128)(2,1)S(1)} %add_convert_fusion.4), channel_id=1, source_target_pairs={{0,8},{1,9},{2,10},{3,11},{4,12},{5,13},{6,14},{7,15},{8,0},{9,1},... | collective-permute-start | bytes 1572872 | tf_op jit(solution)/shard_map/ppermute | solution.py:1062
  449.8 23.2 %collective-permute-start.78 = (bf16[4,128,512]{2,1,0:T(8,128)(2,1)S(1)}, bf16[4,128,512]{2,1,0:T(8,128)(2,1)S(1)}, u32[]{:S(2)}, u32[]{:S(2)}) collective-permute-start(bf16[4,128,512]{2,1,0:T(8,128)(2,1)S(1)} %add_convert_fusion.3), channel_id=1, source_target_pairs={{0,8},{1,9},{2,10},{3,11},{4,12},{5,13},{6,14},{7,15},{8,0},{9,1},... | collective-permute-start | bytes 1572872 | tf_op jit(solution)/shard_map/ppermute | solution.py:1062
  463.0 11.7 %collective-permute-start.74 = (bf16[2,128,512]{2,1,0:T(8,128)(2,1)S(1)}, bf16[2,128,512]{2,1,0:T(8,128)(2,1)S(1)}, u32[]{:S(2)}, u32[]{:S(2)}) collective-permute-start(bf16[2,128,512]{2,1,0:T(8,128)(2,1)S(1)} %add_convert_fusion.9), channel_id=1, source_target_pairs={{0,4},{1,5},{2,6},{3,7},{4,0},{5,1},{6,2},{7,3},{8,12},{9,13},{10,... | collective-permute-start | bytes 786440 | tf_op jit(solution)/shard_map/ppermute | solution.py:1062
  473.2 7.3 %collective-permute-start.79 = (bf16[2,128,512]{2,1,0:T(8,128)(2,1)S(1)}, bf16[2,128,512]{2,1,0:T(8,128)(2,1)S(1)}, u32[]{:S(2)}, u32[]{:S(2)}) collective-permute-start(bf16[2,128,512]{2,1,0:T(8,128)(2,1)S(1)} %add_convert_fusion.8), channel_id=1, source_target_pairs={{0,2},{1,3},{2,0},{3,1},{4,6},{5,7},{6,4},{7,5},{8,10},{9,11},{10,... | collective-permute-start | bytes 786440 | tf_op jit(solution)/shard_map/ppermute | solution.py:1062
  474.8 9.0 %collective-permute-start.75 = (bf16[1,128,512]{2,1,0:T(8,128)(2,1)S(1)}, bf16[1,128,512]{2,1,0:T(8,128)(2,1)S(1)}, u32[]{:S(2)}, u32[]{:S(2)}) collective-permute-start(bf16[1,128,512]{2,1,0:T(8,128)(2,1)S(1)} %add_convert_fusion.14), channel_id=1, source_target_pairs={{0,16},{1,17},{2,18},{3,19},{4,20},{5,21},{6,22},{7,23},{8,24},{9,... | collective-permute-start | bytes 393224 | tf_op jit(solution)/shard_map/ppermute | solution.py:1062
  480.6 6.7 %collective-permute-start.80 = (bf16[1,128,512]{2,1,0:T(8,128)(2,1)S(1)}, bf16[1,128,512]{2,1,0:T(8,128)(2,1)S(1)}, u32[]{:S(2)}, u32[]{:S(2)}) collective-permute-start(bf16[1,128,512]{2,1,0:T(8,128)(2,1)S(1)} %add_convert_fusion.13), channel_id=1, source_target_pairs={{0,16},{1,17},{2,18},{3,19},{4,20},{5,21},{6,22},{7,23},{8,24},{9,... | collective-permute-start | bytes 393224 | tf_op jit(solution)/shard_map/ppermute | solution.py:1062
  (92 other events, 463.9 us)
Sparse Core Ops, SparseCore 0:
  13.0 128.4 all-gather.1
  264.1 145.3 reduce-scatter.1

commit v2 on v1

--- a/solution.py
+++ b/solution.py
@@ -15,6 +15,7 @@
 F32 = jnp.float32
 MID = 512
 HALO = 32
+UNROLL = 4
 NORM_ROW = {"1": 0, "2": 1, "3": 2, "S": 6, "4": 10, "5": 11, "6": 12}
 
 
@@ -59,7 +60,7 @@
 
 
 def aligned(row):
-    return pl.multiple_of(row, 16)
+    return row if isinstance(row, int) else pl.multiple_of(row, 16)
 
 
 def wide(mask):
@@ -92,15 +93,44 @@
         self.R = grid.rows
 
 
-    def chunks(self, body):
+    def sweep(self, cols, make, st=None, sums=()):
         for which in range(3):
-            start = self.g.seg[which]
-
-            def step(i, _, which=which, start=start):
-                body(which, aligned(start + i * 16))
-                return 0
-
-            lax.fori_loop(0, self.g.size[which] // 16, step, 0)
+            start, count = self.g.seg[which], self.g.size[which] // 16
+            for q in range(cols // MID):
+                lane = slice(q * MID, (q + 1) * MID)
+                work = make(which, q, lane)
+
+                def add(acc, row, work=work):
+                    terms = work(aligned(row)) or ()
+                    return tuple(a + t[:8] + t[8:] for a, t in zip(acc, terms))
+
+                def trip(i, acc, start=start, add=add):
+                    for j in range(UNROLL):
+                        acc = add(acc, start + (i * UNROLL + j) * 16)
+                    return acc
+
+                acc = tuple(jnp.zeros((8, MID), F32) for _ in sums)
+                trips = count // UNROLL
+                acc = lax.fori_loop(0, trips, trip, acc)
+                for j in range(trips * UNROLL, count):
+                    acc = add(acc, start + j * 16)
+                for row, a in zip(sums, acc):
+                    st[row + which : row + which + 1, lane] = jnp.sum(a, axis=0, keepdims=True)
+
+    def normal(self, c, nrm, which, lane=slice(0, MID)):
+        mean, rstd = nrm[which : which + 1, lane], nrm[3 + which : 4 + which, lane]
+        return lambda row: (c[pl.ds(row, 16), lane] - mean) * rstd
+
+    def scaled(self, normp, name, q):
+        at = NORM_ROW[name] + q
+        gain, bias = normp[at : at + 1, :], normp[16 + at : 17 + at, :]
+        return lambda xh: gain * xh + bias
+
+    def backed(self, normp, name, q, nrm, sums, which, lane=slice(0, MID)):
+        at = NORM_ROW[name] + q
+        a, b = sums[which : which + 1, lane], sums[3 + which : 4 + which, lane]
+        scale = normp[at : at + 1, :] * nrm[3 + which : 4 + which, lane]
+        return lambda dz, xh, m: scale * (dz - m * (a + xh * b))
 
     def load_start(self, layout, ids, refs, off, rows, dst, sem):
         for ref, (base, places) in zip(refs, layout):
@@ -140,36 +170,30 @@
     def local_stats(self, c_ref, m_ref, sc, out_ref, at, area, phases=1):
         cols = c_ref.shape[1]
         out_ref[pl.ds(at, 8), :] = jnp.zeros((8, cols), F32)
+        def make(which, q, lane):
+            start = self.g.seg[which]
+            base = c_ref[start : start + 1, lane]
+
+            def work(row):
+                m = wide(m_ref[pl.ds(row, 16), :])
+                total = square = None
+                for phase in range(phases):
+                    d = c_ref[pl.ds(aligned(row + phase * self.R), 16), lane] - base
+                    v = d * m
+                    total = v if total is None else total + v
+                    square = v * d if square is None else square + v * d
+                return total, square
+
+            return work
+
+        self.sweep(cols, make, out_ref, (at, at + 3))
         for which in range(3):
-            start, size = self.g.seg[which], self.g.size[which]
             held = sc[0, which] * float(area[which])
-            for q in range(cols // MID):
-                lane = slice(q * MID, (q + 1) * MID)
-
-                def first(i, acc, start=start, lane=lane):
-                    row = aligned(start + i * 16)
-                    m = wide(m_ref[pl.ds(row, 16), :])
-                    for phase in range(phases):
-                        v = c_ref[pl.ds(aligned(row + phase * self.R), 16), lane] * m
-                        acc = acc + v[:8] + v[8:]
-                    return acc
-
-                acc = lax.fori_loop(0, size // 16, first, jnp.zeros((8, MID), F32))
-                total = jnp.sum(acc, axis=0, keepdims=True)
-                mean = total / held
-
-                def second(i, acc, start=start, lane=lane, mean=mean):
-                    row = aligned(start + i * 16)
-                    m = wide(m_ref[pl.ds(row, 16), :])
-                    for phase in range(phases):
-                        v = c_ref[pl.ds(aligned(row + phase * self.R), 16), lane] - mean
-                        v = v * v * m
-                        acc = acc + v[:8] + v[8:]
-                    return acc
-
-                acc = lax.fori_loop(0, size // 16, second, jnp.zeros((8, MID), F32))
-                out_ref[at + which : at + which + 1, lane] = total
-                out_ref[at + 3 + which : at + 4 + which, lane] = jnp.sum(acc, axis=0, keepdims=True)
+            base = c_ref[self.g.seg[which] : self.g.seg[which] + 1, :]
+            total = out_ref[at + which : at + which + 1, :]
+            out_ref[at + which : at + which + 1, :] = total + held * base
+            square = out_ref[at + 3 + which : at + 4 + which, :]
+            out_ref[at + 3 + which : at + 4 + which, :] = square - total * (total / held)
 
     def group_norm(self, st_refs, at, sc, area, out_ref):
         cols = out_ref.shape[1]
@@ -193,23 +217,6 @@
             for row in (which, 3 + which):
                 rows = [ref[at + row : at + row + 1, :] for ref in st_refs]
                 out_ref[row : row + 1, :] = sum(rows[1:], rows[0]) / count
-
-    def xhat(self, c_ref, nrm, which, row, lane=slice(0, MID)):
-        return (c_ref[pl.ds(row, 16), lane] - nrm[which : which + 1, lane]) * nrm[3 + which : 4 + which, lane]
-
-    def affine(self, normp, name, q, xh):
-        at = NORM_ROW[name] + q
-        return normp[at : at + 1, :] * xh + normp[16 + at : 17 + at, :]
-
-    def norm_back(self, normp, name, q, nrm, sums, which, lane, dz, xh, m):
-        at = NORM_ROW[name] + q
-        a = sums[which : which + 1, lane]
-        b = sums[3 + which : 4 + which, lane]
-        scale = normp[at : at + 1, :] * nrm[3 + which : 4 + which, lane]
-        return scale * (dz - m * (a + xh * b))
-
-    def add_rows(self, out_ref, row, value, lane=slice(0, MID)):
-        out_ref[row : row + 1, lane] = out_ref[row : row + 1, lane] + jnp.sum(value, axis=0, keepdims=True)
 
     def shifted(self, hs_ref, dst_ref, col, sign_r, sign_c):
         for which in range(3):
@@ -279,71 +286,67 @@
             [pltpu.VMEM((4 * R, width), F32)],
         )
 
-    def conv_one(self, ids, sc, xp, msk, w, off, rows, norm_off):
+    def conv_one(self, ids, sc, xp, msk, w, off, rows):
         R = self.R
         width = xp.shape[1]
         layout, arrays = w
-        with_norm = norm_off is not None
 
         def body(ids, sc, xp, msk, *rest):
             refs = rest[: len(arrays)]
-            rest = rest[len(arrays) :]
+            c, st, ws, sem = rest[len(arrays) :]
+            self.load_start(layout, ids, refs, off, rows, ws, sem)
+            self.load_wait(ws, sem)
+            for phase in range(4):
+                c[phase * R : (phase + 1) * R, :] = dot_nn(xp[phase * R : (phase + 1) * R, :], ws[...])
+            self.local_stats(c, msk, sc, st, 0, self.area(2), 4)
+
+        return call(
+            body,
+            [(ids, SM), (sc, SM), (xp, VM), (msk, VM)] + [(a, HB) for a in arrays],
+            [((4 * R, MID), F32, VM), ((8, MID), F32, VM)],
+            [pltpu.VMEM((width, MID), BF), pltpu.SemaphoreType.DMA],
+            flops=2 * 4 * R * width * MID,
+        )
+
+    @staticmethod
+    def tap_two(tap):
+        i, j = divmod(tap, 3)
+        return (0 if i == 1 else 2) + (0 if j == 1 else 1), (1 if i == 0 else 0), (1 if j == 0 else 0)
+
+    def conv_two(self, ids, sc, c1, sts, normp, msk, w, off, rows, norm_off=None):
+        R = self.R
+        layout, arrays = w
+        nst, nw = len(sts), len(arrays)
+        with_norm = norm_off is not None
+
+        def body(ids, sc, c1, msk, *rest):
+            st_refs, refs, rest = rest[:nst], rest[nst : nst + nw], rest[nst + nw :]
             if with_norm:
-                c, st, normp, ws, ns, sem, sem2 = rest
+                a1, nrm, c2, st, normp, ws, hs, patches, sem, ns, sem2 = rest
                 self.load_start(layout, ids, refs, norm_off, 16, ns, sem2)
             else:
-                c, st, ws, sem = rest
+                normp, a1, nrm, c2, st, ws, hs, patches, sem = rest
             self.load_start(layout, ids, refs, off, rows, ws, sem)
+            self.group_norm(st_refs, 0, sc, self.area(2), nrm)
+            self.clear_halo(hs)
             if with_norm:
                 self.load_wait(ns, sem2)
                 for b in range(self.blocks):
                     normp[b : b + 1, :] = ns[b * 16 : b * 16 + 16, :].astype(F32)[0:1, :]
-            self.load_wait(ws, sem)
             for phase in range(4):
-                c[phase * R : (phase + 1) * R, :] = dot_nn(xp[phase * R : (phase + 1) * R, :], ws[...])
-            self.local_stats(c, msk, sc, st, 0, self.area(2), 4)
-
-        outs = [((4 * R, MID), F32, VM), ((8, MID), F32, VM)]
-        scratch = [pltpu.VMEM((width, MID), BF)]
-        if with_norm:
-            outs.append(((32, MID), F32, VM))
-            scratch.append(pltpu.VMEM((self.blocks * 16, MID), BF))
-            scratch.append(pltpu.SemaphoreType.DMA)
-        scratch.append(pltpu.SemaphoreType.DMA)
-        return call(
-            body,
-            [(ids, SM), (sc, SM), (xp, VM), (msk, VM)] + [(a, HB) for a in arrays],
-            outs,
-            scratch,
-            flops=2 * 4 * R * width * MID,
-        )
-
-    @staticmethod
-    def tap_two(tap):
-        i, j = divmod(tap, 3)
-        return (0 if i == 1 else 2) + (0 if j == 1 else 1), (1 if i == 0 else 0), (1 if j == 0 else 0)
-
-    def conv_two(self, ids, sc, c1, sts, normp, msk, w, off, rows):
-        R = self.R
-        layout, arrays = w
-        nst, nw = len(sts), len(arrays)
-
-        def body(ids, sc, c1, normp, msk, *rest):
-            st_refs, refs = rest[:nst], rest[nst : nst + nw]
-            a1, nrm, c2, st, ws, hs, patches, sem = rest[nst + nw :]
-            self.load_start(layout, ids, refs, off, rows, ws, sem)
-            self.group_norm(st_refs, 0, sc, self.area(2), nrm)
-            self.clear_halo(hs)
-            for phase in range(4):
-
-                def act(which, row, phase=phase):
-                    at = aligned(row + phase * R)
-                    m = wide(msk[pl.ds(row, 16), :])
-                    v = silu(self.affine(normp, "1", 0, self.xhat(c1, nrm, which, at))) * m
-                    hs[pl.ds(aligned(row + HALO), 16), :] = v
-                    a1[pl.ds(at, 16), :] = v.astype(BF)
-
-                self.chunks(act)
+
+                def make(which, q, lane, phase=phase):
+                    xh, put = self.normal(c1, nrm, which), self.scaled(normp, "1", 0)
+
+                    def work(row):
+                        at = aligned(row + phase * R)
+                        v = silu(put(xh(at))) * wide(msk[pl.ds(row, 16), :])
+                        hs[pl.ds(aligned(row + HALO), 16), :] = v
+                        a1[pl.ds(at, 16), :] = v.astype(BF)
+
+                    return work
+
+                self.sweep(MID, make)
                 for tap in range(9):
                     source, back_r, back_c = self.tap_two(tap)
                     if source == phase:
@@ -352,18 +355,20 @@
             c2[...] = dot_nn(patches[...], ws[...])
             self.local_stats(c2, msk, sc, st, 0, self.area(1))
 
-        return call(
-            body,
-            [(ids, SM), (sc, SM), (c1, VM), (normp, VM), (msk, VM)] + [(s, VM) for s in sts] + [(a, HB) for a in arrays],
-            [((4 * R, MID), BF, VM), ((8, MID), F32, VM), ((R, MID), F32, VM), ((8, MID), F32, VM)],
-            [
-                pltpu.VMEM((9 * MID, MID), BF),
-                pltpu.VMEM((R + 2 * HALO, MID), F32),
-                pltpu.VMEM((R, 9 * MID), BF),
-                pltpu.SemaphoreType.DMA,
-            ],
-            flops=2 * 9 * R * MID * MID,
-        )
+        ins = [(ids, SM), (sc, SM), (c1, VM), (msk, VM)] + [(s, VM) for s in sts] + [(a, HB) for a in arrays]
+        outs = [((4 * R, MID), BF, VM), ((8, MID), F32, VM), ((R, MID), F32, VM), ((8, MID), F32, VM)]
+        scratch = [
+            pltpu.VMEM((9 * MID, MID), BF),
+            pltpu.VMEM((R + 2 * HALO, MID), F32),
+            pltpu.VMEM((R, 9 * MID), BF),
+            pltpu.SemaphoreType.DMA,
+        ]
+        if with_norm:
+            outs.append(((self.blocks, MID), F32, VM))
+            scratch += [pltpu.VMEM((self.blocks * 16, MID), BF), pltpu.SemaphoreType.DMA]
+        else:
+            ins.append((normp, VM))
+        return call(body, ins, outs, scratch, flops=2 * 9 * R * MID * MID)
 
     def conv_short(self, ids, sc, xp, msk, w, off, rows):
         R = self.R
@@ -407,12 +412,16 @@
             self.load_start(layout, ids, refs, off, rows, ws, sem)
             self.group_norm(st_refs, 0, sc, self.area(1), nrm)
 
-            def one(which, row):
-                m = wide(msk[pl.ds(row, 16), :])
-                v = silu(self.affine(normp, name, 0, self.xhat(c, nrm, which, row))) * m
-                act[pl.ds(row, 16), :] = v.astype(BF)
-
-            self.chunks(one)
+            def make(which, q, lane):
+                xh, put = self.normal(c, nrm, which), self.scaled(normp, name, 0)
+
+                def work(row):
+                    v = silu(put(xh(row))) * wide(msk[pl.ds(row, 16), :])
+                    act[pl.ds(row, 16), :] = v.astype(BF)
+
+                return work
+
+            self.sweep(MID, make)
             self.load_wait(ws, sem)
             for q in range(out_width // MID):
                 lane = slice(q * MID, (q + 1) * MID)
@@ -440,26 +449,31 @@
 
         def body(ids, sc, c3, cs, normp, msk, *rest):
             st_refs, refs = rest[:nst], rest[nst : nst + nw]
-            h, hb, nrm3, nrms, c4, st, ws, sem = rest[nst + nw :]
+            h_far, hb_far, nrm3, nrms, c4, st, ws, h, hb, sem, sems = rest[nst + nw :]
             self.load_start(layout, ids, refs, off, rows, ws, sem)
             self.group_norm(st_refs, 0, sc, self.area(1), nrm3)
             self.group_norm(st_refs, 8, sc, self.area(1), nrms)
 
-            def one(which, row):
-                m = wide(msk[pl.ds(row, 16), :])
-                for q in range(out_width // MID):
-                    lane = slice(q * MID, (q + 1) * MID)
-                    pre = self.affine(normp, "3", q, self.xhat(c3, nrm3, which, row, lane)) + self.affine(
-                        normp, "S", q, self.xhat(cs, nrms, which, row, lane)
-                    )
-                    v = silu(pre) * m
+            def make(which, q, lane):
+                xh3, put3 = self.normal(c3, nrm3, which, lane), self.scaled(normp, "3", q)
+                xhs, puts = self.normal(cs, nrms, which, lane), self.scaled(normp, "S", q)
+
+                def work(row):
+                    v = silu(put3(xh3(row)) + puts(xhs(row))) * wide(msk[pl.ds(row, 16), :])
                     h[pl.ds(row, 16), lane] = v
                     hb[pl.ds(row, 16), lane] = v.astype(BF)
 
-            self.chunks(one)
+                return work
+
+            self.sweep(out_width, make)
+            out = [pltpu.make_async_copy(h, h_far, sems.at[0]), pltpu.make_async_copy(hb, hb_far, sems.at[1])]
+            for copy in out:
+                copy.start()
             self.load_wait(ws, sem)
             c4[...] = dot_nn(hb[...], ws[...])
             self.local_stats(c4, msk, sc, st, 0, self.area(1))
+            for copy in out:
+                copy.wait()
 
         return call(
             body,
@@ -467,14 +481,20 @@
             + [(s, VM) for s in sts]
             + [(a, HB) for a in arrays],
             [
-                ((R, out_width), F32, VM),
-                ((R, out_width), BF, VM),
+                ((R, out_width), F32, HB),
+                ((R, out_width), BF, HB),
                 ((8, out_width), F32, VM),
                 ((8, out_width), F32, VM),
                 ((R, MID), F32, VM),
                 ((8, MID), F32, VM),
             ],
-            [pltpu.VMEM((out_width, MID), BF), pltpu.SemaphoreType.DMA],
+            [
+                pltpu.VMEM((out_width, MID), BF),
+                pltpu.VMEM((R, out_width), F32),
+                pltpu.VMEM((R, out_width), BF),
+                pltpu.SemaphoreType.DMA,
+                pltpu.SemaphoreType.DMA((2,)),
+            ],
             flops=2 * R * MID * out_width,
         )
 
@@ -490,13 +510,17 @@
             self.group_norm(st_refs, 0, sc, self.area(1), nrm)
             self.clear_halo(hs)
 
-            def act(which, row):
-                m = wide(msk[pl.ds(row, 16), :])
-                v = silu(self.affine(normp, "4", 0, self.xhat(c4, nrm, which, row))) * m
-                hs[pl.ds(aligned(row + HALO), 16), :] = v
-                a4[pl.ds(row, 16), :] = v.astype(BF)
-
-            self.chunks(act)
+            def make(which, q, lane):
+                xh, put = self.normal(c4, nrm, which), self.scaled(normp, "4", 0)
+
+                def work(row):
+                    v = silu(put(xh(row))) * wide(msk[pl.ds(row, 16), :])
+                    hs[pl.ds(aligned(row + HALO), 16), :] = v
+                    a4[pl.ds(row, 16), :] = v.astype(BF)
+
+                return work
+
+            self.sweep(MID, make)
             for tap in range(9):
                 i, j = divmod(tap, 3)
                 self.shifted(hs, patches, tap * MID, i - 1, j - 1)
@@ -533,20 +557,22 @@
             for which, line, column, row in g.lines():
                 up[row : row + g.counts[which], :] = u_refs[which][line, column].astype(F32)
 
-            def one(which, row):
-                m = wide(msk[pl.ds(row, 16), :])
-                for q in range(out_width // MID):
-                    lane = slice(q * MID, (q + 1) * MID)
-                    xh = self.xhat(c6, nrm, which, row, lane)
-                    pre = self.affine(normp, "6", q, xh) + h[pl.ds(row, 16), lane]
+            def make(which, q, lane):
+                xh6, put = self.normal(c6, nrm, which, lane), self.scaled(normp, "6", q)
+
+                def work(row):
+                    m = wide(msk[pl.ds(row, 16), :])
+                    xh = xh6(row)
+                    pre = put(xh) + h[pl.ds(row, 16), lane]
                     s = jax.nn.sigmoid(pre)
                     res[pl.ds(row, 16), lane] = m * (pre * s)
                     d = up[pl.ds(row, 16), lane] * m * (s * (1.0 + pre * (1.0 - s)))
                     dz[pl.ds(row, 16), lane] = d
-                    self.add_rows(st, which, d, lane)
-                    self.add_rows(st, 3 + which, d * xh, lane)
-
-            self.chunks(one)
+                    return d, d * xh
+
+                return work
+
+            self.sweep(out_width, make, st, (0, 3))
             for which, line, column, row in g.lines():
                 o_refs[which][line, column] = res[row : row + g.counts[which], :].astype(BF)
 
@@ -571,15 +597,16 @@
             self.group_sums(st_refs, 0, sc, self.area(1), sums)
             st[...] = jnp.zeros(st.shape, F32)
 
-            def one(which, row):
-                m = wide(msk[pl.ds(row, 16), :])
-                for q in range(out_width // MID):
-                    lane = slice(q * MID, (q + 1) * MID)
-                    xh = self.xhat(c6, nrm6, which, row, lane)
-                    v = self.norm_back(normp, "6", q, nrm6, sums, which, lane, dz[pl.ds(row, 16), lane], xh, m)
-                    dc[pl.ds(row, 16), lane] = v.astype(BF)
-
-            self.chunks(one)
+            def make(which, q, lane):
+                xh, back = self.normal(c6, nrm6, which, lane), self.backed(normp, "6", q, nrm6, sums, which, lane)
+
+                def work(row):
+                    m = wide(msk[pl.ds(row, 16), :])
+                    dc[pl.ds(row, 16), lane] = back(dz[pl.ds(row, 16), lane], xh(row), m).astype(BF)
+
+                return work
+
+            self.sweep(out_width, make)
             self.load_wait(ws, sem)
             dz5[...] = dot_nn(dc[...], ws[...])
             self.through(dz5, c5, nrm5, normp, "5", msk, st)
@@ -595,17 +622,24 @@
         )
 
     def through(self, dz, c, nrm, normp, name, msk, st, phases=1):
-        def one(which, row):
-            m = wide(msk[pl.ds(row, 16), :])
-            for phase in range(phases):
-                at = aligned(row + phase * self.R)
-                xh = self.xhat(c, nrm, which, at)
-                d = dz[pl.ds(at, 16), :] * slope(self.affine(normp, name, 0, xh)) * m
-                dz[pl.ds(at, 16), :] = d
-                self.add_rows(st, which, d)
-                self.add_rows(st, 3 + which, d * xh)
-
-        self.chunks(one)
+        def make(which, q, lane):
+            xhat, put = self.normal(c, nrm, which), self.scaled(normp, name, 0)
+
+            def work(row):
+                m = wide(msk[pl.ds(row, 16), :])
+                one = two = None
+                for phase in range(phases):
+                    at = aligned(row + phase * self.R)
+                    xh = xhat(at)
+                    d = dz[pl.ds(at, 16), :] * slope(put(xh)) * m
+                    dz[pl.ds(at, 16), :] = d
+                    one = d if one is None else one + d
+                    two = d * xh if two is None else two + d * xh
+                return one, two
+
+            return work
+
+        self.sweep(MID, make, st, (0, 3))
 
     def back_five(self, ids, sc, dz5, c5, nrm5, sts, normp, msk, c4, nrm4, w, off, rows):
         R = self.R
@@ -649,17 +683,21 @@
         )
 
     def own_dc(self, dz, c, nrm, sums, normp, name, msk, dc, hs=None, phases=1):
-        def one(which, row):
-            m = wide(msk[pl.ds(row, 16), :])
-            for phase in range(phases):
-                at = aligned(row + phase * self.R)
-                xh = self.xhat(c, nrm, which, at)
-                v = self.norm_back(normp, name, 0, nrm, sums, which, slice(0, MID), dz[pl.ds(at, 16), :], xh, m)
-                dc[pl.ds(at, 16), :] = v.astype(BF)
-                if hs is not None:
-                    hs[pl.ds(aligned(row + HALO), 16), :] = v
-
-        self.chunks(one)
+        def make(which, q, lane):
+            xh, back = self.normal(c, nrm, which), self.backed(normp, name, 0, nrm, sums, which)
+
+            def work(row):
+                m = wide(msk[pl.ds(row, 16), :])
+                for phase in range(phases):
+                    at = aligned(row + phase * self.R)
+                    v = back(dz[pl.ds(at, 16), :], xh(at), m)
+                    dc[pl.ds(at, 16), :] = v.astype(BF)
+                    if hs is not None:
+                        hs[pl.ds(aligned(row + HALO), 16), :] = v
+
+            return work
+
+        self.sweep(MID, make)
 
     def back_four(self, ids, sc, dz4, c4, nrm4, sts, normp, msk, dz6, c3, nrm3, cs, nrms, w, off, rows):
         R = self.R
@@ -667,10 +705,16 @@
         nst, nw = len(sts), len(arrays)
         out_width = c3.shape[1]
 
-        def body(ids, sc, dz4, c4, nrm4, normp, msk, dz6, c3, nrm3, cs, nrms, *rest):
+        def body(ids, sc, dz4, c4, nrm4, normp, msk, dz6_far, c3_far, nrm3, cs_far, nrms, *rest):
             st_refs, refs = rest[:nst], rest[nst : nst + nw]
-            dc, dz3, st, sums, ws, sem = rest[nst + nw :]
+            dc, dz3, st, sums, ws, dz6, c3, cs, sem, sems = rest[nst + nw :]
             self.load_start(layout, ids, refs, off, rows, ws, sem)
+            late = [
+                pltpu.make_async_copy(far, held, sems.at[k])
+                for k, (far, held) in enumerate(((dz6_far, dz6), (c3_far, c3), (cs_far, cs)))
+            ]
+            for copy in late:
+                copy.start()
             self.group_sums(st_refs, 0, sc, self.area(1), sums)
             st[...] = jnp.zeros(st.shape, F32)
             self.own_dc(dz4, c4, nrm4, sums, normp, "4", msk, dc)
@@ -678,31 +722,35 @@
             for q in range(out_width // MID):
                 lane = slice(q * MID, (q + 1) * MID)
                 dz3[:, lane] = dot_nt(dc[...], ws[lane, :])
-
-            def one(which, row):
-                m = wide(msk[pl.ds(row, 16), :])
-                for q in range(out_width // MID):
-                    lane = slice(q * MID, (q + 1) * MID)
-                    xh3 = self.xhat(c3, nrm3, which, row, lane)
-                    xhs = self.xhat(cs, nrms, which, row, lane)
-                    pre = self.affine(normp, "3", q, xh3) + self.affine(normp, "S", q, xhs)
-                    d = (dz6[pl.ds(row, 16), lane] + dz3[pl.ds(row, 16), lane]) * slope(pre) * m
+            for copy in late:
+                copy.wait()
+
+            def make(which, q, lane):
+                xhat3, put3 = self.normal(c3, nrm3, which, lane), self.scaled(normp, "3", q)
+                xhats, puts = self.normal(cs, nrms, which, lane), self.scaled(normp, "S", q)
+
+                def work(row):
+                    xh3, xhs = xhat3(row), xhats(row)
+                    d = (dz6[pl.ds(row, 16), lane] + dz3[pl.ds(row, 16), lane]) * slope(put3(xh3) + puts(xhs))
+                    d = d * wide(msk[pl.ds(row, 16), :])
                     dz3[pl.ds(row, 16), lane] = d
-                    self.add_rows(st, which, d, lane)
-                    self.add_rows(st, 3 + which, d * xh3, lane)
-                    self.add_rows(st, 8 + 3 + which, d * xhs, lane)
-
-            self.chunks(one)
+                    return d, d * xh3, d * xhs
+
+                return work
+
+            self.sweep(out_width, make, st, (0, 3, 11))
             st[8:11, :] = st[0:3, :]
 
         return call(
             body,
             [(ids, SM), (sc, SM), (dz4, VM), (c4, VM), (nrm4, VM), (normp, VM), (msk, VM)]
-            + [(dz6, VM), (c3, VM), (nrm3, VM), (cs, VM), (nrms, VM)]
+            + [(dz6, HB), (c3, HB), (nrm3, VM), (cs, HB), (nrms, VM)]
             + [(s, VM) for s in sts]
             + [(a, HB) for a in arrays],
             [((R, MID), BF, VM), ((R, out_width), F32, VM), ((16, out_width), F32, VM)],
-            [pltpu.VMEM((8, MID), F32), pltpu.VMEM((out_width, MID), BF), pltpu.SemaphoreType.DMA],
+            [pltpu.VMEM((8, MID), F32), pltpu.VMEM((out_width, MID), BF)]
+            + [pltpu.VMEM((R, out_width), F32)] * 3
+            + [pltpu.SemaphoreType.DMA, pltpu.SemaphoreType.DMA((3,))],
             flops=2 * R * MID * out_width,
         )
 
@@ -714,30 +762,33 @@
 
         def body(ids, sc, dz3, c3, nrm3, cs, nrms, normp, msk, c2, nrm2, *rest):
             st_refs, refs = rest[:nst], rest[nst : nst + nw]
-            dc3, dcs, dz2, st, sums3, sumss, ws, sem = rest[nst + nw :]
+            dc3_far, dcs_far, dz2, st, sums3, sumss, ws, dc3, dcs, sem, sems = rest[nst + nw :]
             self.load_start(layout, ids, refs, off, rows, ws, sem)
             self.group_sums(st_refs, 0, sc, self.area(1), sums3)
             self.group_sums(st_refs, 8, sc, self.area(1), sumss)
             st[...] = jnp.zeros(st.shape, F32)
 
-            def one(which, row):
-                m = wide(msk[pl.ds(row, 16), :])
-                for q in range(out_width // MID):
-                    lane = slice(q * MID, (q + 1) * MID)
+            def make(which, q, lane):
+                xh3, back3 = self.normal(c3, nrm3, which, lane), self.backed(normp, "3", q, nrm3, sums3, which, lane)
+                xhs, backs = self.normal(cs, nrms, which, lane), self.backed(normp, "S", q, nrms, sumss, which, lane)
+
+                def work(row):
+                    m = wide(msk[pl.ds(row, 16), :])
                     d = dz3[pl.ds(row, 16), lane]
-                    xh = self.xhat(c3, nrm3, which, row, lane)
-                    dc3[pl.ds(row, 16), lane] = self.norm_back(
-                        normp, "3", q, nrm3, sums3, which, lane, d, xh, m
-                    ).astype(BF)
-                    xh = self.xhat(cs, nrms, which, row, lane)
-                    dcs[pl.ds(row, 16), lane] = self.norm_back(
-                        normp, "S", q, nrms, sumss, which, lane, d, xh, m
-                    ).astype(BF)
-
-            self.chunks(one)
+                    dc3[pl.ds(row, 16), lane] = back3(d, xh3(row), m).astype(BF)
+                    dcs[pl.ds(row, 16), lane] = backs(d, xhs(row), m).astype(BF)
+
+                return work
+
+            self.sweep(out_width, make)
+            out = [pltpu.make_async_copy(dc3, dc3_far, sems.at[0]), pltpu.make_async_copy(dcs, dcs_far, sems.at[1])]
+            for copy in out:
+                copy.start()
             self.load_wait(ws, sem)
             dz2[...] = dot_nn(dc3[...], ws[...])
             self.through(dz2, c2, nrm2, normp, "2", msk, st)
+            for copy in out:
+                copy.wait()
 
         return call(
             body,
@@ -745,12 +796,15 @@
             + [(c2, VM), (nrm2, VM)]
             + [(s, VM) for s in sts]
             + [(a, HB) for a in arrays],
-            [((R, out_width), BF, VM), ((R, out_width), BF, VM), ((R, MID), F32, VM), ((8, MID), F32, VM)],
+            [((R, out_width), BF, HB), ((R, out_width), BF, HB), ((R, MID), F32, VM), ((8, MID), F32, VM)],
             [
                 pltpu.VMEM((8, out_width), F32),
                 pltpu.VMEM((8, out_width), F32),
                 pltpu.VMEM((out_width, MID), BF),
+                pltpu.VMEM((R, out_width), BF),
+                pltpu.VMEM((R, out_width), BF),
                 pltpu.SemaphoreType.DMA,
+                pltpu.SemaphoreType.DMA((2,)),
             ],
             flops=2 * R * MID * out_width,
         )
@@ -936,10 +990,8 @@
             hs, patches = tail
             self.clear_halo(hs)
 
-            def spread(which, row):
-                hs[pl.ds(aligned(row + HALO), 16), :] = dc[pl.ds(row, 16), :].astype(F32)
-
-            self.chunks(spread)
+            for row in range(0, R, 16):
+                hs[HALO + row : HALO + row + 16, :] = dc[row : row + 16, :].astype(F32)
             if stride == 1:
                 shifts = [(1 - tap // 3, 1 - tap % 3) for tap in range(9)]
             else:
@@ -997,6 +1049,78 @@
     return (list(range(count))[::-1],) * 3
 
 
+class Order:
+    def __init__(self, free=False):
+        self.last, self.free = None, free
+
+    def hold(self, value):
+        if self.last is None:
+            return value
+        return lax.optimization_barrier((value, self.last))[0]
+
+    def mark(self, value):
+        self.last = None if self.free else value
+
+
+class Gather:
+    def __init__(self, seq, swap, buf, order):
+        self.seq, self.swap, self.bits = seq, swap, list(order)
+        self.held, self.places = buf[None], [0]
+        self.go()
+
+    def go(self):
+        bit = self.bits.pop(0)
+        self.got = self.swap(self.held, bit)
+        self.there = [r ^ (1 << bit) for r in self.places]
+
+    def step(self):
+        self.held = jnp.concatenate([self.held, self.seq.hold(self.got)])
+        self.places = self.places + self.there
+        self.seq.mark(self.held)
+        self.go()
+
+    def result(self):
+        return [self.places, self.there], [self.held, self.got]
+
+
+class Scatter:
+    def __init__(self, seq, swap, pieces, order):
+        self.seq, self.swap, self.bits = seq, swap, list(order)
+        self.kept = [pieces[0]]
+        self.got = swap(pieces[1], self.bits.pop(0))
+
+    @staticmethod
+    def places(order):
+        kept = [0]
+        for bit in reversed(order[1:]):
+            kept = kept + [r ^ (1 << bit) for r in kept]
+        return [kept, [r ^ (1 << order[0]) for r in kept]]
+
+    def step(self):
+        kept = self.kept + [self.seq.hold(self.got)]
+        half = kept[0].shape[0] // 2
+        sent = sum([k[half:].astype(F32) for k in kept[1:]], kept[0][half:].astype(F32)).astype(BF)
+        self.kept = [k[:half] for k in kept]
+        self.seq.mark(sent)
+        self.got = self.swap(sent, self.bits.pop(0))
+
+    def result(self):
+        kept = self.kept + [self.seq.hold(self.got)]
+        return sum([k[0].astype(F32) for k in kept[1:]], kept[0][0].astype(F32))
+
+
+def gentle(total):
+    if total == 32:
+        return [1, 4, 3, 2, 0], [1, 2, 4, 3, 0]
+    return orders(total)[:2]
+
+
+def backward_orders(total):
+    if total == 32:
+        return [0, 2, 3, 4, 1], [0, 3, 2, 1, 4], [0, 1, 2, 3, 4], [0, 3, 1, 2, 4]
+    return [orders(total)[0][::-1]] * 4
+
+
 def on_device(*args):
     slots_inside = (1, 2, 0, 3)
     images = [jnp.transpose(args[k], slots_inside) for k in (0, 2, 1)]
@@ -1009,7 +1133,10 @@
     me = pos_dp * members + pos_bn
     grid = Grid([p.shape[2] for p in images], [u.shape[1] for u in ups])
 
-    low = [p.astype(BF) for p in params]
+    seq = Order()
+    low = [params[0].astype(BF)]
+    seq.mark(low[0])
+    low += [seq.hold(p).astype(BF) for p in params[1:]]
     short_t = low[3].T
     shards = {
         "1": low[0],
@@ -1061,80 +1188,92 @@
     def swap(array, bit):
         return lax.ppermute(array, BOTH, [(i, i ^ (1 << bit)) for i in range(total)])
 
-    def butterfly_gather(buf, order):
-        held, places, steps = buf[None], [0], []
-        for step, bit in enumerate(order):
-            got = swap(held, bit)
-            steps.append(got)
-            there = [r ^ (1 << bit) for r in places]
-            if step == len(order) - 1:
-                return [places, there], [held, got], steps
-            held, places = jnp.concatenate([held, got]), places + there
-
-    def gather_near(names, chains, with_norm=False, after=None):
-        if not direct:
-            made, where = gather(names)
-            return made, where, None
-        buf = packed(names, with_norm)
-        if after is not None:
-            buf = lax.optimization_barrier((buf, after))[0]
-        layout, arrays, at, steps = [], [], 0, None
-        for height, order in chains:
-            places, got, steps = butterfly_gather(buf[at : at + height], order)
-            for p, a in zip(places, got):
-                layout.append((at, p))
-                arrays.append(a)
-            at += height
-        return (layout, arrays), offsets(names)[0], steps
-
     def exchange(stat):
         return [stat] + [
             lax.ppermute(stat, "bn", [(i, i ^ k) for i in range(members)]) for k in range(1, members)
         ]
 
     first, second, third = orders(total)
-    r2 = rows["2"] // 48 * 16
-    w1, at_1, steps = gather_near(["1"], [(rows["1"] + 16, first)], True)
-    w2, at_2, _ = gather_near(
-        ["2"],
-        [(r2, first), (r2, second), (rows["2"] - 2 * r2, third)],
-        after=steps[1] if direct else None,
+
+    def chains(buf, cuts, seq):
+        made, at = [], 0
+        for height, order in cuts:
+            made.append((at, Gather(seq, swap, buf[at : at + height], order)))
+            at += height
+        return made
+
+    def steps(made):
+        for _, chain in made:
+            chain.step()
+
+    def results(made):
+        layout, arrays = [], []
+        for at, chain in made:
+            for places, array in zip(*chain.result()):
+                layout.append((at, places))
+                arrays.append(array)
+        return layout, arrays
+
+    if direct:
+        r2 = rows["2"] // 48 * 16
+        quiet_x, _ = gentle(total)
+        free = Order(True)
+        g_one = chains(packed(["1"]), [(rows["1"], first)], free)
+        buf2, buf5 = packed(["2"], True), packed(["5"])
+        wb, at_b = gather(["3", "S", "4", "6"])
+        steps(g_one)
+        later = lax.optimization_barrier((buf2, g_one[0][1].held))[0]
+        g_two = chains(later, [(r2, first), (r2, second), (rows["2"] - 2 * r2 + 16, third)], free)
+        for _ in range(3):
+            steps(g_one)
+        for _ in range(4):
+            steps(g_two)
+        xp, msk, sc = dev.prepare(spot, lives, images)
+        c1, st1 = dev.conv_one(near, sc, xp, msk, results(g_one), 0, rows["1"])
+        seq.mark(st1)
+        st1 = exchange(st1)
+        g_five = chains(seq.hold(buf5), [(rows["5"], quiet_x)], seq)
+        a1, nrm1, c2, st2, normp = dev.conv_two(
+            near, sc, c1, st1, None, seq.hold(msk), results(g_two), 0, rows["2"], rows["2"]
+        )
+        seq.mark(st2)
+        st2 = exchange(st2)
+        steps(g_five)
+        steps(g_five)
+        cs, sts = dev.conv_short(far, sc, xp, seq.hold(msk), wb, at_b["S"], rows["S"])
+        seq.mark(sts)
+        steps(g_five)
+        a2, nrm2, c3, st3 = dev.conv_expand(
+            far, sc, c2, st2, normp, seq.hold(msk), wb, at_b["3"], rows["3"], "2", sts
+        )
+        seq.mark(st3)
+        st3 = exchange(st3)
+        w1, w2 = results(g_one), results(g_two)
+        w3 = w4 = w6 = wb
+        at_3 = at_b
+    else:
+        w1, w2, w4, w5, w6 = [gather([k])[0] for k in ("1", "2", "4", "5", "6")]
+        w3, at_3 = gather(["3", "S"])
+        xp, msk, sc = dev.prepare(spot, lives, images)
+        c1, st1 = dev.conv_one(near, sc, xp, msk, w1, 0, rows["1"])
+        normp = lax.all_gather(low[7], BOTH, axis=0, tiled=True).astype(F32).reshape(32, MID)
+        a1, nrm1, c2, st2 = dev.conv_two(near, sc, c1, exchange(st1), normp, msk, w2, 0, rows["2"])
+        cs, sts = dev.conv_short(far, sc, xp, msk, w3, at_3["S"], rows["S"])
+        a2, nrm2, c3, st3 = dev.conv_expand(
+            far, sc, c2, exchange(st2), normp, msk, w3, at_3["3"], rows["3"], "2", sts
+        )
+        st3 = exchange(st3)
+        at_b = {"4": 0, "6": 0}
+    h, hb, nrm3, nrms, c4, st4 = dev.conv_four(
+        far, sc, c3, cs, st3, normp, msk, w4, at_b["4"], rows["4"]
     )
-    wb, at_b = gather(["3", "S", "4", "5", "6"])
-
-    xp, msk, sc = dev.prepare(spot, lives, images)
     if direct:
-        c1, st1, normp = dev.conv_one(near, sc, xp, msk, w1, at_1["1"], rows["1"], rows["1"])
-    else:
-        c1, st1 = dev.conv_one(near, sc, xp, msk, w1, at_1["1"], rows["1"], None)
-        normp = lax.all_gather(low[7], BOTH, axis=0, tiled=True).astype(F32).reshape(32, MID)
-    a1, nrm1, c2, st2 = dev.conv_two(near, sc, c1, exchange(st1), normp, msk, w2, at_2["2"], rows["2"])
-    cs, sts = dev.conv_short(far, sc, xp, msk, wb, at_b["S"], rows["S"])
-    a2, nrm2, c3, st3 = dev.conv_expand(
-        far, sc, c2, exchange(st2), normp, msk, wb, at_b["3"], rows["3"], "2", sts
-    )
-    h, hb, nrm3, nrms, c4, st4 = dev.conv_four(
-        far, sc, c3, cs, exchange(st3), normp, msk, wb, at_b["4"], rows["4"]
-    )
-    a4, nrm4, c5, st5 = dev.conv_five(far, sc, c4, exchange(st4), normp, msk, wb, at_b["5"], rows["5"])
-    a5, nrm5, c6, st6 = dev.conv_expand(far, sc, c5, exchange(st5), normp, msk, wb, at_b["6"], rows["6"], "5")
+        seq.mark(st4)
+        steps(g_five)
+        w5 = results(g_five)
+    a4, nrm4, c5, st5 = dev.conv_five(near, sc, c4, exchange(st4), normp, msk, w5, 0, rows["5"])
+    a5, nrm5, c6, st6 = dev.conv_expand(far, sc, c5, exchange(st5), normp, msk, w6, at_b["6"], rows["6"], "5")
     oc, oa, ob, dz6, nrm6, su6 = dev.finish(sc, c6, h, exchange(st6), normp, msk, ups)
-
-    def split_places(order):
-        places = [0]
-        for bit in reversed(order[1:]):
-            places = places + [r ^ (1 << bit) for r in places]
-        return [places, [r ^ (1 << order[0]) for r in places]]
-
-    def butterfly_scatter(pieces, order):
-        kept, sent = [pieces[0]], pieces[1]
-        for step, bit in enumerate(order):
-            kept.append(swap(sent, bit))
-            if step < len(order) - 1:
-                half = kept[0].shape[0] // 2
-                sent = sum([k[half:].astype(F32) for k in kept[1:]], kept[0][half:].astype(F32)).astype(BF)
-                kept = [k[:half] for k in kept]
-        return sum([k[0].astype(F32) for k in kept[1:]], kept[0][0].astype(F32))
 
     def scatter(piece, heights):
         if not direct:
@@ -1146,11 +1285,6 @@
         owned = lax.psum_scatter(piece.reshape(-1, MID), BOTH, scatter_dimension=0, tiled=True)
         return owned.astype(F32)
 
-    def scatter_near(pieces, used, heights):
-        if not direct:
-            return [scatter(pieces[0], heights)]
-        return [butterfly_scatter(pieces[2 * c : 2 * c + 2], order) for c, order in enumerate(used)]
-
     def cut(owned, heights):
         parts, spot_row = [], 0
         for height in heights:
@@ -1160,7 +1294,7 @@
         return parts
 
     whole = [[list(range(total)) if direct else [0]]]
-    back_first, back_second = first[::-1], second[::-1]
+    order_a, order_b, order_two, order_one = backward_orders(total)
 
     def halves(k):
         if not direct:
@@ -1168,50 +1302,93 @@
         one = rows[k] // 32 * 16
         return [rows[k] - one, one]
 
-    pair = [back_first, back_second] if direct else [None]
-    pair_places = [split_places(order) for order in pair] if direct else whole
-    single = [back_first] if direct else [None]
-    single_places = [split_places(back_first)] if direct else whole
+    pair = [order_a, order_b] if direct else [None]
+    pair_places = [Scatter.places(order) for order in pair] if direct else whole
+    two_places = [Scatter.places(order_two)] if direct else whole
+    single_places = [Scatter.places(order_one)] if direct else whole
+
+    def sums(made, orders_used):
+        if not direct:
+            return []
+        return [Scatter(seq, swap, made[0][2 * c : 2 * c + 2], order) for c, order in enumerate(orders_used)]
+
+    def advance(made):
+        for chain in made:
+            chain.step()
 
     dc6, dz5, su5 = dev.back_six(
-        far, sc, dz6, c6, nrm6, exchange(su6), normp, msk, c5, nrm5, wb, at_b["6"], rows["6"]
+        far, sc, dz6, c6, nrm6, exchange(su6), normp, msk, c5, nrm5, w6, at_b["6"], rows["6"]
     )
+    seq.mark(su5)
     high = [rows["6"] + rows["5"]]
-    g65 = dev.grad_outer(far, whole, [(dc6, a5)], [(rows["6"], [rows["6"]])], high)
+    g65 = dev.grad_outer(seq.hold(far), whole, [(dc6, a5)], [(rows["6"], [rows["6"]])], high)
+    seq.mark(g65[0][0])
     dc5, dz4, su4 = dev.back_five(
-        far, sc, dz5, c5, nrm5, exchange(su5), normp, msk, c4, nrm4, wb, at_b["5"], rows["5"]
+        near, sc, dz5, c5, nrm5, exchange(su5), normp, seq.hold(msk), c4, nrm4, w5, 0, rows["5"]
     )
-    g65 = dev.grad_taps(far, whole, a4, dc5, [(rows["5"], [rows["5"]])], high, 1, g65)
+    seq.mark(su4)
+    g65 = dev.grad_taps(seq.hold(far), whole, a4, dc5, [(rows["5"], [rows["5"]])], high, 1, g65)
+    seq.mark(g65[0][0])
     hts65 = [rows["6"], rows["5"]]
-    o6, o5 = cut(scatter(g65[0][0], hts65), hts65)
+    owned65 = scatter(g65[0][0], hts65)
 
     dc4, dz3, su3 = dev.back_four(
-        far, sc, dz4, c4, nrm4, exchange(su4), normp, msk, dz6, c3, nrm3, cs, nrms, wb, at_b["4"], rows["4"]
+        far, sc, dz4, c4, nrm4, exchange(su4), normp, seq.hold(msk), dz6, c3, nrm3, cs, nrms, w4, at_b["4"], rows["4"]
     )
+    seq.mark(su3)
     part4, part3 = (rows["4"], halves("4")), (rows["3"], halves("3"))
     mid = [a + 3 * b for a, b in zip(part4[1], part3[1])]
-    g43 = dev.grad_outer(near, pair_places, [(hb, dc4)], [part4], mid)
+    g43 = dev.grad_outer(seq.hold(near), pair_places, [(hb, dc4)], [part4], mid)
+    seq.mark(g43[0][0])
     dc3, dcs, dz2, su2 = dev.back_three(
-        far, sc, dz3, c3, nrm3, cs, nrms, exchange(su3), normp, msk, c2, nrm2, wb, at_b["3"], rows["3"]
+        far, sc, dz3, c3, nrm3, cs, nrms, exchange(su3), normp, seq.hold(msk), c2, nrm2, w3, at_3["3"], rows["3"]
     )
-    g43 = dev.grad_short(near, pair_places, a2, dc3, dcs, xp, [part3] * 3, mid, g43)
-    got = scatter_near(g43[0], pair, [rows["4"]] + [rows["3"]] * 3)
-    cuts = [cut(owned, [part4[1][c]] + [part3[1][c]] * 3) for c, owned in enumerate(got)]
+    seq.mark(su2)
+    g43 = dev.grad_short(seq.hold(near), pair_places, a2, dc3, dcs, xp, [part3] * 3, mid, g43)
+    seq.mark(g43[0][0])
+    s43 = sums(g43, pair)
+    dc2, dz1, su1 = dev.back_two(
+        near, sc, dz2, c2, nrm2, exchange(su2), normp, seq.hold(msk), c1, nrm1, w2, 0, rows["2"]
+    )
+    seq.mark(su1)
+    advance(s43)
+    g2 = dev.grad_taps(seq.hold(near), two_places, a1, dc2, [(rows["2"], [rows["2"]])], [rows["2"]], 2)
+    seq.mark(g2[0][0])
+    s2 = sums(g2, [order_two])
+    dc1 = dev.back_one(sc, dz1, c1, nrm1, exchange(su1), normp, seq.hold(msk))
+    seq.mark(dc1)
+    advance(s2)
+    advance(s43)
+    parts = [(rows["1"], [rows["1"]])] + ([(16, [16])] if direct else [])
+    g1 = dev.grad_first(
+        seq.hold(near), single_places, xp, dc1, (su1, su2, su3, su4, su5, su6), parts, [sum(p for p, _ in parts)]
+    )
+    seq.mark(g1[0][0])
+    s1 = sums(g1, [order_one])
+    grads = dev.input_grad(seq.hold(near), dc1, dcs, w1, 0, rows["1"], far, w3, at_3["S"], rows["S"], images)
+    seq.mark(grads[0])
+    gc_, ga_, gb_ = grads
+    if direct:
+        advance(s1)
+        advance(s43)
+        advance(s2)
+        advance(s1)
+        advance(s43)
+        advance(s2)
+        advance(s1)
+        advance(s2)
+        advance(s1)
+        got43 = [chain.result() for chain in s43]
+        got2 = [chain.result() for chain in s2]
+        last = s1[0].result()
+    else:
+        got43 = [scatter(g43[0][0], [rows["4"]] + [rows["3"]] * 3)]
+        got2 = [scatter(g2[0][0], [rows["2"]])]
+        last = scatter(g1[0][0], [rows["1"]])
+    cuts = [cut(owned, [part4[1][c]] + [part3[1][c]] * 3) for c, owned in enumerate(got43)]
     o4, o3, osa, osb = [jnp.concatenate(p, axis=0) if len(p) > 1 else p[0] for p in zip(*cuts)]
-
-    dc2, dz1, su1 = dev.back_two(
-        near, sc, dz2, c2, nrm2, exchange(su2), normp, msk, c1, nrm1, w2, at_2["2"], rows["2"]
-    )
-    g2 = dev.grad_taps(near, pair_places, a1, dc2, [(rows["2"], halves("2"))], halves("2"), 2)
-    got = scatter_near(g2[0], pair, [rows["2"]])
-    o2 = jnp.concatenate(got, axis=0) if len(got) > 1 else got[0]
-    dc1 = dev.back_one(sc, dz1, c1, nrm1, exchange(su1), normp, msk)
-    sums = (su1, su2, su3, su4, su5, su6)
-    parts = [(rows["1"], [rows["1"]])] + ([(16, [16])] if direct else [])
-    g1 = dev.grad_first(near, single_places, xp, dc1, sums, parts, [sum(p for p, _ in parts)])
-    grads = dev.input_grad(near, dc1, dcs, w1, at_1["1"], rows["1"], far, wb, at_b["S"], rows["S"], images)
-    gc_, ga_, gb_ = grads
-    last = scatter_near(g1[0], single, [rows["1"]])[0]
+    o2 = jnp.concatenate(got2, axis=0) if len(got2) > 1 else got2[0]
+    o6, o5 = cut(owned65, hts65)
     o1 = last[: rows["1"]] if direct else last
     if direct:
         onorm = last[rows["1"]]

time: 505 us -> 482 us (0.954)
  waiting for transfers between devices: 178 us -> 138 us
  other arithmetic: 27.3 us -> 43.6 us
  Pallas kernels: 195 us -> 184 us
  starting transfers between devices: 71.7 us -> 77.7 us
    all_gather x1, waiting for transfers between devices: 26.7 us -> 0.01 us  [gather(): lax.all_gather(buf, BOTH, axis=0, tiled=True)]
    convert_element_type x23 -> x19, other arithmetic: 11.1 us -> 25.9 us  [the longest x16 24.2 us: step(): sum([k[half:].astype(F32) for k in kept[1:]], kept[0][half:].astype(F32))]
    pallas_call x22, Pallas kernels: 195 us -> 184 us  [call(): pl.pallas_call(body, out_shape=[jax.ShapeDtypeStruct(shape, dtype) for sh...]
    ppermute x45, waiting for transfers between devices: 108 us -> 101 us  [swap(): return lax.ppermute(array, BOTH, [(i, i ^ 1 << bit) for i in range(total)])]
    ppermute x45, starting transfers between devices: 47.1 us -> 52.9 us  [swap(): return lax.ppermute(array, BOTH, [(i, i ^ 1 << bit) for i in range(total)])]
    ppermute x36, waiting for transfers between devices: 42.8 us -> 37.1 us  [exchange(): lax.ppermute(stat, 'bn', [(i, i ^ k) for i in range(members)])]
    unnamed x161 -> x174, local copies, waits for them, and re-layouts: 11.5 us -> 16.4 us
  transfers between devices with their start and end apart: 83 -> 83, of which waited for: 47 -> 39; matrix products, arithmetic and copies ran while one was open for 5% -> 9% of each run, Pallas kernels for 25% -> 29%
where the time goes in v2:
time: 482 us; the launch traced here: 476 us
  Pallas kernels  184 us (38%)
  waiting for transfers between devices  138 us (29%)
  starting transfers between devices  77.7 us (16%)
  other arithmetic  43.6 us (9%)
  local copies, waits for them, and re-layouts  17.5 us (4%)
  between operations  15.4 us (3%)
    pallas_call x22, Pallas kernels, call(): pl.pallas_call(body, out_shape=[jax.ShapeDtypeStruct(shape, dtype) for sh...  184 us
    ppermute x45, waiting for transfers between devices, swap(): return lax.ppermute(array, BOTH, [(i, i ^ 1 << bit) for i in range(total)])  101 us
    ppermute x45, starting transfers between devices, swap(): return lax.ppermute(array, BOTH, [(i, i ^ 1 << bit) for i in range(total)])  52.9 us
    ppermute x36, waiting for transfers between devices, exchange(): lax.ppermute(stat, 'bn', [(i, i ^ k) for i in range(members)])  37.1 us
    ppermute x36, starting transfers between devices, exchange(): lax.ppermute(stat, 'bn', [(i, i ^ k) for i in range(members)])  24.8 us
    convert_element_type x16, other arithmetic, step(): sum([k[half:].astype(F32) for k in kept[1:]], kept[0][half:].astype(F32))  24.2 us
    unnamed x174, local copies, waits for them, and re-layouts  16.4 us
  transfers between devices with their start and end apart: 83, of which 39 were waited for; matrix products, arithmetic and copies ran while one was open for 9% of the time, Pallas kernels for 29%

profile of v2, /device:TPU:0, one launch (start us, length us, event | category | flops | bytes accessed | tf_op | source)
XLA Modules:
  0.0 476.3 jit_solution(6879309889657152722)
XLA Ops:
  12.7 4.1 collective-permute-start
  19.0 1.8 collective-permute-start.1
  21.1 2.6 collective-permute-start.13
  28.0 3.1 collective-permute-done.8
  33.9 1.8 collective-permute-start.19
  39.3 4.6 collective-permute-start.20
  43.9 1.8 collective-permute-start.3
  45.8 12.7 %collective-permute-done.20 = bf16[4,64,512]{2,1,0:T(8,128)(2,1)S(1)} collective-permute-done((bf16[4,64,512]{2,1,0:T(8,128)(2,1)S(1)}, bf16[4,64,512]{2,1,0:T(8,128)(2,1)S(1)}, u32[]{:S(2)}, u32[]{:S(2)}) %collective-permute-start.20) | collective-permute-done | bytes 262176 | tf_op jit(solution)/shard_map/ppermute | solution.py:1189
  58.5 2.2 collective-permute-start.21
  61.8 2.0 collective-permute-done.10
  65.5 12.2 %collective-permute-done.21 = bf16[8,64,512]{2,1,0:T(8,128)(2,1)S(1)} collective-permute-done((bf16[8,64,512]{2,1,0:T(8,128)(2,1)S(1)}, bf16[8,64,512]{2,1,0:T(8,128)(2,1)S(1)}, u32[]{:S(2)}, u32[]{:S(2)}) %collective-permute-start.21) | collective-permute-done | bytes 524320 | tf_op jit(solution)/shard_map/ppermute | solution.py:1189
  80.5 7.4 %shard_map.544 = (bf16[1920,1024]{1,0:T(8,128)(2,1)}, f32[480,128]{1,0:T(8,128)}, f32[5,3]{1,0:T(8,128)}) custom-call(s32[2]{0:T(128)} %pad_add_fusion.spot, s32[128]{0:T(128)} %la.1, s32[64]{0:T(128)} %lb.1, s32[64]{0:T(128)} %lc.1, bf16[10,10,4,1024]{3,2,1,0:T(4,128)(2,1)} %bitcast.107, bf16[18,18,2,1024]{3,2,1,0:T(2,128)(2,1)} %bitcast.106, ...), custom_call_target="tpu_custom_call" | custom-call | tf_op jit(solution)/shard_map/pallas_call | solution.py:76
  87.9 8.3 %shard_map.545 = (f32[1920,512]{1,0:T(8,128)}, f32[8,512]{1,0:T(8,128)}) custom-call(s32[1]{0:T(128)} %bitcast.5.ids, f32[5,3]{1,0:T(8,128)} %get-tuple-element.145.sc, bf16[1920,1024]{1,0:T(8,128)(2,1)} %get-tuple-element.146.xp.rest_3_.rest_0_, f32[480,128]{1,0:T(8,128)} %get-tuple-element.234.msk, bf16[16,32,512]{2,1,0:T(8,128)(2,1)} %copy-done.10, ...), custom_call_target="tpu_custom_call" | custom-call | flops 2013265920 | tf_op jit(solution)/shard_map/pallas_call | solution.py:76
  98.2 1.8 collective-permute-done.7.rest_3_
  103.1 11.2 %shard_map.546 = (bf16[1920,512]{1,0:T(8,128)(2,1)}, f32[8,512]{1,0:T(8,128)}, f32[480,512]{1,0:T(8,128)}, f32[8,512]{1,0:T(8,128)}, f32[32,512]{1,0:T(8,128)}) custom-call(s32[1]{0:T(128)} %bitcast.5.ids, f32[5,3]{1,0:T(8,128)} %get-tuple-element.145.sc, f32[1920,512]{1,0:T(8,128)} %get-tuple-element.148.c1, f32[480,128]{1,0:T(8,128)} %get-tuple-element.234.msk, ...), custom_call_target="tpu_custom_call" | custom-call | flops 2264924160 | tf_op jit(solution)/shard_map/pallas_call | solution.py:76
  114.4 2.2 collective-permute-start.24
  116.5 14.1 %collective-permute-done.24 = bf16[2,144,512]{2,1,0:T(8,128)(2,1)S(1)} collective-permute-done((bf16[2,144,512]{2,1,0:T(8,128)(2,1)S(1)}, bf16[2,144,512]{2,1,0:T(8,128)(2,1)S(1)}, u32[]{:S(2)}, u32[]{:S(2)}) %collective-permute-start.24) | collective-permute-done | bytes 294944 | tf_op jit(solution)/shard_map/ppermute | solution.py:1189
  130.8 9.5 %shard_map.547 = (f32[480,2048]{1,0:T(8,128)}, f32[8,2048]{1,0:T(8,128)}) custom-call(s32[1]{0:T(128)} %constant.22.clone.1.ids.ids_s, f32[5,3]{1,0:T(8,128)} %get-tuple-element.145.sc, bf16[1920,1024]{1,0:T(8,128)(2,1)} %get-tuple-element.146.xp.rest_3_.rest_0_, f32[480,128]{1,0:T(8,128)} %get-tuple-element.234.msk, bf16[32,320,512]{2,1,0:T(8,128)(2,1)} %bitcast.93), custom_call_target="tpu_custom_call" | custom-call | flops 2013265920 | tf_op jit(solution)/shard_map/pallas_call | solution.py:76
  140.3 5.2 %collective-permute-done.25 = bf16[4,144,512]{2,1,0:T(8,128)(2,1)S(1)} collective-permute-done((bf16[4,144,512]{2,1,0:T(8,128)(2,1)S(1)}, bf16[4,144,512]{2,1,0:T(8,128)(2,1)S(1)}, u32[]{:S(2)}, u32[]{:S(2)}) %collective-permute-start.25) | collective-permute-done | bytes 589856 | tf_op jit(solution)/shard_map/ppermute | solution.py:1189
  152.3 7.1 %shard_map.548 = (bf16[480,512]{1,0:T(8,128)(2,1)}, f32[8,512]{1,0:T(8,128)}, f32[480,2048]{1,0:T(8,128)}, f32[16,2048]{1,0:T(8,128)}) custom-call(s32[1]{0:T(128)} %constant.22.clone.1.ids.ids_s, f32[5,3]{1,0:T(8,128)} %get-tuple-element.145.sc, f32[480,512]{1,0:T(8,128)} %get-tuple-element.154.c.c2, f32[32,512]{1,0:T(8,128)} %get-tuple-element.155.normp, ...), custom_call_target="tpu_custom_call" | custom-call | flops 1006632960 | tf_op jit(solution)/shard_map/pallas_call | solution.py:76
  164.5 3.8 collective-permute-done.30.rest_2_
  169.0 10.1 %shard_map.549 = (f32[480,2048]{1,0:T(8,128)}, bf16[480,2048]{1,0:T(8,128)(2,1)}, f32[8,2048]{1,0:T(8,128)}, f32[8,2048]{1,0:T(8,128)}, f32[480,512]{1,0:T(8,128)}, /*index=5*/f32[8,512]{1,0:T(8,128)}) custom-call(s32[1]{0:T(128)} %constant.22.clone.1.ids.ids_s, f32[5,3]{1,0:T(8,128)} %get-tuple-element.145.sc, f32[480,2048]{1,0:T(8,128)} %get-tuple-element.169.c3.c3_far, ...), custom_call_target="tpu_custom_call" | custom-call | flops 1006632960 | tf_op jit(solution)/shard_map/pallas_call | solution.py:76
  183.0 1.8 collective-permute-done.33.rest_2_
  186.2 7.6 %shard_map.550 = (bf16[480,512]{1,0:T(8,128)(2,1)}, f32[8,512]{1,0:T(8,128)}, f32[480,512]{1,0:T(8,128)}, f32[8,512]{1,0:T(8,128)}) custom-call(s32[1]{0:T(128)} %bitcast.5.ids, f32[5,3]{1,0:T(8,128)} %get-tuple-element.145.sc, f32[480,512]{1,0:T(8,128)} %get-tuple-element.172.c4, f32[32,512]{1,0:T(8,128)} %get-tuple-element.155.normp, ...), custom_call_target="tpu_custom_call" | custom-call | flops 2264924160 | tf_op jit(solution)/shard_map/pallas_call | solution.py:76
  198.8 7.1 %shard_map.551 = (bf16[480,512]{1,0:T(8,128)(2,1)}, f32[8,512]{1,0:T(8,128)}, f32[480,2048]{1,0:T(8,128)}, f32[8,2048]{1,0:T(8,128)}) custom-call(s32[1]{0:T(128)} %constant.22.clone.1.ids.ids_s, f32[5,3]{1,0:T(8,128)} %get-tuple-element.145.sc, f32[480,512]{1,0:T(8,128)} %get-tuple-element.175.c.c5, f32[32,512]{1,0:T(8,128)} %get-tuple-element.155.normp, ...), custom_call_target="tpu_custom_call" | custom-call | flops 1006632960 | tf_op jit(solution)/shard_map/pallas_call | solution.py:76
  207.8 2.2 collective-permute-done.42.rest_3_
  212.0 10.1 %shard_map.552 = (bf16[5,5,4,2048]{3,2,1,0:T(4,128)(2,1)}, bf16[9,9,2,2048]{3,2,1,0:T(2,128)(2,1)}, bf16[7,7,2,2048]{3,2,1,0:T(2,128)(2,1)}, f32[480,2048]{1,0:T...) custom-call(f32[5,3]{1,0:T(8,128)} %get-tuple-element.145.sc, f32[480,2048]{1,0:T(8,128)} %get-tuple-element.177.c6, ...), custom_call_target="tpu_custom_call" | custom-call | tf_op jit(solution)/shard_map/pallas_call | solution.py:76
  224.0 2.5 collective-permute-done.45.rest_3_
  226.5 1.6 collective-permute-done.44.rest_2_
  228.8 8.6 %shard_map.553 = (bf16[480,2048]{1,0:T(8,128)(2,1)}, f32[480,512]{1,0:T(8,128)}, f32[8,512]{1,0:T(8,128)}) custom-call(s32[1]{0:T(128)} %constant.22.clone.1.ids.ids_s, f32[5,3]{1,0:T(8,128)} %get-tuple-element.145.sc, f32[480,2048]{1,0:T(8,128)} %get-tuple-element.183.dz.dz6_far, f32[480,2048]{1,0:T(8,128)} %get-tuple-element.177.c6, ...), custom_call_target="tpu_custom_call" | custom-call | flops 1006632960 | tf_op jit(solution)/shard_map/pallas_call | solution.py:76
  239.3 4.3 shard_map.554.rest_2_
  244.3 8.5 %shard_map.555 = (bf16[480,512]{1,0:T(8,128)(2,1)}, f32[480,512]{1,0:T(8,128)}, f32[8,512]{1,0:T(8,128)}) custom-call(s32[1]{0:T(128)} %bitcast.5.ids, f32[5,3]{1,0:T(8,128)} %get-tuple-element.145.sc, f32[480,512]{1,0:T(8,128)} %get-tuple-element.187.dz5, f32[480,512]{1,0:T(8,128)} %get-tuple-element.175.c.c5, f32[8,512]{1,0:T(8,128)} %get-tuple-element.185.nrm5, ...), custom_call_target="tpu_custom_call" | custom-call | flops 2264924160 | tf_op jit(solution)/shard_map/pallas_call | solution.py:76
  252.7 6.1 %shard_map.556 = bf16[32,208,512]{2,1,0:T(8,128)(2,1)} custom-call(s32[1]{0:T(128)} %constant.22.clone.1.ids.ids_s, bf16[480,512]{1,0:T(8,128)(2,1)} %get-tuple-element.197.rest_0_, bf16[480,512]{1,0:T(8,128)(2,1)} %get-tuple-element.198.rest_1_, bf16[32,208,512]{2,1,0:T(8,128)(2,1)} %shard_map.554.rest_2_), custom_call_target="tpu_custom_call", output_to_operand_aliasing={{}: (3, {})} | custom-call | flops 2264924160 | tf_op jit(solution)/shard_map/pallas_call | solution.py:76
  264.9 12.7 %shard_map.557 = (bf16[480,512]{1,0:T(8,128)(2,1)}, f32[480,2048]{1,0:T(8,128)}, f32[16,2048]{1,0:T(8,128)}) custom-call(s32[1]{0:T(128)} %constant.22.clone.1.ids.ids_s, f32[5,3]{1,0:T(8,128)} %get-tuple-element.145.sc, f32[480,512]{1,0:T(8,128)} %get-tuple-element.194.dz4, f32[480,512]{1,0:T(8,128)} %get-tuple-element.172.c4, ...), custom_call_target="tpu_custom_call" | custom-call | flops 1006632960 | tf_op jit(solution)/shard_map/pallas_call | solution.py:76
  279.6 4.4 shard_map.558
  284.0 1.7 collective-permute-done.54.rest_3_
  285.7 3.7 collective-permute-done.53.rest_2_
  290.1 10.6 %shard_map.559 = (bf16[480,2048]{1,0:T(8,128)(2,1)}, bf16[480,2048]{1,0:T(8,128)(2,1)}, f32[480,512]{1,0:T(8,128)}, f32[8,512]{1,0:T(8,128)}) custom-call(s32[1]{0:T(128)} %constant.22.clone.1.ids.ids_s, f32[5,3]{1,0:T(8,128)} %get-tuple-element.145.sc, f32[480,2048]{1,0:T(8,128)} %get-tuple-element.202.dz3, f32[480,2048]{1,0:T(8,128)} %get-tuple-element.169.c3.c3_far, ...), custom_call_target="tpu_custom_call" | custom-call | flops 1006632960 | tf_op jit(solution)/shard_map/pallas_call | solution.py:76
  300.7 8.4 %shard_map.560 = (bf16[16,128,512]{2,1,0:T(8,128)(2,1)}, bf16[16,128,512]{2,1,0:T(8,128)(2,1)}, bf16[16,128,512]{2,1,0:T(8,128)(2,1)}, bf16[16,128,512]{2,1,0:T(8,128)(2,1)}) custom-call(s32[1]{0:T(128)} %bitcast.5.ids, bf16[480,512]{1,0:T(8,128)(2,1)} %get-tuple-element.212.rest_0_, ...), custom_call_target="tpu_custom_call", output_to_operand_aliasing={{0}: (5, {}), {1}: (6, {}), {2}: (7, {}), {3}: (8, {})} | custom-call | flops 3019898880 | tf_op jit(solution)/shard_map/pallas_call | solution.py:76
  309.9 2.2 collective-permute-start.59
  313.6 2.7 collective-permute-done.58.rest_2_
  316.8 12.0 %shard_map.561 = (bf16[480,512]{1,0:T(8,128)(2,1)}, f32[1920,512]{1,0:T(8,128)}, f32[8,512]{1,0:T(8,128)}) custom-call(s32[1]{0:T(128)} %bitcast.5.ids, f32[5,3]{1,0:T(8,128)} %get-tuple-element.145.sc, f32[480,512]{1,0:T(8,128)} %get-tuple-element.222.dz2, f32[480,512]{1,0:T(8,128)} %get-tuple-element.154.c.c2, f32[8,512]{1,0:T(8,128)} %get-tuple-element.209.nrm2, ...), custom_call_target="tpu_custom_call" | custom-call | flops 2264924160 | tf_op jit(solution)/shard_map/pallas_call | solution.py:76
  328.9 2.7 add_convert_fusion.2
  331.5 2.5 add_convert_fusion.1
  334.0 6.6 %shard_map.562 = (bf16[16,144,512]{2,1,0:T(8,128)(2,1)}, bf16[16,144,512]{2,1,0:T(8,128)(2,1)}) custom-call(s32[1]{0:T(128)} %bitcast.5.ids, bf16[1920,512]{1,0:T(8,128)(2,1)} %get-tuple-element.229.rest_0_, bf16[480,512]{1,0:T(8,128)(2,1)} %get-tuple-element.230.rest_1_), custom_call_target="tpu_custom_call" | custom-call | flops 2264924160 | tf_op jit(solution)/shard_map/pallas_call | solution.py:76
  340.9 1.8 collective-permute-start.61
  345.4 1.8 collective-permute-done.65.rest_3_
  349.0 6.2 %shard_map.563.rest_1_.dc1 = bf16[1920,512]{1,0:T(8,128)(2,1)} custom-call(f32[5,3]{1,0:T(8,128)} %get-tuple-element.145.sc, f32[1920,512]{1,0:T(8,128)} %get-tuple-element.233.dz1, f32[1920,512]{1,0:T(8,128)} %get-tuple-element.148.c1, f32[8,512]{1,0:T(8,128)} %get-tuple-element.224.nrm1, f32[32,512]{1,0:T(8,128)} %get-tuple-element.155.normp, ...), custom_call_target="tpu_custom_call" | custom-call | tf_op jit(solution)/shard_map/pallas_call | solution.py:76
  355.1 2.0 add_convert_fusion
  357.1 16.4 %collective-permute-done.61 = bf16[8,128,512]{2,1,0:T(8,128)(2,1)} collective-permute-done((bf16[8,128,512]{2,1,0:T(8,128)(2,1)}, bf16[8,128,512]{2,1,0:T(8,128)(2,1)}, u32[]{:S(2)}, u32[]{:S(2)}) %collective-permute-start.61) | collective-permute-done | bytes 1048608 | tf_op jit(solution)/shard_map/ppermute | solution.py:1189
  373.5 2.2 add_convert_fusion.5
  375.8 2.2 add_convert_fusion.4
  378.0 6.3 %shard_map.564 = (bf16[16,48,512]{2,1,0:T(8,128)(2,1)}, bf16[16,48,512]{2,1,0:T(8,128)(2,1)}) custom-call(s32[1]{0:T(128)} %bitcast.5.ids, bf16[1920,1024]{1,0:T(8,128)(2,1)} %get-tuple-element.146.xp.rest_3_.rest_0_, bf16[1920,512]{1,0:T(8,128)(2,1)} %shard_map.563.rest_1_.dc1, f32[8,512]{1,0:T(8,128)} %get-tuple-element.225.rest_0_.rest_2_, ...), custom_call_target="tpu_custom_call" | custom-call | flops 754974720 | tf_op jit(solution)/shard_map/pallas_call | solution.py:76
  386.1 4.9 %collective-permute-start.70 = (bf16[4,128,512]{2,1,0:T(8,128)(2,1)}, bf16[4,128,512]{2,1,0:T(8,128)(2,1)}, u32[]{:S(2)}, u32[]{:S(2)}) collective-permute-start(bf16[4,128,512]{2,1,0:T(8,128)(2,1)} %add_convert_fusion.5), channel_id=1, source_target_pairs={{0,8},{1,9},{2,10},{3,11},{4,12},{5,13},{6,14},{7,15},{8,0},{9,1},... | collective-permute-start | bytes 1572872 | tf_op jit(solution)/shard_map/ppermute | solution.py:1189
  391.0 10.8 %shard_map.565 = (bf16[10,10,4,1024]{3,2,1,0:T(4,128)(2,1)}, bf16[18,18,2,1024]{3,2,1,0:T(2,128)(2,1)}, bf16[14,14,2,1024]{3,2,1,0:T(2,128)(2,1)}) custom-call(s32[1]{0:T(128)} %bitcast.5.ids, s32[1]{0:T(128)} %constant.22.clone.1.ids.ids_s, bf16[1920,512]{1,0:T(8,128)(2,1)} %shard_map.563.rest_1_.dc1, bf16[480,2048]{1,0:T(8,128)(2,1)} %get-tuple-element.214.rest_2_.dcs, ...), custom_call_target="tpu_custom_call" | custom-call | flops 4026531840 | tf_op jit(solution)/shard_map/pallas_call | solution.py:76
  403.3 3.6 collective-permute-done.70
  409.9 12.9 %collective-permute-done.68 = bf16[8,144,512]{2,1,0:T(8,128)(2,1)} collective-permute-done((bf16[8,144,512]{2,1,0:T(8,128)(2,1)S(1)}, bf16[8,144,512]{2,1,0:T(8,128)(2,1)}, u32[]{:S(2)}, u32[]{:S(2)}) %collective-permute-start.68) | collective-permute-done | bytes 1179680 | tf_op jit(solution)/shard_map/ppermute | solution.py:1189
  426.6 1.7 collective-permute-done.73
  429.5 9.8 %collective-permute-done.72 = bf16[4,144,512]{2,1,0:T(8,128)(2,1)S(1)} collective-permute-done((bf16[4,144,512]{2,1,0:T(8,128)(2,1)S(1)}, bf16[4,144,512]{2,1,0:T(8,128)(2,1)S(1)}, u32[]{:S(2)}, u32[]{:S(2)}) %collective-permute-start.72) | collective-permute-done | bytes 589856 | tf_op jit(solution)/shard_map/ppermute | solution.py:1189
  441.9 2.6 collective-permute-start.79
  445.5 1.8 collective-permute-start.75
  447.3 3.7 collective-permute-done.76
  453.1 3.0 collective-permute-start.77
  464.2 2.2 multiply_subtract_fusion.1
  (363 shorter events, 105.1 us)
Async XLA Ops:
  7.2 123.6 %all-gather.2.cloned.1.call-start = ((), (), s32[]{:S(2)}) async-start(), calls=%async_computation.1 | async-start | bytes 10813440 | tf_op jit(solution)/shard_map/all_gather | solution.py:1177
  12.6 453.8 %reduce-scatter.2.cloned.1.call-start = ((), (), s32[]{:S(2)}) async-start(), calls=%async_computation.2 | async-start | bytes 7028736 | tf_op jit(solution)/shard_map/reduce_scatter | solution.py:1285
  12.7 6.3 %collective-permute-start = (bf16[1,32,512]{2,1,0:T(8,128)(2,1)S(1)}, bf16[1,32,512]{2,1,0:T(8,128)(2,1)S(1)}, u32[]{:S(2)}, u32[]{:S(2)}) collective-permute-start(bf16[1,32,512]{2,1,0:T(8,128)(2,1)S(1)} %bitcast.110), channel_id=1, source_target_pairs={{0,16},{1,17},{2,18},{3,19},{4,20},{5,21},{6,22},{7,23},{8,24},{9,... | collective-permute-start | bytes 98312 | tf_op jit(solution)/shard_map/ppermute | solution.py:1189
  19.0 14.2 %collective-permute-start.1 = (bf16[2,32,512]{2,1,0:T(8,128)(2,1)S(1)}, bf16[2,32,512]{2,1,0:T(8,128)(2,1)S(1)}, u32[]{:S(2)}, u32[]{:S(2)}) collective-permute-start(bf16[2,32,512]{2,1,0:T(8,128)(2,1)S(1)} %pad_maximum_fusion.16), channel_id=1, source_target_pairs={{0,4},{1,5},{2,6},{3,7},{4,0},{5,1},{6,2},{7,3},{8,12},{9,13},{10,... | collective-permute-start | bytes 196616 | tf_op jit(solution)/shard_map/ppermute | solution.py:1189
  20.8 13.1 %collective-permute-start.18 = (bf16[1,64,512]{2,1,0:T(8,128)(2,1)S(1)}, bf16[1,64,512]{2,1,0:T(8,128)(2,1)S(1)}, u32[]{:S(2)}, u32[]{:S(2)}) collective-permute-start(bf16[1,64,512]{2,1,0:T(8,128)(2,1)S(1)} %slice_bitcast_fusion.10), channel_id=1, source_target_pairs={{0,4},{1,5},{2,6},{3,7},{4,0},{5,1},{6,2},{7,3},{8,12},{9,13},{10,... | collective-permute-start | bytes 196616 | tf_op jit(solution)/shard_map/ppermute | solution.py:1189
  21.1 5.2 %collective-permute-start.13 = (bf16[1,48,512]{2,1,0:T(8,128)(2,1)S(1)}, bf16[1,48,512]{2,1,0:T(8,128)(2,1)S(1)}, u32[]{:S(2)}, u32[]{:S(2)}) collective-permute-start(bf16[1,48,512]{2,1,0:T(8,128)(2,1)S(1)} %get-tuple-element.294), channel_id=1, source_target_pairs={{0,16},{1,17},{2,18},{3,19},{4,20},{5,21},{6,22},{7,23},{8,24},{9,... | collective-permute-start | bytes 147464 | tf_op jit(solution)/shard_map/ppermute | solution.py:1189
  23.8 7.4 %collective-permute-start.8 = (bf16[1,48,512]{2,1,0:T(8,128)(2,1)S(1)}, bf16[1,48,512]{2,1,0:T(8,128)(2,1)S(1)}, u32[]{:S(2)}, u32[]{:S(2)}) collective-permute-start(bf16[1,48,512]{2,1,0:T(8,128)(2,1)S(1)} %get-tuple-element.295), channel_id=1, source_target_pairs={{0,16},{1,17},{2,18},{3,19},{4,20},{5,21},{6,22},{7,23},{8,24},{9,... | collective-permute-start | bytes 147464 | tf_op jit(solution)/shard_map/ppermute | solution.py:1189
  26.3 9.3 %collective-permute-start.14 = (bf16[2,48,512]{2,1,0:T(8,128)(2,1)S(1)}, bf16[2,48,512]{2,1,0:T(8,128)(2,1)S(1)}, u32[]{:S(2)}, u32[]{:S(2)}) collective-permute-start(bf16[2,48,512]{2,1,0:T(8,128)(2,1)S(1)} %pad_maximum_fusion.15), channel_id=1, source_target_pairs={{0,2},{1,3},{2,0},{3,1},{4,6},{5,7},{6,4},{7,5},{8,10},{9,11},{10,... | collective-permute-start | bytes 294920 | tf_op jit(solution)/shard_map/ppermute | solution.py:1189
  31.1 5.7 %collective-permute-start.9 = (bf16[2,48,512]{2,1,0:T(8,128)(2,1)S(1)}, bf16[2,48,512]{2,1,0:T(8,128)(2,1)S(1)}, u32[]{:S(2)}, u32[]{:S(2)}) collective-permute-start(bf16[2,48,512]{2,1,0:T(8,128)(2,1)S(1)} %pad_maximum_fusion.14), channel_id=1, source_target_pairs={{0,4},{1,5},{2,6},{3,7},{4,0},{5,1},{6,2},{7,3},{8,12},{9,13},{10,... | collective-permute-start | bytes 294920 | tf_op jit(solution)/shard_map/ppermute | solution.py:1189
  33.2 10.7 %collective-permute-start.2 = (bf16[4,32,512]{2,1,0:T(8,128)(2,1)S(1)}, bf16[4,32,512]{2,1,0:T(8,128)(2,1)S(1)}, u32[]{:S(2)}, u32[]{:S(2)}) collective-permute-start(bf16[4,32,512]{2,1,0:T(8,128)(2,1)S(1)} %pad_maximum_fusion.11), channel_id=1, source_target_pairs={{0,8},{1,9},{2,10},{3,11},{4,12},{5,13},{6,14},{7,15},{8,0},{9,1},... | collective-permute-start | bytes 393224 | tf_op jit(solution)/shard_map/ppermute | solution.py:1189
  33.9 5.4 %collective-permute-start.19 = (bf16[2,64,512]{2,1,0:T(8,128)(2,1)S(1)}, bf16[2,64,512]{2,1,0:T(8,128)(2,1)S(1)}, u32[]{:S(2)}, u32[]{:S(2)}) collective-permute-start(bf16[2,64,512]{2,1,0:T(8,128)(2,1)S(1)} %pad_maximum_fusion.12), channel_id=1, source_target_pairs={{0,2},{1,3},{2,0},{3,1},{4,6},{5,7},{6,4},{7,5},{8,10},{9,11},{10,... | collective-permute-start | bytes 393224 | tf_op jit(solution)/shard_map/ppermute | solution.py:1189
  35.7 25.0 %collective-permute-start.15 = (bf16[4,48,512]{2,1,0:T(8,128)(2,1)S(1)}, bf16[4,48,512]{2,1,0:T(8,128)(2,1)S(1)}, u32[]{:S(2)}, u32[]{:S(2)}) collective-permute-start(bf16[4,48,512]{2,1,0:T(8,128)(2,1)S(1)} %pad_maximum_fusion.9), channel_id=1, source_target_pairs={{0,8},{1,9},{2,10},{3,11},{4,12},{5,13},{6,14},{7,15},{8,0},{9,1},... | collective-permute-start | bytes 589832 | tf_op jit(solution)/shard_map/ppermute | solution.py:1189
  36.9 26.9 %collective-permute-start.10 = (bf16[4,48,512]{2,1,0:T(8,128)(2,1)S(1)}, bf16[4,48,512]{2,1,0:T(8,128)(2,1)S(1)}, u32[]{:S(2)}, u32[]{:S(2)}) collective-permute-start(bf16[4,48,512]{2,1,0:T(8,128)(2,1)S(1)} %pad_maximum_fusion.8), channel_id=1, source_target_pairs={{0,8},{1,9},{2,10},{3,11},{4,12},{5,13},{6,14},{7,15},{8,0},{9,1},... | collective-permute-start | bytes 589832 | tf_op jit(solution)/shard_map/ppermute | solution.py:1189
  39.3 19.2 %collective-permute-start.20 = (bf16[4,64,512]{2,1,0:T(8,128)(2,1)S(1)}, bf16[4,64,512]{2,1,0:T(8,128)(2,1)S(1)}, u32[]{:S(2)}, u32[]{:S(2)}) collective-permute-start(bf16[4,64,512]{2,1,0:T(8,128)(2,1)S(1)} %pad_maximum_fusion.7), channel_id=1, source_target_pairs={{0,16},{1,17},{2,18},{3,19},{4,20},{5,21},{6,22},{7,23},{8,24},{9,... | collective-permute-start | bytes 786440 | tf_op jit(solution)/shard_map/ppermute | solution.py:1189
  43.9 35.5 %collective-permute-start.3 = (bf16[8,32,512]{2,1,0:T(8,128)(2,1)S(1)}, bf16[8,32,512]{2,1,0:T(8,128)(2,1)S(1)}, u32[]{:S(2)}, u32[]{:S(2)}) collective-permute-start(bf16[8,32,512]{2,1,0:T(8,128)(2,1)S(1)} %pad_maximum_fusion.6), channel_id=1, source_target_pairs={{0,2},{1,3},{2,0},{3,1},{4,6},{5,7},{6,4},{7,5},{8,10},{9,11},{10,... | collective-permute-start | bytes 786440 | tf_op jit(solution)/shard_map/ppermute | solution.py:1189
  58.5 19.2 %collective-permute-start.21 = (bf16[8,64,512]{2,1,0:T(8,128)(2,1)S(1)}, bf16[8,64,512]{2,1,0:T(8,128)(2,1)S(1)}, u32[]{:S(2)}, u32[]{:S(2)}) collective-permute-start(bf16[8,64,512]{2,1,0:T(8,128)(2,1)S(1)} %pad_maximum_fusion.2), channel_id=1, source_target_pairs={{0,8},{1,9},{2,10},{3,11},{4,12},{5,13},{6,14},{7,15},{8,0},{9,1},... | collective-permute-start | bytes 1572872 | tf_op jit(solution)/shard_map/ppermute | solution.py:1189
  60.7 17.7 %collective-permute-start.16 = (bf16[8,48,512]{2,1,0:T(8,128)(2,1)S(1)}, bf16[8,48,512]{2,1,0:T(8,128)(2,1)S(1)}, u32[]{:S(2)}, u32[]{:S(2)}) collective-permute-start(bf16[8,48,512]{2,1,0:T(8,128)(2,1)S(1)} %pad_maximum_fusion.4), channel_id=1, source_target_pairs={{0,4},{1,5},{2,6},{3,7},{4,0},{5,1},{6,2},{7,3},{8,12},{9,13},{10,... | collective-permute-start | bytes 1179656 | tf_op jit(solution)/shard_map/ppermute | solution.py:1189
  63.8 14.0 %collective-permute-start.11 = (bf16[8,48,512]{2,1,0:T(8,128)(2,1)S(1)}, bf16[8,48,512]{2,1,0:T(8,128)(2,1)S(1)}, u32[]{:S(2)}, u32[]{:S(2)}) collective-permute-start(bf16[8,48,512]{2,1,0:T(8,128)(2,1)S(1)} %pad_maximum_fusion.3), channel_id=1, source_target_pairs={{0,2},{1,3},{2,0},{3,1},{4,6},{5,7},{6,4},{7,5},{8,10},{9,11},{10,... | collective-permute-start | bytes 1179656 | tf_op jit(solution)/shard_map/ppermute | solution.py:1189
  77.8 24.4 %collective-permute-start.22 = (bf16[16,64,512]{2,1,0:T(8,128)(2,1)S(1)}, bf16[16,64,512]{2,1,0:T(8,128)(2,1)S(1)}, u32[]{:S(2)}, u32[]{:S(2)}) collective-permute-start(bf16[16,64,512]{2,1,0:T(8,128)(2,1)S(1)} %constant_dynamic-update-slice_fusion.15.rest_8_), channel_id=1, source_target_pairs={{0,1},{1,0},{2,3},{3,2},{4,5},{5,4},{6,7},{7,6},{8,9},{9,8},{10,11... | collective-permute-start | bytes 3145736 | tf_op jit(solution)/shard_map/ppermute | solution.py:1189
  77.9 24.2 %collective-permute-start.12 = (bf16[16,48,512]{2,1,0:T(8,128)(2,1)S(1)}, bf16[16,48,512]{2,1,0:T(8,128)(2,1)}, u32[]{:S(2)}, u32[]{:S(2)}) collective-permute-start(bf16[16,48,512]{2,1,0:T(8,128)(2,1)S(1)} %constant_dynamic-update-slice_fusion.5.rest_4_), channel_id=1, source_target_pairs={{0,1},{1,0},{2,3},{3,2},{4,5},{5,4},{6,7},{7,6},{8,9},{9,8},{10,11... | collective-permute-start | bytes 2359304 | tf_op jit(solution)/shard_map/ppermute | solution.py:1189
  79.3 22.9 %collective-permute-start.17 = (bf16[16,48,512]{2,1,0:T(8,128)(2,1)}, bf16[16,48,512]{2,1,0:T(8,128)(2,1)}, u32[]{:S(2)}, u32[]{:S(2)}) collective-permute-start(bf16[16,48,512]{2,1,0:T(8,128)(2,1)} %constant_dynamic-update-slice_fusion.10.rest_6_), channel_id=1, source_target_pairs={{0,1},{1,0},{2,3},{3,2},{4,5},{5,4},{6,7},{7,6},{8,9},{9,8},{10,11... | collective-permute-start | bytes 2359304 | tf_op jit(solution)/shard_map/ppermute | solution.py:1189
  79.5 8.4 %collective-permute-start.4 = (bf16[16,32,512]{2,1,0:T(8,128)(2,1)S(1)}, bf16[16,32,512]{2,1,0:T(8,128)(2,1)}, u32[]{:S(2)}, u32[]{:S(2)}) collective-permute-start(bf16[16,32,512]{2,1,0:T(8,128)(2,1)S(1)} %constant_dynamic-update-slice_fusion.rest_0_), channel_id=1, source_target_pairs={{0,1},{1,0},{2,3},{3,2},{4,5},{5,4},{6,7},{7,6},{8,9},{9,8},{10,11... | collective-permute-start | bytes 1572872 | tf_op jit(solution)/shard_map/ppermute | solution.py:1189
  101.8 12.6 %collective-permute-start.23 = (bf16[1,144,512]{2,1,0:T(8,128)(2,1)S(1)}, bf16[1,144,512]{2,1,0:T(8,128)(2,1)S(1)}, u32[]{:S(2)}, u32[]{:S(2)}) collective-permute-start(bf16[1,144,512]{2,1,0:T(8,128)(2,1)S(1)} %bitcast.102), channel_id=1, source_target_pairs={{0,2},{1,3},{2,0},{3,1},{4,6},{5,7},{6,4},{7,5},{8,10},{9,11},{10,... | collective-permute-start | bytes 442376 | tf_op jit(solution)/shard_map/ppermute | solution.py:1189
  114.4 16.3 %collective-permute-start.24 = (bf16[2,144,512]{2,1,0:T(8,128)(2,1)S(1)}, bf16[2,144,512]{2,1,0:T(8,128)(2,1)S(1)}, u32[]{:S(2)}, u32[]{:S(2)}) collective-permute-start(bf16[2,144,512]{2,1,0:T(8,128)(2,1)S(1)} %pad_maximum_fusion.5), channel_id=1, source_target_pairs={{0,16},{1,17},{2,18},{3,19},{4,20},{5,21},{6,22},{7,23},{8,24},{9,... | collective-permute-start | bytes 884744 | tf_op jit(solution)/shard_map/ppermute | solution.py:1189
  130.7 14.8 %collective-permute-start.25 = (bf16[4,144,512]{2,1,0:T(8,128)(2,1)S(1)}, bf16[4,144,512]{2,1,0:T(8,128)(2,1)S(1)}, u32[]{:S(2)}, u32[]{:S(2)}) collective-permute-start(bf16[4,144,512]{2,1,0:T(8,128)(2,1)S(1)} %pad_maximum_fusion.1), channel_id=1, source_target_pairs={{0,8},{1,9},{2,10},{3,11},{4,12},{5,13},{6,14},{7,15},{8,0},{9,1},... | collective-permute-start | bytes 1769480 | tf_op jit(solution)/shard_map/ppermute | solution.py:1189
  145.6 33.5 %collective-permute-start.35 = (bf16[8,144,512]{2,1,0:T(8,128)(2,1)S(1)}, bf16[8,144,512]{2,1,0:T(8,128)(2,1)S(1)}, u32[]{:S(2)}, u32[]{:S(2)}) collective-permute-start(bf16[8,144,512]{2,1,0:T(8,128)(2,1)S(1)} %pad_maximum_fusion), channel_id=1, source_target_pairs={{0,4},{1,5},{2,6},{3,7},{4,0},{5,1},{6,2},{7,3},{8,12},{9,13},{10,... | collective-permute-start | bytes 3538952 | tf_op jit(solution)/shard_map/ppermute | solution.py:1189
  159.4 5.1 %collective-permute-start.31 = (f32[16,2048]{1,0:T(8,128)}, f32[16,2048]{1,0:T(8,128)S(1)}, u32[]{:S(2)}, u32[]{:S(2)}) collective-permute-start(f32[16,2048]{1,0:T(8,128)} %get-tuple-element.171.rest_0_), channel_id=1, source_target_pairs={{0,3},{1,2},{2,1},{3,0},{4,7},{5,6},{6,5},{7,4},{8,11},{9,10},{10,... | collective-permute-start | bytes 393224 | tf_op jit(solution)/shard_map/ppermute | solution.py:1193
  160.4 7.9 %collective-permute-start.30 = (f32[16,2048]{1,0:T(8,128)}, f32[16,2048]{1,0:T(8,128)S(1)}, u32[]{:S(2)}, u32[]{:S(2)}) collective-permute-start(f32[16,2048]{1,0:T(8,128)} %get-tuple-element.171.rest_0_), channel_id=1, source_target_pairs={{0,2},{1,3},{2,0},{3,1},{4,6},{5,7},{6,4},{7,5},{8,10},{9,11},{10,... | collective-permute-start | bytes 393224 | tf_op jit(solution)/shard_map/ppermute | solution.py:1193
  162.0 6.3 %collective-permute-start.29 = (f32[16,2048]{1,0:T(8,128)}, f32[16,2048]{1,0:T(8,128)S(1)}, u32[]{:S(2)}, u32[]{:S(2)}) collective-permute-start(f32[16,2048]{1,0:T(8,128)} %get-tuple-element.171.rest_0_), channel_id=1, source_target_pairs={{0,1},{1,0},{2,3},{3,2},{4,5},{5,4},{6,7},{7,6},{8,9},{9,8},{10,11... | collective-permute-start | bytes 393224 | tf_op jit(solution)/shard_map/ppermute | solution.py:1193
  179.2 5.5 %collective-permute-start.36 = (bf16[16,144,512]{2,1,0:T(8,128)(2,1)S(1)}, bf16[16,144,512]{2,1,0:T(8,128)(2,1)S(1)}, u32[]{:S(2)}, u32[]{:S(2)}) collective-permute-start(bf16[16,144,512]{2,1,0:T(8,128)(2,1)S(1)} %constant_dynamic-update-slice_fusion.20.rest_4_), channel_id=1, source_target_pairs={{0,1},{1,0},{2,3},{3,2},{4,5},{5,4},{6,7},{7,6},{8,9},{9,8},{10,11... | collective-permute-start | bytes 7077896 | tf_op jit(solution)/shard_map/ppermute | solution.py:1189
  205.9 4.1 collective-permute-start.42
  206.2 5.1 %collective-permute-start.41 = (f32[8,2048]{1,0:T(8,128)}, f32[8,2048]{1,0:T(8,128)S(1)}, u32[]{:S(2)}, u32[]{:S(2)}) collective-permute-start(f32[8,2048]{1,0:T(8,128)} %get-tuple-element.179.rest_0_), channel_id=1, source_target_pairs={{0,2},{1,3},{2,0},{3,1},{4,6},{5,7},{6,4},{7,5},{8,10},{9,11},{10,... | collective-permute-start | bytes 196616 | tf_op jit(solution)/shard_map/ppermute | solution.py:1193
  206.8 4.6 collective-permute-start.40
  222.1 4.4 collective-permute-start.45
  222.8 5.4 %collective-permute-start.44 = (f32[8,2048]{1,0:T(8,128)}, f32[8,2048]{1,0:T(8,128)S(1)}, u32[]{:S(2)}, u32[]{:S(2)}) collective-permute-start(f32[8,2048]{1,0:T(8,128)} %get-tuple-element.186.rest_0_.rest_7_), channel_id=1, source_target_pairs={{0,2},{1,3},{2,0},{3,1},{4,6},{5,7},{6,4},{7,5},{8,10},{9,11},{10,... | collective-permute-start | bytes 196616 | tf_op jit(solution)/shard_map/ppermute | solution.py:1193
  223.9 4.3 collective-permute-start.43
  237.4 6.2 %collective-permute-start.48 = (f32[8,512]{1,0:T(8,128)}, f32[8,512]{1,0:T(8,128)S(1)}, u32[]{:S(2)}, u32[]{:S(2)}) collective-permute-start(f32[8,512]{1,0:T(8,128)} %get-tuple-element.188.rest_0_.rest_6_), channel_id=1, source_target_pairs={{0,3},{1,2},{2,1},{3,0},{4,7},{5,6},{6,5},{7,4},{8,11},{9,10},{10,... | collective-permute-start | bytes 49160 | tf_op jit(solution)/shard_map/ppermute | solution.py:1193
  238.2 5.4 %collective-permute-start.47 = (f32[8,512]{1,0:T(8,128)}, f32[8,512]{1,0:T(8,128)S(1)}, u32[]{:S(2)}, u32[]{:S(2)}) collective-permute-start(f32[8,512]{1,0:T(8,128)} %get-tuple-element.188.rest_0_.rest_6_), channel_id=1, source_target_pairs={{0,2},{1,3},{2,0},{3,1},{4,6},{5,7},{6,4},{7,5},{8,10},{9,11},{10,... | collective-permute-start | bytes 49160 | tf_op jit(solution)/shard_map/ppermute | solution.py:1193
  239.0 4.7 collective-permute-start.46
  277.6 8.1 %collective-permute-start.54 = (f32[16,2048]{1,0:T(8,128)}, f32[16,2048]{1,0:T(8,128)S(1)}, u32[]{:S(2)}, u32[]{:S(2)}) collective-permute-start(f32[16,2048]{1,0:T(8,128)} %get-tuple-element.203.rest_0_.rest_4_), channel_id=1, source_target_pairs={{0,3},{1,2},{2,1},{3,0},{4,7},{5,6},{6,5},{7,4},{8,11},{9,10},{10,... | collective-permute-start | bytes 393224 | tf_op jit(solution)/shard_map/ppermute | solution.py:1193
  277.7 11.7 %collective-permute-start.53 = (f32[16,2048]{1,0:T(8,128)}, f32[16,2048]{1,0:T(8,128)S(1)}, u32[]{:S(2)}, u32[]{:S(2)}) collective-permute-start(f32[16,2048]{1,0:T(8,128)} %get-tuple-element.203.rest_0_.rest_4_), channel_id=1, source_target_pairs={{0,2},{1,3},{2,0},{3,1},{4,6},{5,7},{6,4},{7,5},{8,10},{9,11},{10,... | collective-permute-start | bytes 393224 | tf_op jit(solution)/shard_map/ppermute | solution.py:1193
  278.8 10.6 %collective-permute-start.52 = (f32[16,2048]{1,0:T(8,128)}, f32[16,2048]{1,0:T(8,128)S(1)}, u32[]{:S(2)}, u32[]{:S(2)}) collective-permute-start(f32[16,2048]{1,0:T(8,128)} %get-tuple-element.203.rest_0_.rest_4_), channel_id=1, source_target_pairs={{0,1},{1,0},{2,3},{3,2},{4,5},{5,4},{6,7},{7,6},{8,9},{9,8},{10,11... | collective-permute-start | bytes 393224 | tf_op jit(solution)/shard_map/ppermute | solution.py:1193
  309.1 19.7 %collective-permute-start.56 = (bf16[16,128,512]{2,1,0:T(8,128)(2,1)}, bf16[16,128,512]{2,1,0:T(8,128)(2,1)}, u32[]{:S(2)}, u32[]{:S(2)}) collective-permute-start(bf16[16,128,512]{2,1,0:T(8,128)(2,1)} %get-tuple-element.221), channel_id=1, source_target_pairs={{0,1},{1,0},{2,3},{3,2},{4,5},{5,4},{6,7},{7,6},{8,9},{9,8},{10,11... | collective-permute-start | bytes 6291464 | tf_op jit(solution)/shard_map/ppermute | solution.py:1189
  309.8 21.7 %collective-permute-start.55 = (bf16[16,128,512]{2,1,0:T(8,128)(2,1)}, bf16[16,128,512]{2,1,0:T(8,128)(2,1)}, u32[]{:S(2)}, u32[]{:S(2)}) collective-permute-start(bf16[16,128,512]{2,1,0:T(8,128)(2,1)} %get-tuple-element.219), channel_id=1, source_target_pairs={{0,1},{1,0},{2,3},{3,2},{4,5},{5,4},{6,7},{7,6},{8,9},{9,8},{10,11... | collective-permute-start | bytes 6291464 | tf_op jit(solution)/shard_map/ppermute | solution.py:1189
  312.1 4.1 collective-permute-start.58
  312.2 4.1 collective-permute-start.57
  340.6 14.5 %collective-permute-start.62 = (bf16[16,144,512]{2,1,0:T(8,128)(2,1)}, bf16[16,144,512]{2,1,0:T(8,128)(2,1)}, u32[]{:S(2)}, u32[]{:S(2)}) collective-permute-start(bf16[16,144,512]{2,1,0:T(8,128)(2,1)} %get-tuple-element.232), channel_id=1, source_target_pairs={{0,1},{1,0},{2,3},{3,2},{4,5},{5,4},{6,7},{7,6},{8,9},{9,8},{10,11... | collective-permute-start | bytes 7077896 | tf_op jit(solution)/shard_map/ppermute | solution.py:1189
  340.9 32.7 %collective-permute-start.61 = (bf16[8,128,512]{2,1,0:T(8,128)(2,1)}, bf16[8,128,512]{2,1,0:T(8,128)(2,1)}, u32[]{:S(2)}, u32[]{:S(2)}) collective-permute-start(bf16[8,128,512]{2,1,0:T(8,128)(2,1)} %add_convert_fusion.2), channel_id=1, source_target_pairs={{0,4},{1,5},{2,6},{3,7},{4,0},{5,1},{6,2},{7,3},{8,12},{9,13},{10,... | collective-permute-start | bytes 3145736 | tf_op jit(solution)/shard_map/ppermute | solution.py:1189
  342.6 33.1 %collective-permute-start.60 = (bf16[8,128,512]{2,1,0:T(8,128)(2,1)}, bf16[8,128,512]{2,1,0:T(8,128)(2,1)}, u32[]{:S(2)}, u32[]{:S(2)}) collective-permute-start(bf16[8,128,512]{2,1,0:T(8,128)(2,1)} %add_convert_fusion.1), channel_id=1, source_target_pairs={{0,8},{1,9},{2,10},{3,11},{4,12},{5,13},{6,14},{7,15},{8,0},{9,1},... | collective-permute-start | bytes 3145736 | tf_op jit(solution)/shard_map/ppermute | solution.py:1189
  384.3 17.5 %collective-permute-start.66 = (bf16[16,48,512]{2,1,0:T(8,128)(2,1)}, bf16[16,48,512]{2,1,0:T(8,128)(2,1)}, u32[]{:S(2)}, u32[]{:S(2)}) collective-permute-start(bf16[16,48,512]{2,1,0:T(8,128)(2,1)} %get-tuple-element.244), channel_id=1, source_target_pairs={{0,1},{1,0},{2,3},{3,2},{4,5},{5,4},{6,7},{7,6},{8,9},{9,8},{10,11... | collective-permute-start | bytes 2359304 | tf_op jit(solution)/shard_map/ppermute | solution.py:1189
  384.4 38.4 %collective-permute-start.68 = (bf16[8,144,512]{2,1,0:T(8,128)(2,1)S(1)}, bf16[8,144,512]{2,1,0:T(8,128)(2,1)}, u32[]{:S(2)}, u32[]{:S(2)}) collective-permute-start(bf16[8,144,512]{2,1,0:T(8,128)(2,1)S(1)} %add_convert_fusion), channel_id=1, source_target_pairs={{0,2},{1,3},{2,0},{3,1},{4,6},{5,7},{6,4},{7,5},{8,10},{9,11},{10,... | collective-permute-start | bytes 3538952 | tf_op jit(solution)/shard_map/ppermute | solution.py:1189
  384.5 24.1 %collective-permute-start.69 = (bf16[4,128,512]{2,1,0:T(8,128)(2,1)}, bf16[4,128,512]{2,1,0:T(8,128)(2,1)}, u32[]{:S(2)}, u32[]{:S(2)}) collective-permute-start(bf16[4,128,512]{2,1,0:T(8,128)(2,1)} %add_convert_fusion.4), channel_id=1, source_target_pairs={{0,4},{1,5},{2,6},{3,7},{4,0},{5,1},{6,2},{7,3},{8,12},{9,13},{10,... | collective-permute-start | bytes 1572872 | tf_op jit(solution)/shard_map/ppermute | solution.py:1189
  386.1 20.7 %collective-permute-start.70 = (bf16[4,128,512]{2,1,0:T(8,128)(2,1)}, bf16[4,128,512]{2,1,0:T(8,128)(2,1)}, u32[]{:S(2)}, u32[]{:S(2)}) collective-permute-start(bf16[4,128,512]{2,1,0:T(8,128)(2,1)} %add_convert_fusion.5), channel_id=1, source_target_pairs={{0,8},{1,9},{2,10},{3,11},{4,12},{5,13},{6,14},{7,15},{8,0},{9,1},... | collective-permute-start | bytes 1572872 | tf_op jit(solution)/shard_map/ppermute | solution.py:1189
  403.2 21.2 %collective-permute-start.67 = (bf16[8,48,512]{2,1,0:T(8,128)(2,1)S(1)}, bf16[8,48,512]{2,1,0:T(8,128)(2,1)S(1)}, u32[]{:S(2)}, u32[]{:S(2)}) collective-permute-start(bf16[8,48,512]{2,1,0:T(8,128)(2,1)S(1)} %add_convert_fusion.6), channel_id=1, source_target_pairs={{0,8},{1,9},{2,10},{3,11},{4,12},{5,13},{6,14},{7,15},{8,0},{9,1},... | collective-permute-start | bytes 1179656 | tf_op jit(solution)/shard_map/ppermute | solution.py:1189
  408.1 17.4 %collective-permute-start.74 = (bf16[2,128,512]{2,1,0:T(8,128)(2,1)S(1)}, bf16[2,128,512]{2,1,0:T(8,128)(2,1)S(1)}, u32[]{:S(2)}, u32[]{:S(2)}) collective-permute-start(bf16[2,128,512]{2,1,0:T(8,128)(2,1)S(1)} %add_convert_fusion.9), channel_id=1, source_target_pairs={{0,16},{1,17},{2,18},{3,19},{4,20},{5,21},{6,22},{7,23},{8,24},{9,... | collective-permute-start | bytes 786440 | tf_op jit(solution)/shard_map/ppermute | solution.py:1189
  409.8 18.5 %collective-permute-start.73 = (bf16[2,128,512]{2,1,0:T(8,128)(2,1)S(1)}, bf16[2,128,512]{2,1,0:T(8,128)(2,1)S(1)}, u32[]{:S(2)}, u32[]{:S(2)}) collective-permute-start(bf16[2,128,512]{2,1,0:T(8,128)(2,1)S(1)} %add_convert_fusion.8), channel_id=1, source_target_pairs={{0,2},{1,3},{2,0},{3,1},{4,6},{5,7},{6,4},{7,5},{8,10},{9,11},{10,... | collective-permute-start | bytes 786440 | tf_op jit(solution)/shard_map/ppermute | solution.py:1189
  424.3 14.9 %collective-permute-start.72 = (bf16[4,144,512]{2,1,0:T(8,128)(2,1)S(1)}, bf16[4,144,512]{2,1,0:T(8,128)(2,1)S(1)}, u32[]{:S(2)}, u32[]{:S(2)}) collective-permute-start(bf16[4,144,512]{2,1,0:T(8,128)(2,1)S(1)} %add_convert_fusion.3), channel_id=1, source_target_pairs={{0,4},{1,5},{2,6},{3,7},{4,0},{5,1},{6,2},{7,3},{8,12},{9,13},{10,... | collective-permute-start | bytes 1769480 | tf_op jit(solution)/shard_map/ppermute | solution.py:1189
  425.4 19.1 %collective-permute-start.71 = (bf16[4,48,512]{2,1,0:T(8,128)(2,1)S(1)}, bf16[4,48,512]{2,1,0:T(8,128)(2,1)S(1)}, u32[]{:S(2)}, u32[]{:S(2)}) collective-permute-start(bf16[4,48,512]{2,1,0:T(8,128)(2,1)S(1)} %add_convert_fusion.10), channel_id=1, source_target_pairs={{0,2},{1,3},{2,0},{3,1},{4,6},{5,7},{6,4},{7,5},{8,10},{9,11},{10,... | collective-permute-start | bytes 589832 | tf_op jit(solution)/shard_map/ppermute | solution.py:1189
  440.5 10.5 %collective-permute-start.76 = (bf16[2,144,512]{2,1,0:T(8,128)(2,1)S(1)}, bf16[2,144,512]{2,1,0:T(8,128)(2,1)S(1)}, u32[]{:S(2)}, u32[]{:S(2)}) collective-permute-start(bf16[2,144,512]{2,1,0:T(8,128)(2,1)S(1)} %add_convert_fusion.7), channel_id=1, source_target_pairs={{0,8},{1,9},{2,10},{3,11},{4,12},{5,13},{6,14},{7,15},{8,0},{9,1},... | collective-permute-start | bytes 884744 | tf_op jit(solution)/shard_map/ppermute | solution.py:1189
  440.5 15.5 %collective-permute-start.80 = (bf16[1,128,512]{2,1,0:T(8,128)(2,1)S(1)}, bf16[1,128,512]{2,1,0:T(8,128)(2,1)S(1)}, u32[]{:S(2)}, u32[]{:S(2)}) collective-permute-start(bf16[1,128,512]{2,1,0:T(8,128)(2,1)S(1)} %add_convert_fusion.12), channel_id=1, source_target_pairs={{0,16},{1,17},{2,18},{3,19},{4,20},{5,21},{6,22},{7,23},{8,24},{9,... | collective-permute-start | bytes 393224 | tf_op jit(solution)/shard_map/ppermute | solution.py:1189
  441.9 14.1 %collective-permute-start.79 = (bf16[1,128,512]{2,1,0:T(8,128)(2,1)S(1)}, bf16[1,128,512]{2,1,0:T(8,128)(2,1)S(1)}, u32[]{:S(2)}, u32[]{:S(2)}) collective-permute-start(bf16[1,128,512]{2,1,0:T(8,128)(2,1)S(1)} %add_convert_fusion.13), channel_id=1, source_target_pairs={{0,2},{1,3},{2,0},{3,1},{4,6},{5,7},{6,4},{7,5},{8,10},{9,11},{10,... | collective-permute-start | bytes 393224 | tf_op jit(solution)/shard_map/ppermute | solution.py:1189
  445.5 6.7 %collective-permute-start.75 = (bf16[2,48,512]{2,1,0:T(8,128)(2,1)S(1)}, bf16[2,48,512]{2,1,0:T(8,128)(2,1)S(1)}, u32[]{:S(2)}, u32[]{:S(2)}) collective-permute-start(bf16[2,48,512]{2,1,0:T(8,128)(2,1)S(1)} %add_convert_fusion.14), channel_id=1, source_target_pairs={{0,4},{1,5},{2,6},{3,7},{4,0},{5,1},{6,2},{7,3},{8,12},{9,13},{10,... | collective-permute-start | bytes 294920 | tf_op jit(solution)/shard_map/ppermute | solution.py:1189
  452.1 12.1 %collective-permute-start.78 = (bf16[1,144,512]{2,1,0:T(8,128)(2,1)S(1)}, bf16[1,144,512]{2,1,0:T(8,128)(2,1)S(1)}, u32[]{:S(2)}, u32[]{:S(2)}) collective-permute-start(bf16[1,144,512]{2,1,0:T(8,128)(2,1)S(1)} %add_convert_fusion.11), channel_id=1, source_target_pairs={{0,16},{1,17},{2,18},{3,19},{4,20},{5,21},{6,22},{7,23},{8,24},{9,... | collective-permute-start | bytes 442376 | tf_op jit(solution)/shard_map/ppermute | solution.py:1189
  453.1 9.0 %collective-permute-start.77 = (bf16[1,48,512]{2,1,0:T(8,128)(2,1)S(1)}, bf16[1,48,512]{2,1,0:T(8,128)(2,1)S(1)}, u32[]{:S(2)}, u32[]{:S(2)}) collective-permute-start(bf16[1,48,512]{2,1,0:T(8,128)(2,1)S(1)} %add_convert_fusion.15), channel_id=1, source_target_pairs={{0,16},{1,17},{2,18},{3,19},{4,20},{5,21},{6,22},{7,23},{8,24},{9,... | collective-permute-start | bytes 147464 | tf_op jit(solution)/shard_map/ppermute | solution.py:1189
  (96 other events, 380.6 us)
Sparse Core Ops, SparseCore 0:
  12.7 103.6 all-gather.1
  259.0 152.9 reduce-scatter.1

commit v3 on v2

--- a/solution.py
+++ b/solution.py
@@ -1219,8 +1219,8 @@
         quiet_x, _ = gentle(total)
         free = Order(True)
         g_one = chains(packed(["1"]), [(rows["1"], first)], free)
-        buf2, buf5 = packed(["2"], True), packed(["5"])
-        wb, at_b = gather(["3", "S", "4", "6"])
+        buf2, buf6 = packed(["2"], True), packed(["6"])
+        wb, at_b = gather(["3", "S", "4", "5"])
         steps(g_one)
         later = lax.optimization_barrier((buf2, g_one[0][1].held))[0]
         g_two = chains(later, [(r2, first), (r2, second), (rows["2"] - 2 * r2 + 16, third)], free)
@@ -1232,24 +1232,25 @@
         c1, st1 = dev.conv_one(near, sc, xp, msk, results(g_one), 0, rows["1"])
         seq.mark(st1)
         st1 = exchange(st1)
-        g_five = chains(seq.hold(buf5), [(rows["5"], quiet_x)], seq)
+        g_six = chains(seq.hold(buf6), [(rows["6"], quiet_x)], seq)
         a1, nrm1, c2, st2, normp = dev.conv_two(
             near, sc, c1, st1, None, seq.hold(msk), results(g_two), 0, rows["2"], rows["2"]
         )
         seq.mark(st2)
         st2 = exchange(st2)
-        steps(g_five)
-        steps(g_five)
+        steps(g_six)
+        seq.mark((seq.last, *st2[1:]))
         cs, sts = dev.conv_short(far, sc, xp, seq.hold(msk), wb, at_b["S"], rows["S"])
         seq.mark(sts)
-        steps(g_five)
+        steps(g_six)
         a2, nrm2, c3, st3 = dev.conv_expand(
             far, sc, c2, st2, normp, seq.hold(msk), wb, at_b["3"], rows["3"], "2", sts
         )
-        seq.mark(st3)
         st3 = exchange(st3)
+        seq.mark(tuple(st3))
+        steps(g_six)
         w1, w2 = results(g_one), results(g_two)
-        w3 = w4 = w6 = wb
+        w3 = w4 = w5 = wb
         at_3 = at_b
     else:
         w1, w2, w4, w5, w6 = [gather([k])[0] for k in ("1", "2", "4", "5", "6")]
@@ -1263,16 +1264,19 @@
             far, sc, c2, exchange(st2), normp, msk, w3, at_3["3"], rows["3"], "2", sts
         )
         st3 = exchange(st3)
-        at_b = {"4": 0, "6": 0}
+        at_b = {"4": 0, "5": 0}
     h, hb, nrm3, nrms, c4, st4 = dev.conv_four(
         far, sc, c3, cs, st3, normp, msk, w4, at_b["4"], rows["4"]
     )
     if direct:
         seq.mark(st4)
-        steps(g_five)
-        w5 = results(g_five)
-    a4, nrm4, c5, st5 = dev.conv_five(near, sc, c4, exchange(st4), normp, msk, w5, 0, rows["5"])
-    a5, nrm5, c6, st6 = dev.conv_expand(far, sc, c5, exchange(st5), normp, msk, w6, at_b["6"], rows["6"], "5")
+        st4 = exchange(st4)
+        steps(g_six)
+        w6 = results(g_six)
+    else:
+        st4 = exchange(st4)
+    a4, nrm4, c5, st5 = dev.conv_five(far, sc, c4, st4, normp, msk, w5, at_b["5"], rows["5"])
+    a5, nrm5, c6, st6 = dev.conv_expand(near, sc, c5, exchange(st5), normp, msk, w6, 0, rows["6"], "5")
     oc, oa, ob, dz6, nrm6, su6 = dev.finish(sc, c6, h, exchange(st6), normp, msk, ups)
 
     def scatter(piece, heights):
@@ -1317,14 +1321,14 @@
             chain.step()
 
     dc6, dz5, su5 = dev.back_six(
-        far, sc, dz6, c6, nrm6, exchange(su6), normp, msk, c5, nrm5, w6, at_b["6"], rows["6"]
+        near, sc, dz6, c6, nrm6, exchange(su6), normp, msk, c5, nrm5, w6, 0, rows["6"]
     )
     seq.mark(su5)
     high = [rows["6"] + rows["5"]]
     g65 = dev.grad_outer(seq.hold(far), whole, [(dc6, a5)], [(rows["6"], [rows["6"]])], high)
     seq.mark(g65[0][0])
     dc5, dz4, su4 = dev.back_five(
-        near, sc, dz5, c5, nrm5, exchange(su5), normp, seq.hold(msk), c4, nrm4, w5, 0, rows["5"]
+        far, sc, dz5, c5, nrm5, exchange(su5), normp, seq.hold(msk), c4, nrm4, w5, at_b["5"], rows["5"]
     )
     seq.mark(su4)
     g65 = dev.grad_taps(seq.hold(far), whole, a4, dc5, [(rows["5"], [rows["5"]])], high, 1, g65)

time: 482 us -> 480 us (level)
    ppermute x45, waiting for transfers between devices: 101 us -> 86.3 us  [swap(): return lax.ppermute(array, BOTH, [(i, i ^ 1 << bit) for i in range(total)])]
    all_gather x1, waiting for transfers between devices: 0.01 us -> 14 us  [gather(): lax.all_gather(buf, BOTH, axis=0, tiled=True)]
    unnamed x174 -> x168, local copies, waits for them, and re-layouts: 16.4 us -> 11.3 us
  transfers between devices with their start and end apart: 83 -> 83, of which waited for: 39 -> 39; matrix products, arithmetic and copies ran while one was open for 9% -> 8% of each run, Pallas kernels for 29% -> 30%
where the time goes in v3:
time: 480 us; the launch traced here: 475 us
  Pallas kernels  182 us (38%)
  waiting for transfers between devices  139 us (29%)
  starting transfers between devices  81.5 us (17%)
  other arithmetic  42.7 us (9%)
  between operations  15.8 us (3%)
  local copies, waits for them, and re-layouts  13.2 us (3%)
    pallas_call x22, Pallas kernels, call(): pl.pallas_call(body, out_shape=[jax.ShapeDtypeStruct(shape, dtype) for sh...  182 us
    ppermute x45, waiting for transfers between devices, swap(): return lax.ppermute(array, BOTH, [(i, i ^ 1 << bit) for i in range(total)])  86.3 us
    ppermute x45, starting transfers between devices, swap(): return lax.ppermute(array, BOTH, [(i, i ^ 1 << bit) for i in range(total)])  57.2 us
    ppermute x36, waiting for transfers between devices, exchange(): lax.ppermute(stat, 'bn', [(i, i ^ k) for i in range(members)])  38.7 us
    convert_element_type x16, other arithmetic, step(): sum([k[half:].astype(F32) for k in kept[1:]], kept[0][half:].astype(F32))  24.3 us
    ppermute x36, starting transfers between devices, exchange(): lax.ppermute(stat, 'bn', [(i, i ^ k) for i in range(members)])  24.1 us
    all_gather x1, waiting for transfers between devices, gather(): lax.all_gather(buf, BOTH, axis=0, tiled=True)  14 us
    unnamed x168, local copies, waits for them, and re-layouts  11.3 us
  transfers between devices with their start and end apart: 83, of which 39 were waited for; matrix products, arithmetic and copies ran while one was open for 8% of the time, Pallas kernels for 30%

profile of v3, /device:TPU:0, one launch (start us, length us, event | category | flops | bytes accessed | tf_op | source)
XLA Modules:
  0.0 474.6 jit_solution(2969801638994164540)
XLA Ops:
  12.8 4.1 collective-permute-start
  19.2 1.8 collective-permute-start.1
  21.3 2.6 collective-permute-start.13
  28.1 3.4 collective-permute-done.8
  40.2 3.8 collective-permute-start.20
  44.5 1.8 collective-permute-start.3
  46.4 12.5 %collective-permute-done.20 = bf16[4,64,512]{2,1,0:T(8,128)(2,1)S(1)} collective-permute-done((bf16[4,64,512]{2,1,0:T(8,128)(2,1)S(1)}, bf16[4,64,512]{2,1,0:T(8,128)(2,1)S(1)}, u32[]{:S(2)}, u32[]{:S(2)}) %collective-permute-start.20) | collective-permute-done | bytes 262176 | tf_op jit(solution)/shard_map/ppermute | solution.py:1189
  59.0 3.7 collective-permute-start.21
  64.2 2.2 collective-permute-done.10
  66.4 2.4 collective-permute-start.11
  69.5 13.3 %collective-permute-done.21 = bf16[8,64,512]{2,1,0:T(8,128)(2,1)S(1)} collective-permute-done((bf16[8,64,512]{2,1,0:T(8,128)(2,1)S(1)}, bf16[8,64,512]{2,1,0:T(8,128)(2,1)S(1)}, u32[]{:S(2)}, u32[]{:S(2)}) %collective-permute-start.21) | collective-permute-done | bytes 524320 | tf_op jit(solution)/shard_map/ppermute | solution.py:1189
  86.1 7.1 %shard_map.544 = (bf16[1920,1024]{1,0:T(8,128)(2,1)}, f32[480,128]{1,0:T(8,128)}, f32[5,3]{1,0:T(8,128)}) custom-call(s32[2]{0:T(128)} %pad_add_fusion.spot, s32[128]{0:T(128)} %la.1, s32[64]{0:T(128)} %lb.1, s32[64]{0:T(128)} %lc.1, bf16[10,10,4,1024]{3,2,1,0:T(4,128)(2,1)} %bitcast.107, bf16[18,18,2,1024]{3,2,1,0:T(2,128)(2,1)} %bitcast.106, ...), custom_call_target="tpu_custom_call" | custom-call | tf_op jit(solution)/shard_map/pallas_call | solution.py:76
  93.3 8.2 %shard_map.545 = (f32[1920,512]{1,0:T(8,128)}, f32[8,512]{1,0:T(8,128)}) custom-call(s32[1]{0:T(128)} %bitcast.5.ids, f32[5,3]{1,0:T(8,128)} %get-tuple-element.145.sc, bf16[1920,1024]{1,0:T(8,128)(2,1)} %get-tuple-element.146.xp.rest_3_.rest_0_, f32[480,128]{1,0:T(8,128)} %get-tuple-element.234.msk, ...), custom_call_target="tpu_custom_call" | custom-call | flops 2013265920 | tf_op jit(solution)/shard_map/pallas_call | solution.py:76
  103.3 2.0 collective-permute-done.7.rest_3_
  108.7 11.3 %shard_map.546 = (bf16[1920,512]{1,0:T(8,128)(2,1)}, f32[8,512]{1,0:T(8,128)}, f32[480,512]{1,0:T(8,128)}, f32[8,512]{1,0:T(8,128)}, f32[32,512]{1,0:T(8,128)}) custom-call(s32[1]{0:T(128)} %bitcast.5.ids, f32[5,3]{1,0:T(8,128)} %get-tuple-element.145.sc, f32[1920,512]{1,0:T(8,128)} %get-tuple-element.148.c1, f32[480,128]{1,0:T(8,128)} %get-tuple-element.234.msk, ...), custom_call_target="tpu_custom_call" | custom-call | flops 2264924160 | tf_op jit(solution)/shard_map/pallas_call | solution.py:76
  121.9 1.8 collective-permute-start.24
  124.6 14.0 %all-gather.2.cloned.1.call-done = bf16[12800,512]{1,0:T(8,128)(2,1)} async-done(((bf16[400,512]{1,0:T(8,128)(2,1)}), bf16[12800,512]{1,0:T(8,128)(2,1)}) %all-gather.2.cloned.1.call-update) | async-done | bytes 13107216 | tf_op jit(solution)/shard_map/all_gather | solution.py:1177
  138.5 9.4 %shard_map.547 = (f32[480,2048]{1,0:T(8,128)}, f32[8,2048]{1,0:T(8,128)}) custom-call(s32[1]{0:T(128)} %constant.23.clone.1.ids.ids_s, f32[5,3]{1,0:T(8,128)} %get-tuple-element.145.sc, bf16[1920,1024]{1,0:T(8,128)(2,1)} %get-tuple-element.146.xp.rest_3_.rest_0_, f32[480,128]{1,0:T(8,128)} %get-tuple-element.234.msk, bf16[32,400,512]{2,1,0:T(8,128)(2,1)} %bitcast.93), custom_call_target="tpu_custom_call" | custom-call | flops 2013265920 | tf_op jit(solution)/shard_map/pallas_call | solution.py:76
  148.1 7.2 %shard_map.548 = (bf16[480,512]{1,0:T(8,128)(2,1)}, f32[8,512]{1,0:T(8,128)}, f32[480,2048]{1,0:T(8,128)}, f32[16,2048]{1,0:T(8,128)}) custom-call(s32[1]{0:T(128)} %constant.23.clone.1.ids.ids_s, f32[5,3]{1,0:T(8,128)} %get-tuple-element.145.sc, f32[480,512]{1,0:T(8,128)} %get-tuple-element.154.c.c2, f32[32,512]{1,0:T(8,128)} %get-tuple-element.155.normp, ...), custom_call_target="tpu_custom_call" | custom-call | flops 1006632960 | tf_op jit(solution)/shard_map/pallas_call | solution.py:76
  157.3 3.8 collective-permute-done.30.rest_3_
  161.0 3.2 collective-permute-done.29.rest_2_
  165.9 9.5 %shard_map.549 = (f32[480,2048]{1,0:T(8,128)}, bf16[480,2048]{1,0:T(8,128)(2,1)}, f32[8,2048]{1,0:T(8,128)}, f32[8,2048]{1,0:T(8,128)}, f32[480,512]{1,0:T(8,128)}, /*index=5*/f32[8,512]{1,0:T(8,128)}) custom-call(s32[1]{0:T(128)} %constant.23.clone.1.ids.ids_s, f32[5,3]{1,0:T(8,128)} %get-tuple-element.145.sc, f32[480,2048]{1,0:T(8,128)} %get-tuple-element.168.c3.c3_far, ...), custom_call_target="tpu_custom_call" | custom-call | flops 1006632960 | tf_op jit(solution)/shard_map/pallas_call | solution.py:76
  175.4 2.5 collective-permute-done.38
  183.1 7.6 %shard_map.550 = (bf16[480,512]{1,0:T(8,128)(2,1)}, f32[8,512]{1,0:T(8,128)}, f32[480,512]{1,0:T(8,128)}, f32[8,512]{1,0:T(8,128)}) custom-call(s32[1]{0:T(128)} %constant.23.clone.1.ids.ids_s, f32[5,3]{1,0:T(8,128)} %get-tuple-element.145.sc, f32[480,512]{1,0:T(8,128)} %get-tuple-element.171.c4, f32[32,512]{1,0:T(8,128)} %get-tuple-element.155.normp, ...), custom_call_target="tpu_custom_call" | custom-call | flops 2264924160 | tf_op jit(solution)/shard_map/pallas_call | solution.py:76
  195.9 7.1 %shard_map.551 = (bf16[480,512]{1,0:T(8,128)(2,1)}, f32[8,512]{1,0:T(8,128)}, f32[480,2048]{1,0:T(8,128)}, f32[8,2048]{1,0:T(8,128)}) custom-call(s32[1]{0:T(128)} %bitcast.5.ids, f32[5,3]{1,0:T(8,128)} %get-tuple-element.145.sc, f32[480,512]{1,0:T(8,128)} %get-tuple-element.173.c.c5, f32[32,512]{1,0:T(8,128)} %get-tuple-element.155.normp, ...), custom_call_target="tpu_custom_call" | custom-call | flops 1006632960 | tf_op jit(solution)/shard_map/pallas_call | solution.py:76
  205.1 2.0 collective-permute-done.42.rest_3_
  207.1 2.0 collective-permute-done.41.rest_2_
  209.7 10.1 %shard_map.552 = (bf16[5,5,4,2048]{3,2,1,0:T(4,128)(2,1)}, bf16[9,9,2,2048]{3,2,1,0:T(2,128)(2,1)}, bf16[7,7,2,2048]{3,2,1,0:T(2,128)(2,1)}, f32[480,2048]{1,0:T...) custom-call(f32[5,3]{1,0:T(8,128)} %get-tuple-element.145.sc, f32[480,2048]{1,0:T(8,128)} %get-tuple-element.177.c6, ...), custom_call_target="tpu_custom_call" | custom-call | tf_op jit(solution)/shard_map/pallas_call | solution.py:76
  221.7 2.6 collective-permute-done.45.rest_3_
  226.5 8.5 %shard_map.553 = (bf16[480,2048]{1,0:T(8,128)(2,1)}, f32[480,512]{1,0:T(8,128)}, f32[8,512]{1,0:T(8,128)}) custom-call(s32[1]{0:T(128)} %bitcast.5.ids, f32[5,3]{1,0:T(8,128)} %get-tuple-element.145.sc, f32[480,2048]{1,0:T(8,128)} %get-tuple-element.183.dz.dz6_far, f32[480,2048]{1,0:T(8,128)} %get-tuple-element.177.c6, f32[8,2048]{1,0:T(8,128)} %get-tuple-element.184.nrm6, ...), custom_call_target="tpu_custom_call" | custom-call | flops 1006632960 | tf_op jit(solution)/shard_map/pallas_call | solution.py:76
  237.0 4.3 shard_map.554.rest_2_
  241.9 8.5 %shard_map.555 = (bf16[480,512]{1,0:T(8,128)(2,1)}, f32[480,512]{1,0:T(8,128)}, f32[8,512]{1,0:T(8,128)}) custom-call(s32[1]{0:T(128)} %constant.23.clone.1.ids.ids_s, f32[5,3]{1,0:T(8,128)} %get-tuple-element.145.sc, f32[480,512]{1,0:T(8,128)} %get-tuple-element.187.dz5, f32[480,512]{1,0:T(8,128)} %get-tuple-element.173.c.c5, ...), custom_call_target="tpu_custom_call" | custom-call | flops 2264924160 | tf_op jit(solution)/shard_map/pallas_call | solution.py:76
  250.4 6.1 %shard_map.556 = bf16[32,208,512]{2,1,0:T(8,128)(2,1)} custom-call(s32[1]{0:T(128)} %constant.23.clone.1.ids.ids_s, bf16[480,512]{1,0:T(8,128)(2,1)} %get-tuple-element.197.rest_0_, bf16[480,512]{1,0:T(8,128)(2,1)} %get-tuple-element.198.rest_1_, bf16[32,208,512]{2,1,0:T(8,128)(2,1)} %shard_map.554.rest_2_), custom_call_target="tpu_custom_call", output_to_operand_aliasing={{}: (3, {})} | custom-call | flops 2264924160 | tf_op jit(solution)/shard_map/pallas_call | solution.py:76
  262.5 12.7 %shard_map.557 = (bf16[480,512]{1,0:T(8,128)(2,1)}, f32[480,2048]{1,0:T(8,128)}, f32[16,2048]{1,0:T(8,128)}) custom-call(s32[1]{0:T(128)} %constant.23.clone.1.ids.ids_s, f32[5,3]{1,0:T(8,128)} %get-tuple-element.145.sc, f32[480,512]{1,0:T(8,128)} %get-tuple-element.194.dz4, f32[480,512]{1,0:T(8,128)} %get-tuple-element.171.c4, ...), custom_call_target="tpu_custom_call" | custom-call | flops 1006632960 | tf_op jit(solution)/shard_map/pallas_call | solution.py:76
  277.1 4.3 shard_map.558
  283.0 3.8 collective-permute-done.53.rest_2_
  287.6 10.6 %shard_map.559 = (bf16[480,2048]{1,0:T(8,128)(2,1)}, bf16[480,2048]{1,0:T(8,128)(2,1)}, f32[480,512]{1,0:T(8,128)}, f32[8,512]{1,0:T(8,128)}) custom-call(s32[1]{0:T(128)} %constant.23.clone.1.ids.ids_s, f32[5,3]{1,0:T(8,128)} %get-tuple-element.145.sc, f32[480,2048]{1,0:T(8,128)} %get-tuple-element.202.dz3, f32[480,2048]{1,0:T(8,128)} %get-tuple-element.168.c3.c3_far, ...), custom_call_target="tpu_custom_call" | custom-call | flops 1006632960 | tf_op jit(solution)/shard_map/pallas_call | solution.py:76
  298.1 8.4 %shard_map.560 = (bf16[16,128,512]{2,1,0:T(8,128)(2,1)}, bf16[16,128,512]{2,1,0:T(8,128)(2,1)}, bf16[16,128,512]{2,1,0:T(8,128)(2,1)}, bf16[16,128,512]{2,1,0:T(8,128)(2,1)}) custom-call(s32[1]{0:T(128)} %bitcast.5.ids, bf16[480,512]{1,0:T(8,128)(2,1)} %get-tuple-element.212.rest_0_, ...), custom_call_target="tpu_custom_call", output_to_operand_aliasing={{0}: (5, {}), {1}: (6, {}), {2}: (7, {}), {3}: (8, {})} | custom-call | flops 3019898880 | tf_op jit(solution)/shard_map/pallas_call | solution.py:76
  307.3 2.2 collective-permute-start.59
  310.9 2.7 collective-permute-done.58.rest_2_
  314.2 11.9 %shard_map.561 = (bf16[480,512]{1,0:T(8,128)(2,1)}, f32[1920,512]{1,0:T(8,128)}, f32[8,512]{1,0:T(8,128)}) custom-call(s32[1]{0:T(128)} %bitcast.5.ids, f32[5,3]{1,0:T(8,128)} %get-tuple-element.145.sc, f32[480,512]{1,0:T(8,128)} %get-tuple-element.222.dz2, f32[480,512]{1,0:T(8,128)} %get-tuple-element.154.c.c2, f32[8,512]{1,0:T(8,128)} %get-tuple-element.209.nrm2, ...), custom_call_target="tpu_custom_call" | custom-call | flops 2264924160 | tf_op jit(solution)/shard_map/pallas_call | solution.py:76
  326.1 2.7 add_convert_fusion.2
  328.9 2.5 add_convert_fusion.1
  331.4 6.5 %shard_map.562 = (bf16[16,144,512]{2,1,0:T(8,128)(2,1)}, bf16[16,144,512]{2,1,0:T(8,128)(2,1)}) custom-call(s32[1]{0:T(128)} %bitcast.5.ids, bf16[1920,512]{1,0:T(8,128)(2,1)} %get-tuple-element.229.rest_0_, bf16[480,512]{1,0:T(8,128)(2,1)} %get-tuple-element.230.rest_1_), custom_call_target="tpu_custom_call" | custom-call | flops 2264924160 | tf_op jit(solution)/shard_map/pallas_call | solution.py:76
  338.0 3.8 collective-permute-start.61
  341.8 3.1 collective-permute-start.60
  346.4 2.1 collective-permute-done.65.rest_3_
  350.3 6.1 %shard_map.563.rest_1_.dc1 = bf16[1920,512]{1,0:T(8,128)(2,1)} custom-call(f32[5,3]{1,0:T(8,128)} %get-tuple-element.145.sc, f32[1920,512]{1,0:T(8,128)} %get-tuple-element.233.dz1, f32[1920,512]{1,0:T(8,128)} %get-tuple-element.148.c1, f32[8,512]{1,0:T(8,128)} %get-tuple-element.224.nrm1, f32[32,512]{1,0:T(8,128)} %get-tuple-element.155.normp, ...), custom_call_target="tpu_custom_call" | custom-call | tf_op jit(solution)/shard_map/pallas_call | solution.py:76
  356.4 2.0 add_convert_fusion
  358.3 14.4 %collective-permute-done.61 = bf16[8,128,512]{2,1,0:T(8,128)(2,1)} collective-permute-done((bf16[8,128,512]{2,1,0:T(8,128)(2,1)}, bf16[8,128,512]{2,1,0:T(8,128)(2,1)}, u32[]{:S(2)}, u32[]{:S(2)}) %collective-permute-start.61) | collective-permute-done | bytes 1048608 | tf_op jit(solution)/shard_map/ppermute | solution.py:1189
  372.7 2.2 add_convert_fusion.5
  375.0 2.2 add_convert_fusion.4
  377.2 6.4 %shard_map.564 = (bf16[16,48,512]{2,1,0:T(8,128)(2,1)}, bf16[16,48,512]{2,1,0:T(8,128)(2,1)}) custom-call(s32[1]{0:T(128)} %bitcast.5.ids, bf16[1920,1024]{1,0:T(8,128)(2,1)} %get-tuple-element.146.xp.rest_3_.rest_0_, bf16[1920,512]{1,0:T(8,128)(2,1)} %shard_map.563.rest_1_.dc1, f32[8,512]{1,0:T(8,128)} %get-tuple-element.225.rest_0_.rest_2_, ...), custom_call_target="tpu_custom_call" | custom-call | flops 754974720 | tf_op jit(solution)/shard_map/pallas_call | solution.py:76
  383.7 1.8 collective-permute-start.69
  385.5 5.3 %collective-permute-start.70 = (bf16[4,128,512]{2,1,0:T(8,128)(2,1)}, bf16[4,128,512]{2,1,0:T(8,128)(2,1)}, u32[]{:S(2)}, u32[]{:S(2)}) collective-permute-start(bf16[4,128,512]{2,1,0:T(8,128)(2,1)} %add_convert_fusion.5), channel_id=1, source_target_pairs={{0,8},{1,9},{2,10},{3,11},{4,12},{5,13},{6,14},{7,15},{8,0},{9,1},... | collective-permute-start | bytes 1572872 | tf_op jit(solution)/shard_map/ppermute | solution.py:1189
  390.8 10.8 %shard_map.565 = (bf16[10,10,4,1024]{3,2,1,0:T(4,128)(2,1)}, bf16[18,18,2,1024]{3,2,1,0:T(2,128)(2,1)}, bf16[14,14,2,1024]{3,2,1,0:T(2,128)(2,1)}) custom-call(s32[1]{0:T(128)} %bitcast.5.ids, s32[1]{0:T(128)} %constant.23.clone.1.ids.ids_s, bf16[1920,512]{1,0:T(8,128)(2,1)} %shard_map.563.rest_1_.dc1, bf16[480,2048]{1,0:T(8,128)(2,1)} %get-tuple-element.214.rest_2_.dcs, ...), custom_call_target="tpu_custom_call" | custom-call | flops 4026531840 | tf_op jit(solution)/shard_map/pallas_call | solution.py:76
  403.1 3.2 collective-permute-done.70
  409.0 12.1 %collective-permute-done.68 = bf16[8,144,512]{2,1,0:T(8,128)(2,1)} collective-permute-done((bf16[8,144,512]{2,1,0:T(8,128)(2,1)S(1)}, bf16[8,144,512]{2,1,0:T(8,128)(2,1)}, u32[]{:S(2)}, u32[]{:S(2)}) %collective-permute-start.68) | collective-permute-done | bytes 1179680 | tf_op jit(solution)/shard_map/ppermute | solution.py:1189
  424.9 1.7 collective-permute-done.73
  427.7 9.7 %collective-permute-done.72 = bf16[4,144,512]{2,1,0:T(8,128)(2,1)S(1)} collective-permute-done((bf16[4,144,512]{2,1,0:T(8,128)(2,1)S(1)}, bf16[4,144,512]{2,1,0:T(8,128)(2,1)S(1)}, u32[]{:S(2)}, u32[]{:S(2)}) %collective-permute-start.72) | collective-permute-done | bytes 589856 | tf_op jit(solution)/shard_map/ppermute | solution.py:1189
  441.4 1.8 collective-permute-start.75
  443.2 5.8 %collective-permute-done.76 = bf16[2,144,512]{2,1,0:T(8,128)(2,1)S(1)} collective-permute-done((bf16[2,144,512]{2,1,0:T(8,128)(2,1)S(1)}, bf16[2,144,512]{2,1,0:T(8,128)(2,1)S(1)}, u32[]{:S(2)}, u32[]{:S(2)}) %collective-permute-start.76) | collective-permute-done | bytes 294944 | tf_op jit(solution)/shard_map/ppermute | solution.py:1189
  451.1 3.0 collective-permute-start.77
  462.2 2.2 multiply_subtract_fusion.1
  (357 shorter events, 100.8 us)
Async XLA Ops:
  7.2 131.3 %all-gather.2.cloned.1.call-start = ((), (), s32[]{:S(2)}) async-start(), calls=%async_computation.1 | async-start | bytes 13516800 | tf_op jit(solution)/shard_map/all_gather | solution.py:1177
  12.7 451.7 %reduce-scatter.2.cloned.1.call-start = ((), (), s32[]{:S(2)}) async-start(), calls=%async_computation.2 | async-start | bytes 7028736 | tf_op jit(solution)/shard_map/reduce_scatter | solution.py:1289
  12.8 6.3 %collective-permute-start = (bf16[1,32,512]{2,1,0:T(8,128)(2,1)S(1)}, bf16[1,32,512]{2,1,0:T(8,128)(2,1)S(1)}, u32[]{:S(2)}, u32[]{:S(2)}) collective-permute-start(bf16[1,32,512]{2,1,0:T(8,128)(2,1)S(1)} %bitcast.110), channel_id=1, source_target_pairs={{0,16},{1,17},{2,18},{3,19},{4,20},{5,21},{6,22},{7,23},{8,24},{9,... | collective-permute-start | bytes 98312 | tf_op jit(solution)/shard_map/ppermute | solution.py:1189
  19.2 14.4 %collective-permute-start.1 = (bf16[2,32,512]{2,1,0:T(8,128)(2,1)S(1)}, bf16[2,32,512]{2,1,0:T(8,128)(2,1)S(1)}, u32[]{:S(2)}, u32[]{:S(2)}) collective-permute-start(bf16[2,32,512]{2,1,0:T(8,128)(2,1)S(1)} %pad_maximum_fusion.16), channel_id=1, source_target_pairs={{0,4},{1,5},{2,6},{3,7},{4,0},{5,1},{6,2},{7,3},{8,12},{9,13},{10,... | collective-permute-start | bytes 196616 | tf_op jit(solution)/shard_map/ppermute | solution.py:1189
  20.9 13.8 %collective-permute-start.18 = (bf16[1,64,512]{2,1,0:T(8,128)(2,1)S(1)}, bf16[1,64,512]{2,1,0:T(8,128)(2,1)S(1)}, u32[]{:S(2)}, u32[]{:S(2)}) collective-permute-start(bf16[1,64,512]{2,1,0:T(8,128)(2,1)S(1)} %slice_bitcast_fusion.10), channel_id=1, source_target_pairs={{0,4},{1,5},{2,6},{3,7},{4,0},{5,1},{6,2},{7,3},{8,12},{9,13},{10,... | collective-permute-start | bytes 196616 | tf_op jit(solution)/shard_map/ppermute | solution.py:1189
  21.3 5.3 %collective-permute-start.13 = (bf16[1,48,512]{2,1,0:T(8,128)(2,1)S(1)}, bf16[1,48,512]{2,1,0:T(8,128)(2,1)S(1)}, u32[]{:S(2)}, u32[]{:S(2)}) collective-permute-start(bf16[1,48,512]{2,1,0:T(8,128)(2,1)S(1)} %get-tuple-element.294), channel_id=1, source_target_pairs={{0,16},{1,17},{2,18},{3,19},{4,20},{5,21},{6,22},{7,23},{8,24},{9,... | collective-permute-start | bytes 147464 | tf_op jit(solution)/shard_map/ppermute | solution.py:1189
  23.9 7.6 %collective-permute-start.8 = (bf16[1,48,512]{2,1,0:T(8,128)(2,1)S(1)}, bf16[1,48,512]{2,1,0:T(8,128)(2,1)S(1)}, u32[]{:S(2)}, u32[]{:S(2)}) collective-permute-start(bf16[1,48,512]{2,1,0:T(8,128)(2,1)S(1)} %get-tuple-element.295), channel_id=1, source_target_pairs={{0,16},{1,17},{2,18},{3,19},{4,20},{5,21},{6,22},{7,23},{8,24},{9,... | collective-permute-start | bytes 147464 | tf_op jit(solution)/shard_map/ppermute | solution.py:1189
  26.6 9.7 %collective-permute-start.14 = (bf16[2,48,512]{2,1,0:T(8,128)(2,1)S(1)}, bf16[2,48,512]{2,1,0:T(8,128)(2,1)S(1)}, u32[]{:S(2)}, u32[]{:S(2)}) collective-permute-start(bf16[2,48,512]{2,1,0:T(8,128)(2,1)S(1)} %pad_maximum_fusion.15), channel_id=1, source_target_pairs={{0,2},{1,3},{2,0},{3,1},{4,6},{5,7},{6,4},{7,5},{8,10},{9,11},{10,... | collective-permute-start | bytes 294920 | tf_op jit(solution)/shard_map/ppermute | solution.py:1189
  31.5 5.7 %collective-permute-start.9 = (bf16[2,48,512]{2,1,0:T(8,128)(2,1)S(1)}, bf16[2,48,512]{2,1,0:T(8,128)(2,1)S(1)}, u32[]{:S(2)}, u32[]{:S(2)}) collective-permute-start(bf16[2,48,512]{2,1,0:T(8,128)(2,1)S(1)} %pad_maximum_fusion.14), channel_id=1, source_target_pairs={{0,4},{1,5},{2,6},{3,7},{4,0},{5,1},{6,2},{7,3},{8,12},{9,13},{10,... | collective-permute-start | bytes 294920 | tf_op jit(solution)/shard_map/ppermute | solution.py:1189
  33.6 10.9 %collective-permute-start.2 = (bf16[4,32,512]{2,1,0:T(8,128)(2,1)S(1)}, bf16[4,32,512]{2,1,0:T(8,128)(2,1)S(1)}, u32[]{:S(2)}, u32[]{:S(2)}) collective-permute-start(bf16[4,32,512]{2,1,0:T(8,128)(2,1)S(1)} %pad_maximum_fusion.10), channel_id=1, source_target_pairs={{0,8},{1,9},{2,10},{3,11},{4,12},{5,13},{6,14},{7,15},{8,0},{9,1},... | collective-permute-start | bytes 393224 | tf_op jit(solution)/shard_map/ppermute | solution.py:1189
  34.7 5.5 %collective-permute-start.19 = (bf16[2,64,512]{2,1,0:T(8,128)(2,1)S(1)}, bf16[2,64,512]{2,1,0:T(8,128)(2,1)S(1)}, u32[]{:S(2)}, u32[]{:S(2)}) collective-permute-start(bf16[2,64,512]{2,1,0:T(8,128)(2,1)S(1)} %pad_maximum_fusion.11), channel_id=1, source_target_pairs={{0,2},{1,3},{2,0},{3,1},{4,6},{5,7},{6,4},{7,5},{8,10},{9,11},{10,... | collective-permute-start | bytes 393224 | tf_op jit(solution)/shard_map/ppermute | solution.py:1189
  36.3 26.3 %collective-permute-start.15 = (bf16[4,48,512]{2,1,0:T(8,128)(2,1)S(1)}, bf16[4,48,512]{2,1,0:T(8,128)(2,1)S(1)}, u32[]{:S(2)}, u32[]{:S(2)}) collective-permute-start(bf16[4,48,512]{2,1,0:T(8,128)(2,1)S(1)} %pad_maximum_fusion.8), channel_id=1, source_target_pairs={{0,8},{1,9},{2,10},{3,11},{4,12},{5,13},{6,14},{7,15},{8,0},{9,1},... | collective-permute-start | bytes 589832 | tf_op jit(solution)/shard_map/ppermute | solution.py:1189
  37.3 29.1 %collective-permute-start.10 = (bf16[4,48,512]{2,1,0:T(8,128)(2,1)S(1)}, bf16[4,48,512]{2,1,0:T(8,128)(2,1)S(1)}, u32[]{:S(2)}, u32[]{:S(2)}) collective-permute-start(bf16[4,48,512]{2,1,0:T(8,128)(2,1)S(1)} %pad_maximum_fusion.7), channel_id=1, source_target_pairs={{0,8},{1,9},{2,10},{3,11},{4,12},{5,13},{6,14},{7,15},{8,0},{9,1},... | collective-permute-start | bytes 589832 | tf_op jit(solution)/shard_map/ppermute | solution.py:1189
  40.2 18.7 %collective-permute-start.20 = (bf16[4,64,512]{2,1,0:T(8,128)(2,1)S(1)}, bf16[4,64,512]{2,1,0:T(8,128)(2,1)S(1)}, u32[]{:S(2)}, u32[]{:S(2)}) collective-permute-start(bf16[4,64,512]{2,1,0:T(8,128)(2,1)S(1)} %pad_maximum_fusion.5), channel_id=1, source_target_pairs={{0,16},{1,17},{2,18},{3,19},{4,20},{5,21},{6,22},{7,23},{8,24},{9,... | collective-permute-start | bytes 786440 | tf_op jit(solution)/shard_map/ppermute | solution.py:1189
  44.5 38.4 %collective-permute-start.3 = (bf16[8,32,512]{2,1,0:T(8,128)(2,1)S(1)}, bf16[8,32,512]{2,1,0:T(8,128)(2,1)S(1)}, u32[]{:S(2)}, u32[]{:S(2)}) collective-permute-start(bf16[8,32,512]{2,1,0:T(8,128)(2,1)S(1)} %pad_maximum_fusion.4), channel_id=1, source_target_pairs={{0,2},{1,3},{2,0},{3,1},{4,6},{5,7},{6,4},{7,5},{8,10},{9,11},{10,... | collective-permute-start | bytes 786440 | tf_op jit(solution)/shard_map/ppermute | solution.py:1189
  59.0 23.8 %collective-permute-start.21 = (bf16[8,64,512]{2,1,0:T(8,128)(2,1)S(1)}, bf16[8,64,512]{2,1,0:T(8,128)(2,1)S(1)}, u32[]{:S(2)}, u32[]{:S(2)}) collective-permute-start(bf16[8,64,512]{2,1,0:T(8,128)(2,1)S(1)} %pad_maximum_fusion), channel_id=1, source_target_pairs={{0,8},{1,9},{2,10},{3,11},{4,12},{5,13},{6,14},{7,15},{8,0},{9,1},... | collective-permute-start | bytes 1572872 | tf_op jit(solution)/shard_map/ppermute | solution.py:1189
  62.7 21.7 %collective-permute-start.16 = (bf16[8,48,512]{2,1,0:T(8,128)(2,1)S(1)}, bf16[8,48,512]{2,1,0:T(8,128)(2,1)S(1)}, u32[]{:S(2)}, u32[]{:S(2)}) collective-permute-start(bf16[8,48,512]{2,1,0:T(8,128)(2,1)S(1)} %pad_maximum_fusion.3), channel_id=1, source_target_pairs={{0,4},{1,5},{2,6},{3,7},{4,0},{5,1},{6,2},{7,3},{8,12},{9,13},{10,... | collective-permute-start | bytes 1179656 | tf_op jit(solution)/shard_map/ppermute | solution.py:1189
  66.4 17.8 %collective-permute-start.11 = (bf16[8,48,512]{2,1,0:T(8,128)(2,1)S(1)}, bf16[8,48,512]{2,1,0:T(8,128)(2,1)S(1)}, u32[]{:S(2)}, u32[]{:S(2)}) collective-permute-start(bf16[8,48,512]{2,1,0:T(8,128)(2,1)S(1)} %pad_maximum_fusion.2), channel_id=1, source_target_pairs={{0,2},{1,3},{2,0},{3,1},{4,6},{5,7},{6,4},{7,5},{8,10},{9,11},{10,... | collective-permute-start | bytes 1179656 | tf_op jit(solution)/shard_map/ppermute | solution.py:1189
  82.8 24.9 %collective-permute-start.22 = (bf16[16,64,512]{2,1,0:T(8,128)(2,1)S(1)}, bf16[16,64,512]{2,1,0:T(8,128)(2,1)S(1)}, u32[]{:S(2)}, u32[]{:S(2)}) collective-permute-start(bf16[16,64,512]{2,1,0:T(8,128)(2,1)S(1)} %constant_dynamic-update-slice_fusion.15.rest_8_), channel_id=1, source_target_pairs={{0,1},{1,0},{2,3},{3,2},{4,5},{5,4},{6,7},{7,6},{8,9},{9,8},{10,11... | collective-permute-start | bytes 3145736 | tf_op jit(solution)/shard_map/ppermute | solution.py:1189
  83.8 9.4 %collective-permute-start.4 = (bf16[16,32,512]{2,1,0:T(8,128)(2,1)}, bf16[16,32,512]{2,1,0:T(8,128)(2,1)}, u32[]{:S(2)}, u32[]{:S(2)}) collective-permute-start(bf16[16,32,512]{2,1,0:T(8,128)(2,1)} %constant_dynamic-update-slice_fusion.rest_0_), channel_id=1, source_target_pairs={{0,1},{1,0},{2,3},{3,2},{4,5},{5,4},{6,7},{7,6},{8,9},{9,8},{10,11... | collective-permute-start | bytes 1572872 | tf_op jit(solution)/shard_map/ppermute | solution.py:1189
  84.2 23.5 %collective-permute-start.12 = (bf16[16,48,512]{2,1,0:T(8,128)(2,1)S(1)}, bf16[16,48,512]{2,1,0:T(8,128)(2,1)}, u32[]{:S(2)}, u32[]{:S(2)}) collective-permute-start(bf16[16,48,512]{2,1,0:T(8,128)(2,1)S(1)} %constant_dynamic-update-slice_fusion.5.rest_4_), channel_id=1, source_target_pairs={{0,1},{1,0},{2,3},{3,2},{4,5},{5,4},{6,7},{7,6},{8,9},{9,8},{10,11... | collective-permute-start | bytes 2359304 | tf_op jit(solution)/shard_map/ppermute | solution.py:1189
  85.3 22.5 %collective-permute-start.17 = (bf16[16,48,512]{2,1,0:T(8,128)(2,1)}, bf16[16,48,512]{2,1,0:T(8,128)(2,1)}, u32[]{:S(2)}, u32[]{:S(2)}) collective-permute-start(bf16[16,48,512]{2,1,0:T(8,128)(2,1)} %constant_dynamic-update-slice_fusion.10.rest_6_), channel_id=1, source_target_pairs={{0,1},{1,0},{2,3},{3,2},{4,5},{5,4},{6,7},{7,6},{8,9},{9,8},{10,11... | collective-permute-start | bytes 2359304 | tf_op jit(solution)/shard_map/ppermute | solution.py:1189
  102.7 4.3 collective-permute-start.6
  107.0 14.9 %collective-permute-start.23 = (bf16[1,64,512]{2,1,0:T(8,128)(2,1)S(1)}, bf16[1,64,512]{2,1,0:T(8,128)(2,1)S(1)}, u32[]{:S(2)}, u32[]{:S(2)}) collective-permute-start(bf16[1,64,512]{2,1,0:T(8,128)(2,1)S(1)} %bitcast.102), channel_id=1, source_target_pairs={{0,2},{1,3},{2,0},{3,1},{4,6},{5,7},{6,4},{7,5},{8,10},{9,11},{10,... | collective-permute-start | bytes 196616 | tf_op jit(solution)/shard_map/ppermute | solution.py:1189
  121.9 26.1 %collective-permute-start.24 = (bf16[2,64,512]{2,1,0:T(8,128)(2,1)S(1)}, bf16[2,64,512]{2,1,0:T(8,128)(2,1)S(1)}, u32[]{:S(2)}, u32[]{:S(2)}) collective-permute-start(bf16[2,64,512]{2,1,0:T(8,128)(2,1)S(1)} %pad_maximum_fusion.12), channel_id=1, source_target_pairs={{0,16},{1,17},{2,18},{3,19},{4,20},{5,21},{6,22},{7,23},{8,24},{9,... | collective-permute-start | bytes 393224 | tf_op jit(solution)/shard_map/ppermute | solution.py:1189
  148.0 16.2 %collective-permute-start.37 = (bf16[4,64,512]{2,1,0:T(8,128)(2,1)S(1)}, bf16[4,64,512]{2,1,0:T(8,128)(2,1)S(1)}, u32[]{:S(2)}, u32[]{:S(2)}) collective-permute-start(bf16[4,64,512]{2,1,0:T(8,128)(2,1)S(1)} %pad_maximum_fusion.6), channel_id=1, source_target_pairs={{0,8},{1,9},{2,10},{3,11},{4,12},{5,13},{6,14},{7,15},{8,0},{9,1},... | collective-permute-start | bytes 786440 | tf_op jit(solution)/shard_map/ppermute | solution.py:1189
  155.3 5.7 %collective-permute-start.30 = (f32[16,2048]{1,0:T(8,128)}, f32[16,2048]{1,0:T(8,128)S(1)}, u32[]{:S(2)}, u32[]{:S(2)}) collective-permute-start(f32[16,2048]{1,0:T(8,128)} %get-tuple-element.170.rest_0_), channel_id=1, source_target_pairs={{0,3},{1,2},{2,1},{3,0},{4,7},{5,6},{6,5},{7,4},{8,11},{9,10},{10,... | collective-permute-start | bytes 393224 | tf_op jit(solution)/shard_map/ppermute | solution.py:1193
  155.6 8.6 %collective-permute-start.29 = (f32[16,2048]{1,0:T(8,128)}, f32[16,2048]{1,0:T(8,128)S(1)}, u32[]{:S(2)}, u32[]{:S(2)}) collective-permute-start(f32[16,2048]{1,0:T(8,128)} %get-tuple-element.170.rest_0_), channel_id=1, source_target_pairs={{0,2},{1,3},{2,0},{3,1},{4,6},{5,7},{6,4},{7,5},{8,10},{9,11},{10,... | collective-permute-start | bytes 393224 | tf_op jit(solution)/shard_map/ppermute | solution.py:1193
  157.3 6.9 %collective-permute-start.28 = (f32[16,2048]{1,0:T(8,128)}, f32[16,2048]{1,0:T(8,128)S(1)}, u32[]{:S(2)}, u32[]{:S(2)}) collective-permute-start(f32[16,2048]{1,0:T(8,128)} %get-tuple-element.170.rest_0_), channel_id=1, source_target_pairs={{0,1},{1,0},{2,3},{3,2},{4,5},{5,4},{6,7},{7,6},{8,9},{9,8},{10,11... | collective-permute-start | bytes 393224 | tf_op jit(solution)/shard_map/ppermute | solution.py:1193
  164.3 13.7 %collective-permute-start.38 = (bf16[8,64,512]{2,1,0:T(8,128)(2,1)S(1)}, bf16[8,64,512]{2,1,0:T(8,128)(2,1)S(1)}, u32[]{:S(2)}, u32[]{:S(2)}) collective-permute-start(bf16[8,64,512]{2,1,0:T(8,128)(2,1)S(1)} %pad_maximum_fusion.1), channel_id=1, source_target_pairs={{0,4},{1,5},{2,6},{3,7},{4,0},{5,1},{6,2},{7,3},{8,12},{9,13},{10,... | collective-permute-start | bytes 1572872 | tf_op jit(solution)/shard_map/ppermute | solution.py:1189
  178.0 16.9 %collective-permute-start.39 = (bf16[16,64,512]{2,1,0:T(8,128)(2,1)S(1)}, bf16[16,64,512]{2,1,0:T(8,128)(2,1)S(1)}, u32[]{:S(2)}, u32[]{:S(2)}) collective-permute-start(bf16[16,64,512]{2,1,0:T(8,128)(2,1)S(1)} %constant_dynamic-update-slice_fusion.20.rest_4_), channel_id=1, source_target_pairs={{0,1},{1,0},{2,3},{3,2},{4,5},{5,4},{6,7},{7,6},{8,9},{9,8},{10,11... | collective-permute-start | bytes 3145736 | tf_op jit(solution)/shard_map/ppermute | solution.py:1189
  203.0 4.1 collective-permute-start.42
  203.7 5.4 %collective-permute-start.41 = (f32[8,2048]{1,0:T(8,128)}, f32[8,2048]{1,0:T(8,128)S(1)}, u32[]{:S(2)}, u32[]{:S(2)}) collective-permute-start(f32[8,2048]{1,0:T(8,128)} %get-tuple-element.179.rest_0_), channel_id=1, source_target_pairs={{0,2},{1,3},{2,0},{3,1},{4,6},{5,7},{6,4},{7,5},{8,10},{9,11},{10,... | collective-permute-start | bytes 196616 | tf_op jit(solution)/shard_map/ppermute | solution.py:1193
  219.8 4.5 collective-permute-start.45
  220.7 5.1 %collective-permute-start.44 = (f32[8,2048]{1,0:T(8,128)}, f32[8,2048]{1,0:T(8,128)S(1)}, u32[]{:S(2)}, u32[]{:S(2)}) collective-permute-start(f32[8,2048]{1,0:T(8,128)} %get-tuple-element.186.rest_0_.rest_7_), channel_id=1, source_target_pairs={{0,2},{1,3},{2,0},{3,1},{4,6},{5,7},{6,4},{7,5},{8,10},{9,11},{10,... | collective-permute-start | bytes 196616 | tf_op jit(solution)/shard_map/ppermute | solution.py:1193
  221.5 4.4 collective-permute-start.43
  235.1 6.2 %collective-permute-start.48 = (f32[8,512]{1,0:T(8,128)}, f32[8,512]{1,0:T(8,128)S(1)}, u32[]{:S(2)}, u32[]{:S(2)}) collective-permute-start(f32[8,512]{1,0:T(8,128)} %get-tuple-element.188.rest_0_.rest_6_), channel_id=1, source_target_pairs={{0,3},{1,2},{2,1},{3,0},{4,7},{5,6},{6,5},{7,4},{8,11},{9,10},{10,... | collective-permute-start | bytes 49160 | tf_op jit(solution)/shard_map/ppermute | solution.py:1193
  235.8 5.5 %collective-permute-start.47 = (f32[8,512]{1,0:T(8,128)}, f32[8,512]{1,0:T(8,128)S(1)}, u32[]{:S(2)}, u32[]{:S(2)}) collective-permute-start(f32[8,512]{1,0:T(8,128)} %get-tuple-element.188.rest_0_.rest_6_), channel_id=1, source_target_pairs={{0,2},{1,3},{2,0},{3,1},{4,6},{5,7},{6,4},{7,5},{8,10},{9,11},{10,... | collective-permute-start | bytes 49160 | tf_op jit(solution)/shard_map/ppermute | solution.py:1193
  236.7 4.6 collective-permute-start.46
  275.2 7.8 %collective-permute-start.54 = (f32[16,2048]{1,0:T(8,128)}, f32[16,2048]{1,0:T(8,128)S(1)}, u32[]{:S(2)}, u32[]{:S(2)}) collective-permute-start(f32[16,2048]{1,0:T(8,128)} %get-tuple-element.203.rest_0_.rest_4_), channel_id=1, source_target_pairs={{0,3},{1,2},{2,1},{3,0},{4,7},{5,6},{6,5},{7,4},{8,11},{9,10},{10,... | collective-permute-start | bytes 393224 | tf_op jit(solution)/shard_map/ppermute | solution.py:1193
  275.3 11.6 %collective-permute-start.53 = (f32[16,2048]{1,0:T(8,128)}, f32[16,2048]{1,0:T(8,128)S(1)}, u32[]{:S(2)}, u32[]{:S(2)}) collective-permute-start(f32[16,2048]{1,0:T(8,128)} %get-tuple-element.203.rest_0_.rest_4_), channel_id=1, source_target_pairs={{0,2},{1,3},{2,0},{3,1},{4,6},{5,7},{6,4},{7,5},{8,10},{9,11},{10,... | collective-permute-start | bytes 393224 | tf_op jit(solution)/shard_map/ppermute | solution.py:1193
  276.4 10.4 %collective-permute-start.52 = (f32[16,2048]{1,0:T(8,128)}, f32[16,2048]{1,0:T(8,128)S(1)}, u32[]{:S(2)}, u32[]{:S(2)}) collective-permute-start(f32[16,2048]{1,0:T(8,128)} %get-tuple-element.203.rest_0_.rest_4_), channel_id=1, source_target_pairs={{0,1},{1,0},{2,3},{3,2},{4,5},{5,4},{6,7},{7,6},{8,9},{9,8},{10,11... | collective-permute-start | bytes 393224 | tf_op jit(solution)/shard_map/ppermute | solution.py:1193
  306.5 19.6 %collective-permute-start.56 = (bf16[16,128,512]{2,1,0:T(8,128)(2,1)}, bf16[16,128,512]{2,1,0:T(8,128)(2,1)}, u32[]{:S(2)}, u32[]{:S(2)}) collective-permute-start(bf16[16,128,512]{2,1,0:T(8,128)(2,1)} %get-tuple-element.221), channel_id=1, source_target_pairs={{0,1},{1,0},{2,3},{3,2},{4,5},{5,4},{6,7},{7,6},{8,9},{9,8},{10,11... | collective-permute-start | bytes 6291464 | tf_op jit(solution)/shard_map/ppermute | solution.py:1189
  307.2 21.7 %collective-permute-start.55 = (bf16[16,128,512]{2,1,0:T(8,128)(2,1)}, bf16[16,128,512]{2,1,0:T(8,128)(2,1)}, u32[]{:S(2)}, u32[]{:S(2)}) collective-permute-start(bf16[16,128,512]{2,1,0:T(8,128)(2,1)} %get-tuple-element.219), channel_id=1, source_target_pairs={{0,1},{1,0},{2,3},{3,2},{4,5},{5,4},{6,7},{7,6},{8,9},{9,8},{10,11... | collective-permute-start | bytes 6291464 | tf_op jit(solution)/shard_map/ppermute | solution.py:1189
  309.4 4.2 collective-permute-start.58
  337.9 18.5 %collective-permute-start.62 = (bf16[16,144,512]{2,1,0:T(8,128)(2,1)}, bf16[16,144,512]{2,1,0:T(8,128)(2,1)}, u32[]{:S(2)}, u32[]{:S(2)}) collective-permute-start(bf16[16,144,512]{2,1,0:T(8,128)(2,1)} %get-tuple-element.232), channel_id=1, source_target_pairs={{0,1},{1,0},{2,3},{3,2},{4,5},{5,4},{6,7},{7,6},{8,9},{9,8},{10,11... | collective-permute-start | bytes 7077896 | tf_op jit(solution)/shard_map/ppermute | solution.py:1189
  338.0 34.7 %collective-permute-start.61 = (bf16[8,128,512]{2,1,0:T(8,128)(2,1)}, bf16[8,128,512]{2,1,0:T(8,128)(2,1)}, u32[]{:S(2)}, u32[]{:S(2)}) collective-permute-start(bf16[8,128,512]{2,1,0:T(8,128)(2,1)} %add_convert_fusion.2), channel_id=1, source_target_pairs={{0,4},{1,5},{2,6},{3,7},{4,0},{5,1},{6,2},{7,3},{8,12},{9,13},{10,... | collective-permute-start | bytes 3145736 | tf_op jit(solution)/shard_map/ppermute | solution.py:1189
  341.8 33.2 %collective-permute-start.60 = (bf16[8,128,512]{2,1,0:T(8,128)(2,1)}, bf16[8,128,512]{2,1,0:T(8,128)(2,1)}, u32[]{:S(2)}, u32[]{:S(2)}) collective-permute-start(bf16[8,128,512]{2,1,0:T(8,128)(2,1)} %add_convert_fusion.1), channel_id=1, source_target_pairs={{0,8},{1,9},{2,10},{3,11},{4,12},{5,13},{6,14},{7,15},{8,0},{9,1},... | collective-permute-start | bytes 3145736 | tf_op jit(solution)/shard_map/ppermute | solution.py:1189
  344.9 4.4 collective-permute-start.64
  383.5 18.1 %collective-permute-start.66 = (bf16[16,48,512]{2,1,0:T(8,128)(2,1)}, bf16[16,48,512]{2,1,0:T(8,128)(2,1)}, u32[]{:S(2)}, u32[]{:S(2)}) collective-permute-start(bf16[16,48,512]{2,1,0:T(8,128)(2,1)} %get-tuple-element.244), channel_id=1, source_target_pairs={{0,1},{1,0},{2,3},{3,2},{4,5},{5,4},{6,7},{7,6},{8,9},{9,8},{10,11... | collective-permute-start | bytes 2359304 | tf_op jit(solution)/shard_map/ppermute | solution.py:1189
  383.6 37.5 %collective-permute-start.68 = (bf16[8,144,512]{2,1,0:T(8,128)(2,1)S(1)}, bf16[8,144,512]{2,1,0:T(8,128)(2,1)}, u32[]{:S(2)}, u32[]{:S(2)}) collective-permute-start(bf16[8,144,512]{2,1,0:T(8,128)(2,1)S(1)} %add_convert_fusion), channel_id=1, source_target_pairs={{0,2},{1,3},{2,0},{3,1},{4,6},{5,7},{6,4},{7,5},{8,10},{9,11},{10,... | collective-permute-start | bytes 3538952 | tf_op jit(solution)/shard_map/ppermute | solution.py:1189
  383.7 23.9 %collective-permute-start.69 = (bf16[4,128,512]{2,1,0:T(8,128)(2,1)}, bf16[4,128,512]{2,1,0:T(8,128)(2,1)}, u32[]{:S(2)}, u32[]{:S(2)}) collective-permute-start(bf16[4,128,512]{2,1,0:T(8,128)(2,1)} %add_convert_fusion.4), channel_id=1, source_target_pairs={{0,4},{1,5},{2,6},{3,7},{4,0},{5,1},{6,2},{7,3},{8,12},{9,13},{10,... | collective-permute-start | bytes 1572872 | tf_op jit(solution)/shard_map/ppermute | solution.py:1189
  385.5 20.8 %collective-permute-start.70 = (bf16[4,128,512]{2,1,0:T(8,128)(2,1)}, bf16[4,128,512]{2,1,0:T(8,128)(2,1)}, u32[]{:S(2)}, u32[]{:S(2)}) collective-permute-start(bf16[4,128,512]{2,1,0:T(8,128)(2,1)} %add_convert_fusion.5), channel_id=1, source_target_pairs={{0,8},{1,9},{2,10},{3,11},{4,12},{5,13},{6,14},{7,15},{8,0},{9,1},... | collective-permute-start | bytes 1572872 | tf_op jit(solution)/shard_map/ppermute | solution.py:1189
  403.0 19.7 %collective-permute-start.67 = (bf16[8,48,512]{2,1,0:T(8,128)(2,1)S(1)}, bf16[8,48,512]{2,1,0:T(8,128)(2,1)S(1)}, u32[]{:S(2)}, u32[]{:S(2)}) collective-permute-start(bf16[8,48,512]{2,1,0:T(8,128)(2,1)S(1)} %add_convert_fusion.6), channel_id=1, source_target_pairs={{0,8},{1,9},{2,10},{3,11},{4,12},{5,13},{6,14},{7,15},{8,0},{9,1},... | collective-permute-start | bytes 1179656 | tf_op jit(solution)/shard_map/ppermute | solution.py:1189
  407.6 16.2 %collective-permute-start.74 = (bf16[2,128,512]{2,1,0:T(8,128)(2,1)S(1)}, bf16[2,128,512]{2,1,0:T(8,128)(2,1)S(1)}, u32[]{:S(2)}, u32[]{:S(2)}) collective-permute-start(bf16[2,128,512]{2,1,0:T(8,128)(2,1)S(1)} %add_convert_fusion.9), channel_id=1, source_target_pairs={{0,16},{1,17},{2,18},{3,19},{4,20},{5,21},{6,22},{7,23},{8,24},{9,... | collective-permute-start | bytes 786440 | tf_op jit(solution)/shard_map/ppermute | solution.py:1189
  409.0 17.7 %collective-permute-start.73 = (bf16[2,128,512]{2,1,0:T(8,128)(2,1)S(1)}, bf16[2,128,512]{2,1,0:T(8,128)(2,1)S(1)}, u32[]{:S(2)}, u32[]{:S(2)}) collective-permute-start(bf16[2,128,512]{2,1,0:T(8,128)(2,1)S(1)} %add_convert_fusion.8), channel_id=1, source_target_pairs={{0,2},{1,3},{2,0},{3,1},{4,6},{5,7},{6,4},{7,5},{8,10},{9,11},{10,... | collective-permute-start | bytes 786440 | tf_op jit(solution)/shard_map/ppermute | solution.py:1189
  422.6 14.8 %collective-permute-start.72 = (bf16[4,144,512]{2,1,0:T(8,128)(2,1)S(1)}, bf16[4,144,512]{2,1,0:T(8,128)(2,1)S(1)}, u32[]{:S(2)}, u32[]{:S(2)}) collective-permute-start(bf16[4,144,512]{2,1,0:T(8,128)(2,1)S(1)} %add_convert_fusion.3), channel_id=1, source_target_pairs={{0,4},{1,5},{2,6},{3,7},{4,0},{5,1},{6,2},{7,3},{8,12},{9,13},{10,... | collective-permute-start | bytes 1769480 | tf_op jit(solution)/shard_map/ppermute | solution.py:1189
  423.7 16.7 %collective-permute-start.71 = (bf16[4,48,512]{2,1,0:T(8,128)(2,1)S(1)}, bf16[4,48,512]{2,1,0:T(8,128)(2,1)S(1)}, u32[]{:S(2)}, u32[]{:S(2)}) collective-permute-start(bf16[4,48,512]{2,1,0:T(8,128)(2,1)S(1)} %add_convert_fusion.10), channel_id=1, source_target_pairs={{0,2},{1,3},{2,0},{3,1},{4,6},{5,7},{6,4},{7,5},{8,10},{9,11},{10,... | collective-permute-start | bytes 589832 | tf_op jit(solution)/shard_map/ppermute | solution.py:1189
  438.6 10.4 %collective-permute-start.76 = (bf16[2,144,512]{2,1,0:T(8,128)(2,1)S(1)}, bf16[2,144,512]{2,1,0:T(8,128)(2,1)S(1)}, u32[]{:S(2)}, u32[]{:S(2)}) collective-permute-start(bf16[2,144,512]{2,1,0:T(8,128)(2,1)S(1)} %add_convert_fusion.7), channel_id=1, source_target_pairs={{0,8},{1,9},{2,10},{3,11},{4,12},{5,13},{6,14},{7,15},{8,0},{9,1},... | collective-permute-start | bytes 884744 | tf_op jit(solution)/shard_map/ppermute | solution.py:1189
  438.7 15.3 %collective-permute-start.80 = (bf16[1,128,512]{2,1,0:T(8,128)(2,1)S(1)}, bf16[1,128,512]{2,1,0:T(8,128)(2,1)S(1)}, u32[]{:S(2)}, u32[]{:S(2)}) collective-permute-start(bf16[1,128,512]{2,1,0:T(8,128)(2,1)S(1)} %add_convert_fusion.12), channel_id=1, source_target_pairs={{0,16},{1,17},{2,18},{3,19},{4,20},{5,21},{6,22},{7,23},{8,24},{9,... | collective-permute-start | bytes 393224 | tf_op jit(solution)/shard_map/ppermute | solution.py:1189
  438.8 15.3 %collective-permute-start.79 = (bf16[1,128,512]{2,1,0:T(8,128)(2,1)S(1)}, bf16[1,128,512]{2,1,0:T(8,128)(2,1)S(1)}, u32[]{:S(2)}, u32[]{:S(2)}) collective-permute-start(bf16[1,128,512]{2,1,0:T(8,128)(2,1)S(1)} %add_convert_fusion.13), channel_id=1, source_target_pairs={{0,2},{1,3},{2,0},{3,1},{4,6},{5,7},{6,4},{7,5},{8,10},{9,11},{10,... | collective-permute-start | bytes 393224 | tf_op jit(solution)/shard_map/ppermute | solution.py:1189
  441.4 8.8 %collective-permute-start.75 = (bf16[2,48,512]{2,1,0:T(8,128)(2,1)S(1)}, bf16[2,48,512]{2,1,0:T(8,128)(2,1)S(1)}, u32[]{:S(2)}, u32[]{:S(2)}) collective-permute-start(bf16[2,48,512]{2,1,0:T(8,128)(2,1)S(1)} %add_convert_fusion.14), channel_id=1, source_target_pairs={{0,4},{1,5},{2,6},{3,7},{4,0},{5,1},{6,2},{7,3},{8,12},{9,13},{10,... | collective-permute-start | bytes 294920 | tf_op jit(solution)/shard_map/ppermute | solution.py:1189
  450.1 12.1 %collective-permute-start.78 = (bf16[1,144,512]{2,1,0:T(8,128)(2,1)S(1)}, bf16[1,144,512]{2,1,0:T(8,128)(2,1)S(1)}, u32[]{:S(2)}, u32[]{:S(2)}) collective-permute-start(bf16[1,144,512]{2,1,0:T(8,128)(2,1)S(1)} %add_convert_fusion.11), channel_id=1, source_target_pairs={{0,16},{1,17},{2,18},{3,19},{4,20},{5,21},{6,22},{7,23},{8,24},{9,... | collective-permute-start | bytes 442376 | tf_op jit(solution)/shard_map/ppermute | solution.py:1189
  451.1 8.9 %collective-permute-start.77 = (bf16[1,48,512]{2,1,0:T(8,128)(2,1)S(1)}, bf16[1,48,512]{2,1,0:T(8,128)(2,1)S(1)}, u32[]{:S(2)}, u32[]{:S(2)}) collective-permute-start(bf16[1,48,512]{2,1,0:T(8,128)(2,1)S(1)} %add_convert_fusion.15), channel_id=1, source_target_pairs={{0,16},{1,17},{2,18},{3,19},{4,20},{5,21},{6,22},{7,23},{8,24},{9,... | collective-permute-start | bytes 147464 | tf_op jit(solution)/shard_map/ppermute | solution.py:1189
  (93 other events, 468.7 us)
Sparse Core Ops, SparseCore 0:
  12.9 125.6 all-gather.1
  256.6 152.6 reduce-scatter.1
